TPU v7x, 512 devices: a whole 4x4x16 slice. The times are simulated.
512 devices in a mesh: dp: 64 (over z, x), expert: 8 (over y, core).
Axes of the slice: x: 4, y: 4, z: 16, core: 2. Of those that a mesh axis runs over, the one named last changes fastest.
Arguments:
- stream_grad: bfloat16 [65536, 4096], P('dp', 'expert'), may hold values from -6 to 6
- value_grad: bfloat16 [65536, 1024], P(('dp', 'expert')), may hold values from -24 to 24
- attn_input: bfloat16 [65536, 4096], P('dp', 'expert'), may hold values from -200 to 200
- norm_gain: float32 [4096], P('expert'), may hold values from 0.1 to 1.9
- value_weight: bfloat16 [1024, 4096], P('dp', 'expert'), may hold values from -0.1875 to 0.1875
- gate_logits: float32 [65536, 2], P('dp'), may hold values from -6 to 6
- routes: int32 [65536, 2], P('dp'), may hold values from 0 to 7, all different within a row; in each aligned block of 1024 rows (0 to 1023, 1024 to 2047, ...) at most 320 rows name the same one
Outputs:
- d_value: bfloat16 [1024, 4096], P('dp', 'expert')
- d_gain: float32 [4096], P('expert')
- dispatched: bfloat16 [8, 20480, 4096], P('expert', 'dp')
Inputs may be any that keep to these rules, and one draw needn't show every extreme that they name: `routes`: among the rows of one block of 1024 tokens no expert is named by more than 320 rows, and in some blocks one expert is named by exactly 320 rows; the two experts of a token differ.
All inputs are finite; a program needn't handle non-finite values.
Results may differ from a plain program's by a relative error of at most 0.005.
Values may be sent and summed in bfloat16 or wider, within the bound.
No kernel may reach another device: no remote copies, remote signals or barrier semaphores. Data moves between devices by JAX's collectives and lax.ppermute only.
A program may use at most 64 MiB of HBM per device.

v0:
```python
import jax
import jax.numpy as jnp
from jax import lax
from jax.sharding import PartitionSpec as P

epsilon = 1e-05


def on_device(stream_grad, value_grad, attn_input, norm_gain, value_weight, gate_logits, routes):
    group, columns = attn_input.shape
    experts_all = lax.axis_size("expert")
    width = columns * experts_all
    tokens_all = group * lax.axis_size("dp")
    rescale = float(tokens_all) ** (-0.5)
    capacity = min(group, 5 * group // (2 * experts_all))
    inputs = attn_input.astype(jnp.float32)
    own_squares = jnp.sum(inputs * inputs, axis=1)
    every_value = lax.all_gather(value_grad, "expert", axis=0, tiled=True)
    d_normed = jnp.dot(
        every_value,
        lax.all_gather(value_weight, "dp", axis=0, tiled=True),
        preferred_element_type=jnp.float32,
    )
    weighted = d_normed * norm_gain
    total_squares = lax.psum(own_squares, "expert")
    root_mean = jnp.sqrt(total_squares / width + epsilon)[:, None]
    scaled = inputs / root_mean
    inner = lax.psum(jnp.sum(weighted * scaled, axis=1), "expert") / width
    normed = (scaled * norm_gain).astype(jnp.bfloat16)
    d_gain = lax.psum(jnp.sum(d_normed * scaled, axis=0) * rescale, "dp")
    d_value = lax.psum_scatter(
        lax.dot_general(
            every_value, normed, (((0,), (0,)), ((), ())), preferred_element_type=jnp.float32
        )
        * rescale,
        "dp",
        scatter_dimension=0,
        tiled=True,
    ).astype(jnp.bfloat16)
    stream = stream_grad.astype(jnp.float32) + (weighted - scaled * inner[:, None]) / root_mean
    gate_prob = 1.0 / (1.0 + jnp.exp(gate_logits[:, ::-1] - gate_logits))
    flat_routes = routes.reshape(-1)
    onehot = (flat_routes[:, None] == jnp.arange(experts_all, dtype=jnp.int32)[None, :]).astype(
        jnp.int32
    )
    slot_index = jnp.sum((jnp.cumsum(onehot, axis=0) - onehot) * onehot, axis=-1)
    sent_rows = (
        (gate_prob[:, :, None] * stream[:, None, :]).astype(jnp.bfloat16).reshape(-1, columns)
    )
    buffer = (
        jnp.zeros((experts_all, capacity, columns), jnp.bfloat16)
        .at[flat_routes, slot_index]
        .set(sent_rows)
    )
    arrived = lax.all_to_all(buffer, "expert", split_axis=0, concat_axis=2, tiled=True)
    return (d_value, d_gain, arrived)


def solution(mesh):
    return jax.shard_map(
        on_device,
        mesh=mesh,
        in_specs=(
            P("dp", "expert"),
            P(("dp", "expert"), None),
            P("dp", "expert"),
            P("expert"),
            P("dp", "expert"),
            P("dp", None),
            P("dp", None),
        ),
        out_specs=(P("dp", "expert"), P("expert"), P("expert", "dp", None)),
        check_vma=False,
    )
```

profile of v0, /device:TPU:1, one launch (start us, length us, event | category | flops | bytes accessed | tf_op | source)
XLA Modules:
  0.0 882.0 jit_solution(8986424246928186255)
XLA Ops:
  7.2 0.7 all-gather.3.cloned.1.call-update
  8.0 0.7 all-gather.5.cloned.1.call-update
  8.7 0.9 copy.22
  10.2 0.3 reshape.76
  10.5 2.3 reduce-window.6
  12.8 0.3 slice_reduce_fusion
  14.3 18.7 %psum.21 = f32[1024]{0:T(1024)S(1)} all-reduce(f32[1024]{0:T(1024)S(1)} %fusion), channel_id=1, replica_groups=mesh['dp'=64,'expert'=8] {'expert'}, use_global_device_ids=true, to_apply=%region_1.0 | all-reduce | flops 1024 | bytes 8192 | tf_op jit(solution)/shard_map/psum | solution.py:25
  33.1 15.7 %all-gather.3.cloned.1.call-done = bf16[1024,1024]{1,0:T(8,128)(2,1)} async-done(((bf16[128,1024]{1,0:T(8,128)(2,1)}), bf16[1024,1024]{1,0:T(8,128)(2,1)}) %all-gather.3.cloned.1.call-update) | async-done | bytes 2097168 | tf_op jit(solution)/shard_map/all_gather | solution.py:18
  48.8 4.3 multiply_bitcast_fusion
  53.1 3.0 copy.28
  56.1 0.6 copy-done.5
  56.9 124.2 %all-gather.5.cloned.1.call-done = bf16[1024,512]{1,0:T(8,128)(2,1)} async-done(((bf16[16,512]{1,0:T(8,128)(2,1)}), bf16[1024,512]{1,0:T(8,128)(2,1)}) %all-gather.5.cloned.1.call-update) | async-done | bytes 1048592 | tf_op jit(solution)/shard_map/all_gather | solution.py:21
  181.1 4.6 multiply_reduce_fusion
  185.7 21.9 %psum.23 = f32[1024]{0:T(1024)S(1)} all-reduce(f32[1024]{0:T(1024)S(1)} %get-tuple-element.15), channel_id=1, replica_groups=mesh['dp'=64,'expert'=8] {'expert'}, use_global_device_ids=true, to_apply=%region_9.10 | all-reduce | flops 1024 | bytes 8192 | tf_op jit(solution)/shard_map/psum | solution.py:28
  207.7 2.3 divide_add_fusion
  210.0 3.4 mul.83
  213.4 6.1 mul.84
  219.4 12.8 %scatter_custom_fusion = bf16[2560,512]{1,0:T(8,128)(2,1)} fusion(s32[2048]{0:T(1024)S(1)} %broadcast_select_fusion, f32[2048,512]{1,0:T(8,128)} %mul.84, f32[2048]{0:T(1024)S(1)} %mul.77, bf16[]{:T(256)} %constant.6.clone.1), kind=kCustom, calls=%fused_computation.5 | custom fusion | flops 2097152 | bytes 6823938
  232.2 4.2 all-to-all-start
  236.3 114.6 %psum.22 = f32[512]{0:T(512)} all-reduce(f32[512]{0:T(512)S(1)} %broadcast_multiply_fusion.1), channel_id=1, replica_groups=mesh['dp'=64,'expert'=8] {'dp'}, use_global_device_ids=true, to_apply=%region_4.0 | all-reduce | flops 512 | bytes 4096 | tf_op jit(solution)/shard_map/psum | solution.py:30
  351.0 1.9 copy.30
  352.8 521.1 %reduce-scatter.4.cloned.1.call-done = f32[16,512]{1,0:T(8,128)} async-done(((f32[1024,512]{1,0:T(8,128)}), f32[16,512]{1,0:T(8,128)}) %reduce-scatter.4.cloned.1.call-update) | async-done | bytes 32784
  873.9 0.9 copy.29
  874.8 0.7 copy.27
  (34 shorter events, 2.2 us)
Async XLA Ops:
  7.2 6.1 copy-start.2
  7.2 6.8 copy-start
  7.2 41.6 %all-gather.3.cloned.1.call-start = ((), (), s32[]{:S(2)}) async-start(), calls=%async_computation.2 | async-start | bytes 2359296 | tf_op jit(solution)/shard_map/all_gather | solution.py:18
  7.9 173.2 %all-gather.5.cloned.1.call-start = ((), (), s32[]{:S(2)}) async-start(), calls=%async_computation.3 | async-start | bytes 1064960 | tf_op jit(solution)/shard_map/all_gather | solution.py:21
  8.7 865.2 %reduce-scatter.4.cloned.1.call-start = ((), (), s32[]{:S(2)}) async-start(), calls=%async_computation.4 | async-start | bytes 2129920
  9.6 39.2 %copy-start.3 = (f32[512]{0:T(512)S(1)}, f32[512]{0:T(512)}, u32[]{:S(2)}) copy-start(f32[512]{0:T(512)} %param.10) | copy-start | bytes 6148
  56.0 0.7 copy-start.5
  56.0 0.7 copy-start.4
  56.9 150.8 %copy-start.1 = (bf16[1024,512]{1,0:T(8,128)(2,1)S(1)}, bf16[1024,512]{1,0:T(8,128)(2,1)}, u32[]{:S(2)}) copy-start(bf16[1024,512]{1,0:T(8,128)(2,1)} %param.7) | copy-start | bytes 3145732
  232.2 118.8 %all-to-all-start = ((bf16[8,320,512]{2,1,0:T(8,128)(2,1)}), bf16[8,320,512]{2,1,0:T(8,128)(2,1)S(1)}, u32[]{:S(2)}, u32[]{:S(2)}) async-start(bf16[8,320,512]{2,1,0:T(8,128)(2,1)} %bitcast.33), calls=%async_computation | async-start | bytes 5242880 | tf_op jit(solution)/shard_map/all_to_all | solution.py:55
Sparse Core Ops, SparseCore 0:
  10.2 38.5 all-gather.2
  51.7 129.3 all-gather.4
  185.5 688.3 reduce-scatter.3
where the time goes:
time: 893 us; the launch traced here: 882 us
  waiting for transfers between devices  662 us (74%)
  blocking collectives  155 us (17%)
  local copies, waits for them, and re-layouts  19.2 us (2%)
  other arithmetic  18.2 us (2%)
  between operations  13.9 us (2%)
    unnamed x4, waiting for transfers between devices  522 us
    all_gather x1, waiting for transfers between devices, on_device(): lax.all_gather(value_weight, 'dp', axis=0, tiled=True)  124 us
    psum x1, blocking collectives, on_device(): d_gain = lax.psum(jnp.sum(d_normed * scaled, axis=0) * rescale, 'dp')  115 us
    psum x1, blocking collectives, on_device(): inner = lax.psum(jnp.sum(weighted * scaled, axis=1), 'expert') / width  21.9 us
    psum x1, blocking collectives, on_device(): total_squares = lax.psum(own_squares, 'expert')  18.7 us
  transfers between devices with their start and end apart: 4, of which 3 were waited for; matrix products, arithmetic and copies ran while one was open for 5% of the time, Pallas kernels for 0%

commit v1 on v0

v1 whole, which is shorter than its diff:
```python
import jax
import jax.numpy as jnp
from jax import lax
from jax.experimental import pallas as pl
from jax.experimental.pallas import tpu as pltpu
from jax.sharding import Mesh, PartitionSpec as P

epsilon = 1e-05
EXPERT = ("y", "core")


def route_kernel(routes_ref, logits_ref, slot_ref, gate_ref):
    experts, group = slot_ref.shape
    expert = lax.broadcasted_iota(jnp.int32, (experts, group), 0)
    first = routes_ref[0:1, :] == expert
    second = routes_ref[1:2, :] == expert
    named = jnp.where(first | second, 1.0, 0.0)
    earlier = lax.broadcasted_iota(jnp.int32, (group, group), 0) < lax.broadcasted_iota(
        jnp.int32, (group, group), 1
    )
    count = jnp.dot(
        named.astype(jnp.bfloat16),
        jnp.where(earlier, 1.0, 0.0).astype(jnp.bfloat16),
        preferred_element_type=jnp.float32,
    )
    slot_ref[...] = jnp.where(named > 0.0, count, -1.0).astype(jnp.int32)
    low, high = logits_ref[0:1, :], logits_ref[1:2, :]
    gate_first = 1.0 / (1.0 + jnp.exp(high - low))
    gate_second = 1.0 / (1.0 + jnp.exp(low - high))
    gate_ref[...] = jnp.where(first, gate_first, jnp.where(second, gate_second, 0.0))


def column(row):
    return jnp.transpose(jnp.broadcast_to(row, (8, row.shape[1])))[:, 0:1]


def dispatch_kernel(
    width, squares_ref, inner_ref, gain_ref, slot_ref, gate_ref, grad_ref, input_ref, normed_ref,
    out_ref, stream_ref,
):
    expert = pl.program_id(0)
    group = grad_ref.shape[0]
    capacity = out_ref.shape[1]

    @pl.when(expert == 0)
    def _():
        squares = jnp.sum(squares_ref[...], axis=0, keepdims=True)
        root_mean = jnp.sqrt(squares / width + epsilon)
        inner = jnp.sum(inner_ref[...], axis=0, keepdims=True) / width
        root_column, inner_column = column(root_mean), column(inner)
        scaled = input_ref[...].astype(jnp.float32) / root_column
        weighted = normed_ref[...] * gain_ref[...]
        stream_ref[...] = (
            grad_ref[...].astype(jnp.float32) + (weighted - scaled * inner_column) / root_column
        )

    slot = slot_ref[pl.ds(expert, 1), :]
    gate = column(gate_ref[pl.ds(expert, 1), :])
    rows = (gate * stream_ref[...]).astype(jnp.bfloat16)
    taken = lax.broadcasted_iota(jnp.int32, (capacity, group), 0) == slot
    picked = jnp.dot(
        jnp.where(taken, 1.0, 0.0).astype(jnp.bfloat16), rows, preferred_element_type=jnp.float32
    )
    out_ref[0] = picked.astype(jnp.bfloat16)


def to_all(part, axis):
    size = lax.axis_size(axis)
    return lax.all_to_all(
        jnp.broadcast_to(part[None], (size,) + part.shape), axis, 0, 0, tiled=True
    )


def swapped(parts, axis):
    return lax.all_to_all(parts, axis, 0, 0, tiled=True)


def on_device(stream_grad, value_grad, attn_input, norm_gain, value_weight, gate_logits, routes):
    group, columns = attn_input.shape
    experts = lax.axis_size(EXPERT)
    zh, zl, xs = lax.axis_size("zh"), lax.axis_size("zl"), lax.axis_size("x")
    width = columns * experts
    tokens_all = group * zh * zl * xs
    rescale = float(tokens_all) ** (-0.5)
    capacity = min(group, 5 * group // (2 * experts))
    rows = value_weight.shape[0]
    features = rows * zh * zl * xs
    vmem = pl.BlockSpec(memory_space=pltpu.VMEM)

    every_value = lax.all_gather(value_grad, EXPERT, axis=0, tiled=True)

    weight = to_all(value_weight, "zh")
    weight = to_all(weight, "zl")
    weight = to_all(weight, "x")
    weight = jnp.transpose(weight, (2, 1, 0, 3, 4)).reshape(features, columns)

    slot, gate = pl.pallas_call(
        route_kernel,
        in_specs=[vmem, vmem],
        out_specs=[vmem, vmem],
        out_shape=[
            jax.ShapeDtypeStruct((experts, group), jnp.int32),
            jax.ShapeDtypeStruct((experts, group), jnp.float32),
        ],
        compiler_params=pltpu.CompilerParams(vmem_limit_bytes=32 * 2**20),
    )(routes.T, gate_logits.T)

    inputs = attn_input.astype(jnp.float32)
    own_squares = jnp.sum(inputs * inputs, axis=1)
    squares = to_all(own_squares.reshape(8, group // 8), EXPERT).reshape(experts, group)
    root_mean = jnp.sqrt(jnp.sum(squares, axis=0) / width + epsilon)[:, None]
    scaled = inputs / root_mean
    normed = (scaled * norm_gain).astype(jnp.bfloat16)

    d_value = lax.dot_general(
        every_value, normed, (((0,), (0,)), ((), ())), preferred_element_type=jnp.float32
    )
    d_value = d_value.reshape(zh, zl, xs, rows, columns).transpose(2, 1, 0, 3, 4)
    d_value = swapped(d_value.astype(jnp.bfloat16), "x").astype(jnp.float32).sum(axis=0)

    d_normed = jnp.dot(every_value, weight, preferred_element_type=jnp.float32)
    weighted = d_normed * norm_gain
    own_inner = jnp.sum(weighted * scaled, axis=1)
    inner = to_all(own_inner.reshape(8, group // 8), EXPERT).reshape(experts, group)
    own_gain = jnp.sum(d_normed * scaled, axis=0)

    sent = pl.pallas_call(
        lambda *refs: dispatch_kernel(width, *refs),
        grid=(experts,),
        in_specs=[
            pl.BlockSpec((experts, group), lambda e: (0, 0)),
            pl.BlockSpec((experts, group), lambda e: (0, 0)),
            pl.BlockSpec((1, columns), lambda e: (0, 0)),
            pl.BlockSpec((experts, group), lambda e: (0, 0)),
            pl.BlockSpec((experts, group), lambda e: (0, 0)),
            pl.BlockSpec((group, columns), lambda e: (0, 0)),
            pl.BlockSpec((group, columns), lambda e: (0, 0)),
            pl.BlockSpec((group, columns), lambda e: (0, 0)),
        ],
        out_specs=pl.BlockSpec((1, capacity, columns), lambda e: (e, 0, 0)),
        out_shape=jax.ShapeDtypeStruct((experts, capacity, columns), jnp.bfloat16),
        scratch_shapes=[pltpu.VMEM((group, columns), jnp.float32)],
        compiler_params=pltpu.CompilerParams(
            dimension_semantics=("arbitrary",), vmem_limit_bytes=40 * 2**20
        ),
    )(squares, inner, norm_gain[None], slot, gate, stream_grad, attn_input, d_normed)
    arrived = lax.all_to_all(sent, EXPERT, split_axis=0, concat_axis=2, tiled=True)

    d_value = swapped(d_value, "zl").sum(axis=0)
    d_value = swapped(d_value, "zh").sum(axis=0)
    d_value = (d_value * rescale).astype(jnp.bfloat16)

    d_gain = own_gain.reshape(4, columns // 4)
    for axis in ("x", "zl", "zh"):
        d_gain = to_all(d_gain, axis).sum(axis=0)
    d_gain = d_gain.reshape(columns) * rescale
    return (d_value, d_gain, arrived)


def solution(mesh):
    split = Mesh(mesh.devices.reshape(4, 4, 4, 4, 2), ("zh", "zl", "x", "y", "core"))
    dp = ("zh", "zl", "x")
    return jax.shard_map(
        on_device,
        mesh=split,
        in_specs=(
            P(dp, EXPERT),
            P(dp + EXPERT, None),
            P(dp, EXPERT),
            P(EXPERT),
            P(dp, EXPERT),
            P(dp, None),
            P(dp, None),
        ),
        out_specs=(P(dp, EXPERT), P(EXPERT), P(EXPERT, dp, None)),
        check_vma=False,
    )
```

time: 893 us -> 231 us (0.26)
  waiting for transfers between devices: 662 us -> 91.9 us
  blocking collectives: 155 us -> 34.4 us
  starting transfers between devices: 4.28 us -> 48.7 us
  other arithmetic: 18.2 us -> 5.97 us
  Pallas kernels: 0 us -> 9.86 us
    unnamed x4 -> x1, waiting for transfers between devices: 522 us -> 0.68 us
    psum x3 -> x0, blocking collectives: 155 us -> none  [the longest x1 115 us: on_device(): d_gain = lax.psum(jnp.sum(d_normed * scaled, axis=0) * rescale, 'dp')]
    all_gather x2 -> x1, waiting for transfers between devices: 140 us -> 0.01 us  [on_device(): every_value = lax.all_gather(value_grad, EXPERT, axis=0, tiled=True)]
    all_to_all x1 -> x10, waiting for transfers between devices: 0.01 us -> 91.2 us  [the longest x6 36.8 us: to_all(): lax.all_to_all(jnp.broadcast_to(part[None], (size,) + part.shape), axis,...]
    all_to_all x1 -> x10, starting transfers between devices: 4.16 us -> 48.7 us  [the longest x6 29.1 us: to_all(): lax.all_to_all(jnp.broadcast_to(part[None], (size,) + part.shape), axis,...]
    all_to_all x0 -> x2, blocking collectives: none -> 34.4 us  [to_all(): lax.all_to_all(jnp.broadcast_to(part[None], (size,) + part.shape), axis,...]
    unnamed x5 -> x0, other arithmetic: 13 us -> none
    pallas_call x0 -> x2, Pallas kernels: none -> 9.86 us  [the longest x1 9.56 us: on_device(): pl.pallas_call(lambda *refs: dispatch_kernel(width, *refs), grid=(experts...]
  transfers between devices with their start and end apart: 4 -> 11, of which waited for: 3 -> 8; matrix products, arithmetic and copies ran while one was open for 5% -> 9% of each run, Pallas kernels for 0% -> 4%
where the time goes in v1:
time: 231 us; the launch traced here: 227 us
  waiting for transfers between devices  91.9 us (40%)
  starting transfers between devices  48.7 us (21%)
  blocking collectives  34.4 us (15%)
  local copies, waits for them, and re-layouts  14.6 us (6%)
  between operations  14.2 us (6%)
  Pallas kernels  9.86 us (4%)
  matrix products  7.32 us (3%)
  other arithmetic  5.97 us (3%)
    all_to_all x6, waiting for transfers between devices, to_all(): lax.all_to_all(jnp.broadcast_to(part[None], (size,) + part.shape), axis,...  36.8 us
    all_to_all x2, blocking collectives, to_all(): lax.all_to_all(jnp.broadcast_to(part[None], (size,) + part.shape), axis,...  34.4 us
    all_to_all x1, waiting for transfers between devices, on_device(): lax.all_to_all(sent, EXPERT, split_axis=0, concat_axis=2, tiled=True)  30.2 us
    all_to_all x6, starting transfers between devices, to_all(): lax.all_to_all(jnp.broadcast_to(part[None], (size,) + part.shape), axis,...  29.1 us
    all_to_all x3, waiting for transfers between devices, swapped(): return lax.all_to_all(parts, axis, 0, 0, tiled=True)  24.1 us
    all_to_all x3, starting transfers between devices, swapped(): return lax.all_to_all(parts, axis, 0, 0, tiled=True)  11.7 us
    pallas_call x1, Pallas kernels, on_device(): pl.pallas_call(lambda *refs: dispatch_kernel(width, *refs), grid=(experts...  9.56 us
    all_to_all x1, starting transfers between devices, on_device(): lax.all_to_all(sent, EXPERT, split_axis=0, concat_axis=2, tiled=True)  7.91 us
  transfers between devices with their start and end apart: 11, of which 8 were waited for; matrix products, arithmetic and copies ran while one was open for 9% of the time, Pallas kernels for 4%

profile of v1, /device:TPU:1, one launch (start us, length us, event | category | flops | bytes accessed | tf_op | source)
XLA Modules:
  0.0 227.0 jit_solution(13803857790658960771)
XLA Ops:
  8.6 27.9 %all_to_all.73 = bf16[4,16,512]{2,1,0:T(8,128)(2,1)S(1)} all-to-all(bf16[4,16,512]{2,1,0:T(8,128)(2,1)S(1)} %broadcast_in_dim.26), channel_id=1, replica_groups=mesh['zh'=4,'zl'=4,'x'=4,'y'=4,'core'=2] {'zh'}, dimensions={0} | all-to-all | bytes 131072 | tf_op jit(solution)/shard_map/all_to_all | solution.py:69
  37.3 3.4 %all-to-all-start.5 = ((bf16[4,4,16,512]{3,2,1,0:T(8,128)(2,1)}), bf16[4,4,16,512]{3,2,1,0:T(8,128)(2,1)S(1)}, u32[]{:S(2)}, u32[]{:S(2)}) async-start(bf16[4,4,16,512]{3,2,1,0:T(8,128)(2,1)} %broadcast_in_dim.27), calls=%async_computation.5 | async-start | bytes 524288 | tf_op jit(solution)/shard_map/all_to_all | solution.py:69
  42.2 4.3 %all-to-all-done.5 = bf16[4,4,16,512]{3,2,1,0:T(8,128)(2,1)S(1)} async-done(((bf16[4,4,16,512]{3,2,1,0:T(8,128)(2,1)}), bf16[4,4,16,512]{3,2,1,0:T(8,128)(2,1)S(1)}, u32[]{:S(2)}, u32[]{:S(2)}) %all-to-all-start.5) | async-done | bytes 262176 | tf_op jit(solution)/shard_map/all_to_all | solution.py:69
  47.1 8.7 %all-to-all-start = ((f32[8,8,128]{2,1,0:T(8,128)}), f32[8,8,128]{2,1,0:T(8,128)S(1)}, u32[]{:S(2)}, u32[]{:S(2)}) async-start(f32[8,8,128]{2,1,0:T(8,128)} %broadcast_in_dim.25), calls=%async_computation | async-start | bytes 65536 | tf_op jit(solution)/shard_map/all_to_all | solution.py:69
  55.8 4.7 %all-to-all-done = f32[8,8,128]{2,1,0:T(8,128)S(1)} async-done(((f32[8,8,128]{2,1,0:T(8,128)}), f32[8,8,128]{2,1,0:T(8,128)S(1)}, u32[]{:S(2)}, u32[]{:S(2)}) %all-to-all-start) | async-done | bytes 32800 | tf_op jit(solution)/shard_map/all_to_all | solution.py:69
  61.6 4.1 %all-to-all-start.6 = ((bf16[4,4,4,16,512]{4,3,1,2,0:T(8,128)(2,1)}), bf16[4,4,4,16,512]{4,3,1,2,0:T(8,128)(2,1)S(1)}, u32[]{:S(2)}, u32[]{:S(2)}) async-start(bf16[4,4,4,16,512]{4,3,1,2,0:T(8,128)(2,1)} %broadcast_in_dim.28), calls=%async_computation.6 | async-start | bytes 2097152 | tf_op jit(solution)/shard_map/all_to_all | solution.py:69
  65.8 14.1 %all-to-all-done.6 = bf16[4,4,4,16,512]{4,3,1,2,0:T(8,128)(2,1)S(1)} async-done(((bf16[4,4,4,16,512]{4,3,1,2,0:T(8,128)(2,1)}), bf16[4,4,4,16,512]{4,3,1,2,0:T(8,128)(2,1)S(1)}, u32[]{:S(2)}, u32[]{:S(2)}) %all-to-all-start.6) | async-done | bytes 1048608 | tf_op jit(solution)/shard_map/all_to_all | solution.py:69
  80.9 3.4 %multiply_reduce_fusion = (f32[1024]{0:T(1024)S(1)}, f32[512]{0:T(512)S(1)}, f32[1024,512]{1,0:T(8,128)S(1)}) fusion(f32[512]{0:T(512)S(1)} %copy-done.4, f32[1024]{0:T(1024)S(1)} %sqrt_bitcast_fusion, bf16[1024,512]{1,0:T(8,128)(2,1)S(1)} %copy-done, bf16[1024,1024]{1,0:T(8,128)(2,1)} %all-gather.2.cloned.1.call-done, bf16[1024,512]{1,0:T(8,128)(2,1)} %bitcast.42), kind=kOutput, calls=%fused_computation.3 | convolution fusion | flops 1077410304 | bytes 6303744 | tf_op jit(solution)/shard_map/dot_general | solution.py:121
  84.3 6.5 %all_to_all.74 = f32[4,4,128]{2,1,0:T(4,128)S(1)} all-to-all(f32[4,4,128]{2,1,0:T(4,128)S(1)} %broadcast_in_dim.30), channel_id=1, replica_groups=mesh['zh'=4,'zl'=4,'x'=4,'y'=4,'core'=2] {'x'}, dimensions={0} | all-to-all | bytes 16384 | tf_op jit(solution)/shard_map/all_to_all | solution.py:69
  91.4 6.3 %all-to-all-start.10 = ((f32[8,8,128]{2,1,0:T(8,128)}), f32[8,8,128]{2,1,0:T(8,128)S(1)}, u32[]{:S(2)}, u32[]{:S(2)}) async-start(f32[8,8,128]{2,1,0:T(8,128)} %broadcast_in_dim.67), calls=%async_computation.10 | async-start | bytes 65536 | tf_op jit(solution)/shard_map/all_to_all | solution.py:69
  97.8 4.7 %all-to-all-done.10 = f32[8,8,128]{2,1,0:T(8,128)S(1)} async-done(((f32[8,8,128]{2,1,0:T(8,128)}), f32[8,8,128]{2,1,0:T(8,128)S(1)}, u32[]{:S(2)}, u32[]{:S(2)}) %all-to-all-start.10) | async-done | bytes 32800 | tf_op jit(solution)/shard_map/all_to_all | solution.py:69
  103.1 3.2 %all-to-all-start.8 = ((f32[4,4,128]{2,1,0:T(4,128)}), f32[4,4,128]{2,1,0:T(4,128)S(1)}, u32[]{:S(2)}, u32[]{:S(2)}) async-start(f32[4,4,128]{2,1,0:T(4,128)} %broadcast_in_dim.31), calls=%async_computation.8 | async-start | bytes 16384 | tf_op jit(solution)/shard_map/all_to_all | solution.py:69
  106.4 3.9 %fusion.1 = bf16[1024,512]{0,1:T(8,128)(2,1)} fusion(bf16[1024,1024]{1,0:T(8,128)(2,1)} %all-gather.2.cloned.1.call-done, f32[512]{0:T(512)S(1)} %copy-done.4, bf16[1024,512]{1,0:T(8,128)(2,1)S(1)} %copy-done, f32[1024]{0:T(1024)S(1)} %sqrt_bitcast_fusion), kind=kOutput, calls=%fused_computation.8 | convolution fusion | flops 1076363264 | bytes 4200448 | tf_op jit(solution)/shard_map/dot_general | solution.py:115
  110.3 2.3 %copy.25 = bf16[1024,512]{1,0:T(8,128)(2,1)} copy(bf16[1024,512]{0,1:T(8,128)(2,1)} %fusion.1) | data formatting | bytes 2097152 | tf_op jit(solution)/shard_map/convert_element_type | solution.py:119
  114.9 4.2 %all-to-all-start.1 = ((bf16[4,4,4,16,512]{4,3,1,2,0:T(8,128)(2,1)}), bf16[4,4,4,16,512]{4,3,1,2,0:T(8,128)(2,1)}, u32[]{:S(2)}, u32[]{:S(2)}) async-start(bf16[4,4,4,16,512]{4,3,1,2,0:T(8,128)(2,1)} %copy.26), calls=%async_computation.1 | async-start | bytes 2097152 | tf_op jit(solution)/shard_map/all_to_all | solution.py:75
  119.2 14.5 %all-to-all-done.1 = bf16[4,4,4,16,512]{4,3,1,2,0:T(8,128)(2,1)} async-done(((bf16[4,4,4,16,512]{4,3,1,2,0:T(8,128)(2,1)}), bf16[4,4,4,16,512]{4,3,1,2,0:T(8,128)(2,1)}, u32[]{:S(2)}, u32[]{:S(2)}) %all-to-all-start.1) | async-done | bytes 1048608 | tf_op jit(solution)/shard_map/all_to_all | solution.py:75
  134.2 3.2 %all-to-all-start.9 = ((f32[4,4,128]{2,1,0:T(4,128)}), f32[4,4,128]{2,1,0:T(4,128)S(1)}, u32[]{:S(2)}, u32[]{:S(2)}) async-start(f32[4,4,128]{2,1,0:T(4,128)} %broadcast_in_dim.32), calls=%async_computation.9 | async-start | bytes 16384 | tf_op jit(solution)/shard_map/all_to_all | solution.py:69
  139.8 9.1 %all-to-all-done.9 = f32[4,4,128]{2,1,0:T(4,128)S(1)} async-done(((f32[4,4,128]{2,1,0:T(4,128)}), f32[4,4,128]{2,1,0:T(4,128)S(1)}, u32[]{:S(2)}, u32[]{:S(2)}) %all-to-all-start.9) | async-done | bytes 8224 | tf_op jit(solution)/shard_map/all_to_all | solution.py:69
  148.9 4.1 %all-to-all-start.2 = ((f32[4,4,16,512]{3,2,1,0:T(8,128)}), f32[4,4,16,512]{3,2,1,0:T(8,128)}, u32[]{:S(2)}, u32[]{:S(2)}) async-start(f32[4,4,16,512]{3,2,1,0:T(8,128)} %copy.28), calls=%async_computation.2 | async-start | bytes 1048576 | tf_op jit(solution)/shard_map/all_to_all | solution.py:75
  154.6 9.6 %shard_map.95 = bf16[8,320,512]{2,1,0:T(8,128)(2,1)} custom-call(f32[8,1024]{1,0:T(8,128)S(1)} %bitcast.34, f32[8,1024]{1,0:T(8,128)S(1)} %bitcast.35, f32[1,512]{1,0:T(1,128)S(1)} %bitcast.38, s32[8,1024]{1,0:T(8,128)S(1)} %get-tuple-element.5.refs_3_, f32[8,1024]{1,0:T(8,128)S(1)} %get-tuple-element.6.refs_4_, bf16[1024,512]{1,0:T(8,128)(2,1)S(1)} %copy-done.1, ...), custom_call_target="tpu_custom_call" | custom-call | tf_op jit(solution)/shard_map/pallas_call | solution.py:127
  164.2 7.9 %all-to-all-start.11 = ((bf16[8,320,512]{2,1,0:T(8,128)(2,1)}), bf16[8,320,512]{2,1,0:T(8,128)(2,1)S(1)}, u32[]{:S(2)}, u32[]{:S(2)}) async-start(bf16[8,320,512]{2,1,0:T(8,128)(2,1)} %shard_map.95), calls=%async_computation.11 | async-start | bytes 5242880 | tf_op jit(solution)/shard_map/all_to_all | solution.py:147
  173.8 30.2 %all-to-all-done.11 = bf16[8,320,512]{2,1,0:T(8,128)(2,1)S(1)} async-done(((bf16[8,320,512]{2,1,0:T(8,128)(2,1)}), bf16[8,320,512]{2,1,0:T(8,128)(2,1)S(1)}, u32[]{:S(2)}, u32[]{:S(2)}) %all-to-all-start.11) | async-done | bytes 2621472 | tf_op jit(solution)/shard_map/all_to_all | solution.py:147
  204.1 3.3 %all-to-all-start.3 = ((f32[4,16,512]{2,1,0:T(8,128)}), f32[4,16,512]{2,1,0:T(8,128)S(1)}, u32[]{:S(2)}, u32[]{:S(2)}) async-start(f32[4,16,512]{2,1,0:T(8,128)} %reduce_sum.93), calls=%async_computation.3 | async-start | bytes 262144 | tf_op jit(solution)/shard_map/all_to_all | solution.py:75
  209.8 9.7 %all-to-all-done.3 = f32[4,16,512]{2,1,0:T(8,128)S(1)} async-done(((f32[4,16,512]{2,1,0:T(8,128)}), f32[4,16,512]{2,1,0:T(8,128)S(1)}, u32[]{:S(2)}, u32[]{:S(2)}) %all-to-all-start.3) | async-done | bytes 131104 | tf_op jit(solution)/shard_map/all_to_all | solution.py:75
  (42 shorter events, 19.3 us)
Async XLA Ops:
  7.2 73.8 %all-gather.2.cloned.1.call-start = ((), (), s32[]{:S(2)}) async-start(), calls=%async_computation.12 | async-start | bytes 2359296 | tf_op jit(solution)/shard_map/all_gather | solution.py:90
  37.3 9.2 %all-to-all-start.5 = ((bf16[4,4,16,512]{3,2,1,0:T(8,128)(2,1)}), bf16[4,4,16,512]{3,2,1,0:T(8,128)(2,1)S(1)}, u32[]{:S(2)}, u32[]{:S(2)}) async-start(bf16[4,4,16,512]{3,2,1,0:T(8,128)(2,1)} %broadcast_in_dim.27), calls=%async_computation.5 | async-start | bytes 524288 | tf_op jit(solution)/shard_map/all_to_all | solution.py:69
  47.1 13.4 %all-to-all-start = ((f32[8,8,128]{2,1,0:T(8,128)}), f32[8,8,128]{2,1,0:T(8,128)S(1)}, u32[]{:S(2)}, u32[]{:S(2)}) async-start(f32[8,8,128]{2,1,0:T(8,128)} %broadcast_in_dim.25), calls=%async_computation | async-start | bytes 65536 | tf_op jit(solution)/shard_map/all_to_all | solution.py:69
  61.6 19.3 %copy-start = (bf16[1024,512]{1,0:T(8,128)(2,1)S(1)}, bf16[1024,512]{1,0:T(8,128)(2,1)}, u32[]{:S(2)}) copy-start(bf16[1024,512]{1,0:T(8,128)(2,1)} %refs_6_.1) | copy-start | bytes 3145732
  61.6 19.3 %copy-start.4 = (f32[512]{0:T(512)S(1)}, f32[512]{0:T(512)}, u32[]{:S(2)}) copy-start(f32[512]{0:T(512)} %param.10) | copy-start | bytes 6148
  61.6 18.3 %all-to-all-start.6 = ((bf16[4,4,4,16,512]{4,3,1,2,0:T(8,128)(2,1)}), bf16[4,4,4,16,512]{4,3,1,2,0:T(8,128)(2,1)S(1)}, u32[]{:S(2)}, u32[]{:S(2)}) async-start(bf16[4,4,4,16,512]{4,3,1,2,0:T(8,128)(2,1)} %broadcast_in_dim.28), calls=%async_computation.6 | async-start | bytes 2097152 | tf_op jit(solution)/shard_map/all_to_all | solution.py:69
  91.4 11.1 %all-to-all-start.10 = ((f32[8,8,128]{2,1,0:T(8,128)}), f32[8,8,128]{2,1,0:T(8,128)S(1)}, u32[]{:S(2)}, u32[]{:S(2)}) async-start(f32[8,8,128]{2,1,0:T(8,128)} %broadcast_in_dim.67), calls=%async_computation.10 | async-start | bytes 65536 | tf_op jit(solution)/shard_map/all_to_all | solution.py:69
  103.1 11.8 %all-to-all-start.8 = ((f32[4,4,128]{2,1,0:T(4,128)}), f32[4,4,128]{2,1,0:T(4,128)S(1)}, u32[]{:S(2)}, u32[]{:S(2)}) async-start(f32[4,4,128]{2,1,0:T(4,128)} %broadcast_in_dim.31), calls=%async_computation.8 | async-start | bytes 16384 | tf_op jit(solution)/shard_map/all_to_all | solution.py:69
  114.9 18.7 %all-to-all-start.1 = ((bf16[4,4,4,16,512]{4,3,1,2,0:T(8,128)(2,1)}), bf16[4,4,4,16,512]{4,3,1,2,0:T(8,128)(2,1)}, u32[]{:S(2)}, u32[]{:S(2)}) async-start(bf16[4,4,4,16,512]{4,3,1,2,0:T(8,128)(2,1)} %copy.26), calls=%async_computation.1 | async-start | bytes 2097152 | tf_op jit(solution)/shard_map/all_to_all | solution.py:75
  119.1 33.9 %copy-start.2 = (s32[1024,2]{0,1:T(2,128)S(1)}, s32[1024,2]{0,1:T(2,128)}, u32[]{:S(2)}) copy-start(s32[1024,2]{0,1:T(2,128)} %param.13) | copy-start | bytes 24580
  119.1 33.9 %copy-start.3 = (f32[1024,2]{0,1:T(2,128)S(1)}, f32[1024,2]{0,1:T(2,128)}, u32[]{:S(2)}) copy-start(f32[1024,2]{0,1:T(2,128)} %param.12) | copy-start | bytes 24580
  134.2 14.6 %all-to-all-start.9 = ((f32[4,4,128]{2,1,0:T(4,128)}), f32[4,4,128]{2,1,0:T(4,128)S(1)}, u32[]{:S(2)}, u32[]{:S(2)}) async-start(f32[4,4,128]{2,1,0:T(4,128)} %broadcast_in_dim.32), calls=%async_computation.9 | async-start | bytes 16384 | tf_op jit(solution)/shard_map/all_to_all | solution.py:69
  148.9 15.3 %all-to-all-start.2 = ((f32[4,4,16,512]{3,2,1,0:T(8,128)}), f32[4,4,16,512]{3,2,1,0:T(8,128)}, u32[]{:S(2)}, u32[]{:S(2)}) async-start(f32[4,4,16,512]{3,2,1,0:T(8,128)} %copy.28), calls=%async_computation.2 | async-start | bytes 1048576 | tf_op jit(solution)/shard_map/all_to_all | solution.py:75
  153.4 1.2 copy-start.1
  164.2 39.9 %all-to-all-start.11 = ((bf16[8,320,512]{2,1,0:T(8,128)(2,1)}), bf16[8,320,512]{2,1,0:T(8,128)(2,1)S(1)}, u32[]{:S(2)}, u32[]{:S(2)}) async-start(bf16[8,320,512]{2,1,0:T(8,128)(2,1)} %shard_map.95), calls=%async_computation.11 | async-start | bytes 5242880 | tf_op jit(solution)/shard_map/all_to_all | solution.py:147
  204.1 15.4 %all-to-all-start.3 = ((f32[4,16,512]{2,1,0:T(8,128)}), f32[4,16,512]{2,1,0:T(8,128)S(1)}, u32[]{:S(2)}, u32[]{:S(2)}) async-start(f32[4,16,512]{2,1,0:T(8,128)} %reduce_sum.93), calls=%async_computation.3 | async-start | bytes 262144 | tf_op jit(solution)/shard_map/all_to_all | solution.py:75
Sparse Core Ops, SparseCore 0:
  10.2 38.5 all-gather.1

commit v2 on v1

--- a/solution.py
+++ b/solution.py
@@ -44,8 +44,7 @@
 
     @pl.when(expert == 0)
     def _():
-        squares = jnp.sum(squares_ref[...], axis=0, keepdims=True)
-        root_mean = jnp.sqrt(squares / width + epsilon)
+        root_mean = jnp.sqrt(squares_ref[...] / width + epsilon)
         inner = jnp.sum(inner_ref[...], axis=0, keepdims=True) / width
         root_column, inner_column = column(root_mean), column(inner)
         scaled = input_ref[...].astype(jnp.float32) / root_column
@@ -71,10 +70,6 @@
     )
 
 
-def swapped(parts, axis):
-    return lax.all_to_all(parts, axis, 0, 0, tiled=True)
-
-
 def on_device(stream_grad, value_grad, attn_input, norm_gain, value_weight, gate_logits, routes):
     group, columns = attn_input.shape
     experts = lax.axis_size(EXPERT)
@@ -89,11 +84,6 @@
 
     every_value = lax.all_gather(value_grad, EXPERT, axis=0, tiled=True)
 
-    weight = to_all(value_weight, "zh")
-    weight = to_all(weight, "zl")
-    weight = to_all(weight, "x")
-    weight = jnp.transpose(weight, (2, 1, 0, 3, 4)).reshape(features, columns)
-
     slot, gate = pl.pallas_call(
         route_kernel,
         in_specs=[vmem, vmem],
@@ -107,8 +97,14 @@
 
     inputs = attn_input.astype(jnp.float32)
     own_squares = jnp.sum(inputs * inputs, axis=1)
-    squares = to_all(own_squares.reshape(8, group // 8), EXPERT).reshape(experts, group)
-    root_mean = jnp.sqrt(jnp.sum(squares, axis=0) / width + epsilon)[:, None]
+    weight = to_all(value_weight, "zh")
+    weight, own_squares = lax.optimization_barrier((weight, own_squares))
+    weight = to_all(weight, "zl")
+    squares = lax.psum(own_squares, EXPERT)
+    weight, squares = lax.optimization_barrier((weight, squares))
+    weight = to_all(weight, "x")
+    weight = jnp.transpose(weight, (2, 1, 0, 3, 4)).reshape(features, columns)
+    root_mean = jnp.sqrt(squares / width + epsilon)[:, None]
     scaled = inputs / root_mean
     normed = (scaled * norm_gain).astype(jnp.bfloat16)
 
@@ -116,7 +112,10 @@
         every_value, normed, (((0,), (0,)), ((), ())), preferred_element_type=jnp.float32
     )
     d_value = d_value.reshape(zh, zl, xs, rows, columns).transpose(2, 1, 0, 3, 4)
-    d_value = swapped(d_value.astype(jnp.bfloat16), "x").astype(jnp.float32).sum(axis=0)
+    d_value = d_value.reshape(features, columns)
+    for axis in ("x", "zl", "zh"):
+        d_value = lax.psum_scatter(d_value, axis, scatter_dimension=0, tiled=True)
+    d_value = (d_value * rescale).astype(jnp.bfloat16)
 
     d_normed = jnp.dot(every_value, weight, preferred_element_type=jnp.float32)
     weighted = d_normed * norm_gain
@@ -128,7 +127,7 @@
         lambda *refs: dispatch_kernel(width, *refs),
         grid=(experts,),
         in_specs=[
-            pl.BlockSpec((experts, group), lambda e: (0, 0)),
+            pl.BlockSpec((1, group), lambda e: (0, 0)),
             pl.BlockSpec((experts, group), lambda e: (0, 0)),
             pl.BlockSpec((1, columns), lambda e: (0, 0)),
             pl.BlockSpec((experts, group), lambda e: (0, 0)),
@@ -143,17 +142,13 @@
         compiler_params=pltpu.CompilerParams(
             dimension_semantics=("arbitrary",), vmem_limit_bytes=40 * 2**20
         ),
-    )(squares, inner, norm_gain[None], slot, gate, stream_grad, attn_input, d_normed)
+    )(squares[None], inner, norm_gain[None], slot, gate, stream_grad, attn_input, d_normed)
     arrived = lax.all_to_all(sent, EXPERT, split_axis=0, concat_axis=2, tiled=True)
 
-    d_value = swapped(d_value, "zl").sum(axis=0)
-    d_value = swapped(d_value, "zh").sum(axis=0)
-    d_value = (d_value * rescale).astype(jnp.bfloat16)
-
-    d_gain = own_gain.reshape(4, columns // 4)
+    d_gain = own_gain
     for axis in ("x", "zl", "zh"):
-        d_gain = to_all(d_gain, axis).sum(axis=0)
-    d_gain = d_gain.reshape(columns) * rescale
+        d_gain = lax.psum(d_gain, axis)
+    d_gain = d_gain * rescale
     return (d_value, d_gain, arrived)
 
 

time: 231 us -> 192 us (0.83)
  waiting for transfers between devices: 91.9 us -> 45.9 us
  blocking collectives: 34.4 us -> 65 us
  starting transfers between devices: 48.7 us -> 34.8 us
  local copies, waits for them, and re-layouts: 14.6 us -> 9.42 us
  other arithmetic: 5.97 us -> 3.45 us
    psum x0 -> x4, blocking collectives: none -> 44.6 us  [the longest x3 30.7 us: on_device(): d_gain = lax.psum(d_gain, axis)]
    all_to_all x1, waiting for transfers between devices: 30.2 us -> 0.01 us  [on_device(): lax.all_to_all(sent, EXPERT, split_axis=0, concat_axis=2, tiled=True)]
    reduce_scatter x0 -> x3, waiting for transfers between devices: none -> 29 us  [on_device(): d_value = lax.psum_scatter(d_value, axis, scatter_dimension=0, tiled=True)]
    all_to_all x3 -> x0, waiting for transfers between devices: 24.1 us -> none  [swapped(): return lax.all_to_all(parts, axis, 0, 0, tiled=True)]
    all_to_all x6 -> x3, waiting for transfers between devices: 36.8 us -> 15.4 us  [to_all(): lax.all_to_all(jnp.broadcast_to(part[None], (size,) + part.shape), axis,...]
    all_to_all x2 -> x1, blocking collectives: 34.4 us -> 20.4 us  [to_all(): lax.all_to_all(jnp.broadcast_to(part[None], (size,) + part.shape), axis,...]
    all_to_all x3 -> x0, starting transfers between devices: 11.7 us -> none  [swapped(): return lax.all_to_all(parts, axis, 0, 0, tiled=True)]
    convert_element_type x2 -> x0, local copies, waits for them, and re-layouts: 4.57 us -> none  [on_device(): d_value.astype(jnp.bfloat16)]
  transfers between devices with their start and end apart: 11 -> 8, of which waited for: 8 -> 4; matrix products, arithmetic and copies ran while one was open for 9% -> 4% of each run, Pallas kernels for 4% -> 5%
where the time goes in v2:
time: 192 us; the launch traced here: 188 us
  blocking collectives  65 us (34%)
  waiting for transfers between devices  45.9 us (24%)
  starting transfers between devices  34.8 us (18%)
  between operations  13.9 us (7%)
  Pallas kernels  9.84 us (5%)
  local copies, waits for them, and re-layouts  9.42 us (5%)
  matrix products  5.82 us (3%)
  other arithmetic  3.45 us (2%)
    psum x3, blocking collectives, on_device(): d_gain = lax.psum(d_gain, axis)  30.7 us
    all_to_all x3, starting transfers between devices, to_all(): lax.all_to_all(jnp.broadcast_to(part[None], (size,) + part.shape), axis,...  30.4 us
    reduce_scatter x3, waiting for transfers between devices, on_device(): d_value = lax.psum_scatter(d_value, axis, scatter_dimension=0, tiled=True)  29 us
    all_to_all x1, blocking collectives, to_all(): lax.all_to_all(jnp.broadcast_to(part[None], (size,) + part.shape), axis,...  20.4 us
    all_to_all x3, waiting for transfers between devices, to_all(): lax.all_to_all(jnp.broadcast_to(part[None], (size,) + part.shape), axis,...  15.4 us
    psum x1, blocking collectives, on_device(): squares = lax.psum(own_squares, EXPERT)  13.9 us
    pallas_call x1, Pallas kernels, on_device(): pl.pallas_call(lambda *refs: dispatch_kernel(width, *refs), grid=(experts...  9.53 us
    dot_general x1, matrix products, on_device(): lax.dot_general(every_value, normed, (((0,), (0,)), ((), ())), preferred_...  4.29 us
  transfers between devices with their start and end apart: 8, of which 4 were waited for; matrix products, arithmetic and copies ran while one was open for 4% of the time, Pallas kernels for 5%

profile of v2, /device:TPU:1, one launch (start us, length us, event | category | flops | bytes accessed | tf_op | source)
XLA Modules:
  0.0 188.0 jit_solution(4530923478974014537)
XLA Ops:
  7.9 1.4 broadcast_in_dim.14
  9.3 15.6 %all-to-all-start = ((bf16[4,16,512]{2,1,0:T(8,128)(2,1)}), bf16[4,16,512]{2,1,0:T(8,128)(2,1)S(1)}, u32[]{:S(2)}, u32[]{:S(2)}) async-start(bf16[4,16,512]{2,1,0:T(8,128)(2,1)} %broadcast_in_dim.14), calls=%async_computation | async-start | bytes 131072 | tf_op jit(solution)/shard_map/all_to_all | solution.py:68
  24.9 1.5 fusion
  26.4 11.0 %all-to-all-done = bf16[4,16,512]{2,1,0:T(8,128)(2,1)S(1)} async-done(((bf16[4,16,512]{2,1,0:T(8,128)(2,1)}), bf16[4,16,512]{2,1,0:T(8,128)(2,1)S(1)}, u32[]{:S(2)}, u32[]{:S(2)}) %all-to-all-start) | async-done | bytes 65568 | tf_op jit(solution)/shard_map/all_to_all | solution.py:68
  37.4 0.7 broadcast_in_dim.15
  38.1 3.4 %all-to-all-start.1 = ((bf16[4,4,16,512]{3,2,1,0:T(8,128)(2,1)}), bf16[4,4,16,512]{3,2,1,0:T(8,128)(2,1)S(1)}, u32[]{:S(2)}, u32[]{:S(2)}) async-start(bf16[4,4,16,512]{3,2,1,0:T(8,128)(2,1)} %broadcast_in_dim.15), calls=%async_computation.1 | async-start | bytes 524288 | tf_op jit(solution)/shard_map/all_to_all | solution.py:68
  41.6 13.9 %psum.28 = f32[1024]{0:T(1024)S(1)} all-reduce(f32[1024]{0:T(1024)S(1)} %fusion), channel_id=1, replica_groups=mesh['zh'=4,'zl'=4,'x'=4,'y'=4,'core'=2] {'y','core'}, use_global_device_ids=true, to_apply=%region_1.0 | all-reduce | flops 1024 | bytes 8192 | tf_op jit(solution)/shard_map/psum | solution.py:103
  55.5 4.3 %convolution_bitcast_fusion.1 = f32[1024,512]{0,1:T(8,128)} fusion(bf16[1024,1024]{1,0:T(8,128)(2,1)} %all-gather.2.cloned.1.call-done, f32[512]{0:T(512)S(1)} %copy-done.4, bf16[1024,512]{1,0:T(8,128)(2,1)S(1)} %copy-done, f32[1024]{0:T(1024)S(1)} %add_sqrt_fusion), kind=kOutput, calls=%fused_computation.7 | convolution fusion | flops 1075838976 | bytes 5249024 | tf_op jit(solution)/shard_map/dot_general | solution.py:111
  59.8 1.9 %copy.19 = f32[1024,512]{1,0:T(8,128)S(1)} copy(f32[1024,512]{0,1:T(8,128)} %convolution_bitcast_fusion.1) | data formatting | bytes 4194304 | tf_op jit(solution)/shard_map/dot_general | solution.py:111
  61.8 1.5 copy.20
  63.4 20.4 %all_to_all.38 = bf16[4,4,4,16,512]{4,3,1,2,0:T(8,128)(2,1)S(1)} all-to-all(bf16[4,4,4,16,512]{4,3,1,2,0:T(8,128)(2,1)S(1)} %broadcast_in_dim.16), channel_id=1, replica_groups=mesh['zh'=4,'zl'=4,'x'=4,'y'=4,'core'=2] {'x'}, dimensions={0} | all-to-all | bytes 2097152 | tf_op jit(solution)/shard_map/all_to_all | solution.py:68
  83.9 1.5 multiply_reduce_fusion
  86.1 11.3 %all-to-all-start.3 = ((f32[8,8,128]{2,1,0:T(8,128)}), f32[8,8,128]{2,1,0:T(8,128)S(1)}, u32[]{:S(2)}, u32[]{:S(2)}) async-start(f32[8,8,128]{2,1,0:T(8,128)} %broadcast_in_dim.19), calls=%async_computation.6 | async-start | bytes 65536 | tf_op jit(solution)/shard_map/all_to_all | solution.py:68
  97.7 4.4 %all-to-all-done.3 = f32[8,8,128]{2,1,0:T(8,128)S(1)} async-done(((f32[8,8,128]{2,1,0:T(8,128)}), f32[8,8,128]{2,1,0:T(8,128)S(1)}, u32[]{:S(2)}, u32[]{:S(2)}) %all-to-all-start.3) | async-done | bytes 32800 | tf_op jit(solution)/shard_map/all_to_all | solution.py:68
  102.2 1.2 copy-done.1
  103.4 9.5 %shard_map.95 = bf16[8,320,512]{2,1,0:T(8,128)(2,1)} custom-call(f32[1,1024]{1,0:T(1,128)S(1)} %bitcast.29, f32[8,1024]{1,0:T(8,128)S(1)} %bitcast.28, f32[1,512]{1,0:T(1,128)S(1)} %bitcast.32, s32[8,1024]{1,0:T(8,128)S(1)} %get-tuple-element.13.refs_3_, f32[8,1024]{1,0:T(8,128)S(1)} %get-tuple-element.14.refs_4_, bf16[1024,512]{1,0:T(8,128)(2,1)S(1)} %copy-done.1, ...), custom_call_target="tpu_custom_call" | custom-call | tf_op jit(solution)/shard_map/pallas_call | solution.py:126
  112.9 4.3 %all-to-all-start.4 = ((bf16[8,320,512]{2,1,0:T(8,128)(2,1)}), bf16[8,320,512]{2,1,0:T(8,128)(2,1)S(1)}, u32[]{:S(2)}, u32[]{:S(2)}) async-start(bf16[8,320,512]{2,1,0:T(8,128)(2,1)} %shard_map.95), calls=%async_computation.7 | async-start | bytes 5242880 | tf_op jit(solution)/shard_map/all_to_all | solution.py:146
  118.0 25.3 %reduce-scatter.6.cloned.1.call-done = f32[64,512]{1,0:T(8,128)} async-done(((f32[256,512]{1,0:T(8,128)}), f32[64,512]{1,0:T(8,128)}) %reduce-scatter.6.cloned.1.call-update) | async-done | bytes 131088 | tf_op jit(solution)/shard_map/reduce_scatter | solution.py:117
  143.3 8.6 %psum.29 = f32[512]{0:T(512)S(1)} all-reduce(f32[512]{0:T(512)S(1)} %get-tuple-element.16), channel_id=1, replica_groups=mesh['zh'=4,'zl'=4,'x'=4,'y'=4,'core'=2] {'x'}, use_global_device_ids=true, to_apply=%region_6.0 | all-reduce | flops 512 | bytes 4096 | tf_op jit(solution)/shard_map/psum | solution.py:150
  151.9 8.2 %psum.30 = f32[512]{0:T(512)S(1)} all-reduce(f32[512]{0:T(512)S(1)} %psum.29), channel_id=1, replica_groups=mesh['zh'=4,'zl'=4,'x'=4,'y'=4,'core'=2] {'zl'}, use_global_device_ids=true, to_apply=%region_7.0 | all-reduce | flops 512 | bytes 4096 | tf_op jit(solution)/shard_map/psum | solution.py:150
  160.1 13.9 %psum.31 = f32[512]{0:T(512)S(1)} all-reduce(f32[512]{0:T(512)S(1)} %psum.30), channel_id=1, replica_groups=mesh['zh'=4,'zl'=4,'x'=4,'y'=4,'core'=2] {'zh'}, use_global_device_ids=true, to_apply=%region_8.0 | all-reduce | flops 512 | bytes 4096 | tf_op jit(solution)/shard_map/psum | solution.py:150
  174.6 1.9 copy.26
  176.5 3.7 %reduce-scatter.8.cloned.1.call-done = f32[16,512]{1,0:T(8,128)} async-done(((f32[64,512]{1,0:T(8,128)}), f32[16,512]{1,0:T(8,128)}) %reduce-scatter.8.cloned.1.call-update) | async-done | bytes 32784 | tf_op jit(solution)/shard_map/reduce_scatter | solution.py:117
  180.1 1.4 multiply_convert_fusion.2
  (31 shorter events, 3.3 us)
Async XLA Ops:
  7.2 48.4 %copy-start = (bf16[1024,512]{1,0:T(8,128)(2,1)S(1)}, bf16[1024,512]{1,0:T(8,128)(2,1)}, u32[]{:S(2)}) copy-start(bf16[1024,512]{1,0:T(8,128)(2,1)} %refs_6_.1) | copy-start | bytes 3145732
  7.2 48.4 %copy-start.4 = (f32[512]{0:T(512)S(1)}, f32[512]{0:T(512)}, u32[]{:S(2)}) copy-start(f32[512]{0:T(512)} %param.10) | copy-start | bytes 6148
  7.2 48.3 %all-gather.2.cloned.1.call-start = ((), (), s32[]{:S(2)}) async-start(), calls=%async_computation.8 | async-start | bytes 2359296 | tf_op jit(solution)/shard_map/all_gather | solution.py:85
  9.3 28.1 %all-to-all-start = ((bf16[4,16,512]{2,1,0:T(8,128)(2,1)}), bf16[4,16,512]{2,1,0:T(8,128)(2,1)S(1)}, u32[]{:S(2)}, u32[]{:S(2)}) async-start(bf16[4,16,512]{2,1,0:T(8,128)(2,1)} %broadcast_in_dim.14), calls=%async_computation | async-start | bytes 131072 | tf_op jit(solution)/shard_map/all_to_all | solution.py:68
  38.1 17.3 %all-to-all-start.1 = ((bf16[4,4,16,512]{3,2,1,0:T(8,128)(2,1)}), bf16[4,4,16,512]{3,2,1,0:T(8,128)(2,1)S(1)}, u32[]{:S(2)}, u32[]{:S(2)}) async-start(bf16[4,4,16,512]{3,2,1,0:T(8,128)(2,1)} %broadcast_in_dim.15), calls=%async_computation.1 | async-start | bytes 524288 | tf_op jit(solution)/shard_map/all_to_all | solution.py:68
  41.6 75.7 %reduce-scatter.4.cloned.1.call-start = ((), (), s32[]{:S(2)}) async-start(), calls=%async_computation.9 | async-start | bytes 2621440 | tf_op jit(solution)/shard_map/reduce_scatter | solution.py:117
  63.4 20.5 %copy-start.5 = (bf16[1024,1024]{1,0:T(8,128)(2,1)S(1)}, bf16[1024,1024]{1,0:T(8,128)(2,1)}, u32[]{:S(2)}) copy-start(bf16[1024,1024]{1,0:T(8,128)(2,1)} %all-gather.2.cloned.1.call-done) | copy-start | bytes 6291460
  83.9 13.5 %copy-start.2 = (s32[1024,2]{0,1:T(2,128)S(1)}, s32[1024,2]{0,1:T(2,128)}, u32[]{:S(2)}) copy-start(s32[1024,2]{0,1:T(2,128)} %param.13) | copy-start | bytes 24580
  83.9 13.5 %copy-start.3 = (f32[1024,2]{0,1:T(2,128)S(1)}, f32[1024,2]{0,1:T(2,128)}, u32[]{:S(2)}) copy-start(f32[1024,2]{0,1:T(2,128)} %param.12) | copy-start | bytes 24580
  86.1 16.1 %all-to-all-start.3 = ((f32[8,8,128]{2,1,0:T(8,128)}), f32[8,8,128]{2,1,0:T(8,128)S(1)}, u32[]{:S(2)}, u32[]{:S(2)}) async-start(f32[8,8,128]{2,1,0:T(8,128)} %broadcast_in_dim.19), calls=%async_computation.6 | async-start | bytes 65536 | tf_op jit(solution)/shard_map/all_to_all | solution.py:68
  102.2 1.2 copy-start.1
  112.9 61.7 %all-to-all-start.4 = ((bf16[8,320,512]{2,1,0:T(8,128)(2,1)}), bf16[8,320,512]{2,1,0:T(8,128)(2,1)S(1)}, u32[]{:S(2)}, u32[]{:S(2)}) async-start(bf16[8,320,512]{2,1,0:T(8,128)(2,1)} %shard_map.95), calls=%async_computation.7 | async-start | bytes 5242880 | tf_op jit(solution)/shard_map/all_to_all | solution.py:146
  117.2 26.1 %reduce-scatter.6.cloned.1.call-start = ((), (), s32[]{:S(2)}) async-start(), calls=%async_computation.10 | async-start | bytes 655360 | tf_op jit(solution)/shard_map/reduce_scatter | solution.py:117
  117.9 62.2 %reduce-scatter.8.cloned.1.call-start = ((), (), s32[]{:S(2)}) async-start(), calls=%async_computation.11 | async-start | bytes 163840 | tf_op jit(solution)/shard_map/reduce_scatter | solution.py:117
Sparse Core Ops, SparseCore 0:
  10.2 38.5 all-gather.1
  63.4 37.2 reduce-scatter.3
  121.1 22.1 reduce-scatter.5
  146.2 33.9 reduce-scatter.7

commit v3 on v2

v3 whole, which is shorter than its diff:
```python
import jax
import jax.numpy as jnp
from jax import lax
from jax.experimental import pallas as pl
from jax.experimental.pallas import tpu as pltpu
from jax.sharding import Mesh, PartitionSpec as P

epsilon = 1e-05
EXPERT = ("y", "core")
VMEM = pl.BlockSpec(memory_space=pltpu.VMEM)
SMEM = pl.BlockSpec(memory_space=pltpu.SMEM)
PAD = 16


def call(kernel, *operands, out, limit=32):
    return pl.pallas_call(
        kernel,
        in_specs=[SMEM if o.shape == (1,) else VMEM for o in operands],
        out_specs=[VMEM] * len(out),
        out_shape=[jax.ShapeDtypeStruct(shape, kind) for shape, kind in out],
        compiler_params=pltpu.CompilerParams(vmem_limit_bytes=limit * 2**20),
    )(*operands)


def column(row):
    return jnp.transpose(jnp.broadcast_to(row, (8, row.shape[1])))[:, 0:1]


def pieces(row):
    high = row.astype(jnp.bfloat16).astype(jnp.float32)
    middle = (row - high).astype(jnp.bfloat16).astype(jnp.float32)
    low = row - high - middle
    at = lax.broadcasted_iota(jnp.int32, (PAD, row.shape[1]), 0)
    rows = jnp.where(at == 0, high, jnp.where(at == 1, middle, jnp.where(at == 2, low, 0.0)))
    return rows.astype(jnp.bfloat16)


def pack_kernel(value_ref, input_ref, weight_ref, packed_ref, copies_ref):
    rows = value_ref.shape[0]
    inputs = input_ref[...].astype(jnp.float32)
    squares = jnp.sum(inputs * inputs, axis=1, keepdims=True)
    row = jnp.transpose(jnp.broadcast_to(squares, (squares.shape[0], 8)))[0:1, :]
    packed_ref[0:rows, :] = value_ref[...]
    packed_ref[rows:, :] = pieces(row)
    for peer in range(copies_ref.shape[0]):
        copies_ref[peer] = weight_ref[...]


def route_kernel(routes_ref, logits_ref, slot_ref, gate_ref):
    experts, group = slot_ref.shape
    expert = lax.broadcasted_iota(jnp.int32, (experts, group), 0)
    first = routes_ref[0:1, :] == expert
    second = routes_ref[1:2, :] == expert
    named = jnp.where(first | second, 1.0, 0.0)
    earlier = lax.broadcasted_iota(jnp.int32, (group, group), 0) < lax.broadcasted_iota(
        jnp.int32, (group, group), 1
    )
    count = jnp.dot(
        named.astype(jnp.bfloat16),
        jnp.where(earlier, 1.0, 0.0).astype(jnp.bfloat16),
        preferred_element_type=jnp.float32,
    )
    slot_ref[...] = jnp.where(named > 0.0, count, -1.0).astype(jnp.int32)
    low, high = logits_ref[0:1, :], logits_ref[1:2, :]
    gate_first = 1.0 / (1.0 + jnp.exp(high - low))
    gate_second = 1.0 / (1.0 + jnp.exp(low - high))
    gate_ref[...] = jnp.where(first, gate_first, jnp.where(second, gate_second, 0.0))


def value_kernel(width, gathered_ref, input_ref, gain_ref, d_value_ref, value_ref, inverse_ref):
    devices, packed, features = gathered_ref.shape
    rows = packed - PAD
    group = input_ref.shape[0]
    squares = jnp.zeros((1, features), jnp.float32)
    for device in range(devices):
        part = gathered_ref[device, rows:, :].astype(jnp.float32)
        squares += jnp.sum(part, axis=0, keepdims=True)
        value_ref[device * rows : (device + 1) * rows, :] = gathered_ref[device, 0:rows, :]
    inverse = 1.0 / jnp.sqrt(squares / width + epsilon)
    tile = group // 8
    for at in range(8):
        inverse_ref[at : at + 1, :] = inverse[:, at * tile : (at + 1) * tile]
    scaled = input_ref[...].astype(jnp.float32) * column(inverse)
    normed = (scaled * gain_ref[...]).astype(jnp.bfloat16)
    xs, zl, zh, own, _ = d_value_ref.shape
    block = features // zh
    for high in range(zh):
        partial = lax.dot_general(
            value_ref[:, high * block : (high + 1) * block],
            normed,
            (((0,), (0,)), ((), ())),
            preferred_element_type=jnp.float32,
        )
        for low in range(zl):
            for x in range(xs):
                start = (low * xs + x) * own
                d_value_ref[x, low, high] = partial[start : start + own, :]


def dispatch_kernel(
    width, inverse_ref, inner_ref, slot_ref, gate_ref, base_ref, input_ref, out_ref, stream_ref
):
    expert = pl.program_id(0)
    group = input_ref.shape[0]
    capacity = out_ref.shape[1]

    @pl.when(expert == 0)
    def _():
        inverse = inverse_ref[...]
        inner = jnp.sum(inner_ref[...], axis=0) / width
        factor = jnp.transpose(inner * inverse * inverse)
        tile = group // 8
        for at in range(8):
            rows = pl.ds(at * tile, tile)
            stream_ref[rows, :] = (
                base_ref[rows, :]
                - input_ref[rows, :].astype(jnp.float32) * factor[:, at : at + 1]
            )

    slot = slot_ref[pl.ds(expert, 1), :]
    gate = column(gate_ref[pl.ds(expert, 1), :])
    rows = (gate * stream_ref[...]).astype(jnp.bfloat16)
    taken = lax.broadcasted_iota(jnp.int32, (capacity, group), 0) == slot
    picked = jnp.dot(
        jnp.where(taken, 1.0, 0.0).astype(jnp.bfloat16), rows, preferred_element_type=jnp.float32
    )
    out_ref[0] = picked.astype(jnp.bfloat16)


def low_split_kernel(me_ref, d_value_ref, d_gain_ref, *outs):
    count = len(outs)
    rows = d_value_ref.shape[0] // count
    behind = pieces(d_gain_ref[...])
    for k, out in enumerate(outs):
        start = pl.multiple_of(lax.rem(me_ref[0] + k, count) * rows, rows)
        out[0:rows, :] = d_value_ref[pl.ds(start, rows), :].astype(jnp.bfloat16)
        out[rows:, :] = behind


def high_split_kernel(me_ref, a_ref, b_ref, c_ref, d_ref, sum_ref, *outs):
    count = len(outs)
    total = a_ref[...].astype(jnp.float32)
    for ref in (b_ref, c_ref, d_ref):
        total += ref[...].astype(jnp.float32)
    sum_ref[...] = total
    rows = total.shape[0] - PAD
    gain = jnp.sum(total[rows:, :], axis=0, keepdims=True)
    own = rows // count
    for k, out in enumerate(outs):
        start = pl.multiple_of(lax.rem(me_ref[0] + k, count) * own, own)
        out[0:own, :] = sum_ref[pl.ds(start, own), :]
        out[own:, :] = jnp.broadcast_to(gain, (8, gain.shape[1]))


def finish_kernel(rescale, a_ref, b_ref, c_ref, d_ref, d_value_ref, d_gain_ref):
    total = (a_ref[...] + b_ref[...]) + (c_ref[...] + d_ref[...])
    rows = d_value_ref.shape[0]
    d_value_ref[...] = (total[0:rows, :] * rescale).astype(jnp.bfloat16)
    d_gain_ref[...] = total[rows : rows + 1, :] * rescale


def to_all(part, axis):
    size = lax.axis_size(axis)
    return lax.all_to_all(
        jnp.broadcast_to(part[None], (size,) + part.shape), axis, 0, 0, tiled=True
    )


def further(part, axis, step):
    size = lax.axis_size(axis)
    return lax.ppermute(part, axis, [(i, (i + step) % size) for i in range(size)])


def on_device(stream_grad, value_grad, attn_input, norm_gain, value_weight, gate_logits, routes):
    group, columns = attn_input.shape
    experts = lax.axis_size(EXPERT)
    zh, zl, xs = lax.axis_size("zh"), lax.axis_size("zl"), lax.axis_size("x")
    width = columns * experts
    tokens_all = group * zh * zl * xs
    rescale = float(tokens_all) ** (-0.5)
    capacity = min(group, 5 * group // (2 * experts))
    rows = value_weight.shape[0]
    features = rows * zh * zl * xs
    own_rows = value_grad.shape[0]
    f32, bf16 = jnp.float32, jnp.bfloat16
    gain_row = norm_gain[None]
    me_x = lax.axis_index("x").astype(jnp.uint32)

    packed, copies = call(
        pack_kernel, value_grad, attn_input, value_weight,
        out=[((own_rows + PAD, features), bf16), ((zh, rows, columns), bf16)],
    )
    gathered = lax.all_gather(packed, EXPERT, axis=0)

    weight = to_all(lax.all_to_all(copies, "zh", 0, 0, tiled=True), "zl")
    weight = jnp.transpose(weight, (1, 0, 2, 3))
    others = [further(weight, "x", step) for step in range(1, xs)]
    gathered, others[0] = lax.optimization_barrier((gathered, others[0]))
    every_weight = jnp.zeros((zh, zl, xs, rows, columns), bf16)
    for step, part in enumerate([weight] + others):
        place = lax.rem(me_x + jnp.uint32(xs - step), jnp.uint32(xs))
        zero = jnp.uint32(0)
        every_weight = lax.dynamic_update_slice(
            every_weight, part[:, :, None], (zero, zero, place, zero, zero)
        )
    every_weight = every_weight.reshape(features, columns)

    slot, gate = call(
        route_kernel, routes.T, gate_logits.T,
        out=[((experts, group), jnp.int32), ((experts, group), f32)],
    )

    d_value, every_value, inverse = call(
        lambda *refs: value_kernel(width, *refs), gathered, attn_input, gain_row,
        out=[
            ((xs, zl, zh, rows, columns), f32),
            ((group, features), bf16),
            ((8, group // 8), f32),
        ],
        limit=40,
    )
    d_value = lax.psum_scatter(
        d_value.reshape(features, columns), "x", scatter_dimension=0, tiled=True
    )

    inverse_column = inverse.reshape(group)[:, None]
    scaled = attn_input.astype(f32) * inverse_column
    d_normed = jnp.dot(every_value, every_weight, preferred_element_type=f32)
    weighted = d_normed * norm_gain
    own_inner = jnp.sum(weighted * scaled, axis=1)
    own_gain = jnp.sum(d_normed * scaled, axis=0)
    base = stream_grad.astype(f32) + weighted * inverse_column
    inner = to_all(own_inner.reshape(8, group // 8), EXPERT)

    whole = lambda *shape: pl.BlockSpec(shape, lambda e: (0,) * len(shape))
    sent = pl.pallas_call(
        lambda *refs: dispatch_kernel(width, *refs),
        grid=(experts,),
        in_specs=[
            whole(8, group // 8),
            whole(experts, 8, group // 8),
            whole(experts, group),
            whole(experts, group),
            whole(group, columns),
            whole(group, columns),
        ],
        out_specs=pl.BlockSpec((1, capacity, columns), lambda e: (e, 0, 0)),
        out_shape=jax.ShapeDtypeStruct((experts, capacity, columns), bf16),
        scratch_shapes=[pltpu.VMEM((group, columns), f32)],
        compiler_params=pltpu.CompilerParams(
            dimension_semantics=("arbitrary",), vmem_limit_bytes=40 * 2**20
        ),
        cost_estimate=pl.CostEstimate(flops=15 * 10**9, bytes_accessed=10**7, transcendentals=0),
    )(inverse, inner, slot, gate, base, attn_input)
    sent, own_gain = lax.optimization_barrier((sent, own_gain))
    arrived = lax.all_to_all(sent, EXPERT, split_axis=0, concat_axis=2, tiled=True)

    d_gain = lax.psum(own_gain, "x")
    part = (features // xs // zl + PAD, columns)
    parts = call(
        low_split_kernel, lax.axis_index("zl").reshape(1), d_value, d_gain[None],
        out=[(part, bf16)] * zl,
    )
    parts = [parts[0]] + [further(parts[k], "zl", k) for k in range(1, zl)]
    part = (rows + 8, columns)
    _, *parts = call(
        high_split_kernel, lax.axis_index("zh").reshape(1), *parts,
        out=[(parts[0].shape, f32)] + [(part, f32)] * zh,
    )
    parts = [parts[0]] + [further(parts[k], "zh", k) for k in range(1, zh)]
    d_value, d_gain = call(
        lambda *refs: finish_kernel(rescale, *refs), *parts,
        out=[((rows, columns), bf16), ((1, columns), f32)],
    )
    return (d_value, d_gain.reshape(columns), arrived)


def solution(mesh):
    split = Mesh(mesh.devices.reshape(4, 4, 4, 4, 2), ("zh", "zl", "x", "y", "core"))
    dp = ("zh", "zl", "x")
    return jax.shard_map(
        on_device,
        mesh=split,
        in_specs=(
            P(dp, EXPERT),
            P(dp + EXPERT, None),
            P(dp, EXPERT),
            P(EXPERT),
            P(dp, EXPERT),
            P(dp, None),
            P(dp, None),
        ),
        out_specs=(P(dp, EXPERT), P(EXPERT), P(EXPERT, dp, None)),
        check_vma=False,
    )
```

time: 192 us -> 159 us (0.83); the launches traced: 188 us -> 158 us
  waiting for transfers between devices: 45.9 us -> 16.9 us
  blocking collectives: 65 us -> 43.8 us
  starting transfers between devices: 34.8 us -> 45.4 us
  local copies, waits for them, and re-layouts: 9.42 us -> 18.9 us
  Pallas kernels: 9.84 us -> 14 us
  other arithmetic: 3.45 us -> 0 us
    psum x4 -> x1, blocking collectives: 44.6 us -> 7.03 us  [on_device(): d_gain = lax.psum(own_gain, 'x')]
    ppermute x0 -> x9, starting transfers between devices: none -> 31.1 us  [further(): lax.ppermute(part, axis, [(i, (i + step) % size) for i in range(size)])]
    reduce_scatter x3 -> x1, waiting for transfers between devices: 29 us -> 0.01 us  [on_device(): lax.psum_scatter(d_value.reshape(features, columns), 'x', scatter_dimensi...]
    all_to_all x0 -> x1, blocking collectives: none -> 27.9 us  [on_device(): weight = to_all(lax.all_to_all(copies, 'zh', 0, 0, tiled=True), 'zl')]
    all_to_all x3 -> x1, starting transfers between devices: 30.4 us -> 9.25 us  [to_all(): lax.all_to_all(jnp.broadcast_to(part[None], (size,) + part.shape), axis,...]
    ppermute x0 -> x9, waiting for transfers between devices: none -> 12.5 us  [further(): lax.ppermute(part, axis, [(i, (i + step) % size) for i in range(size)])]
    all_to_all x1, blocking collectives: 20.4 us -> 8.85 us  [to_all(): lax.all_to_all(jnp.broadcast_to(part[None], (size,) + part.shape), axis,...]
    all_to_all x3 -> x1, waiting for transfers between devices: 15.4 us -> 4.42 us  [to_all(): lax.all_to_all(jnp.broadcast_to(part[None], (size,) + part.shape), axis,...]
  transfers between devices with their start and end apart: 8 -> 13, of which waited for: 4 -> 5; matrix products, arithmetic and copies ran while one was open for 4% -> 9% of each run, Pallas kernels for 5% -> 8%
where the time goes in v3:
time: 159 us; the launch traced here: 158 us
  starting transfers between devices  45.4 us (29%)
  blocking collectives  43.8 us (28%)
  local copies, waits for them, and re-layouts  18.9 us (12%)
  waiting for transfers between devices  16.9 us (11%)
  between operations  14.2 us (9%)
  Pallas kernels  14 us (9%)
  matrix products  4.55 us (3%)
    ppermute x9, starting transfers between devices, further(): lax.ppermute(part, axis, [(i, (i + step) % size) for i in range(size)])  31.1 us
    all_to_all x1, blocking collectives, on_device(): weight = to_all(lax.all_to_all(copies, 'zh', 0, 0, tiled=True), 'zl')  27.9 us
    ppermute x9, waiting for transfers between devices, further(): lax.ppermute(part, axis, [(i, (i + step) % size) for i in range(size)])  12.5 us
    unnamed x24, local copies, waits for them, and re-layouts  9.66 us
    all_to_all x1, starting transfers between devices, to_all(): lax.all_to_all(jnp.broadcast_to(part[None], (size,) + part.shape), axis,...  9.25 us
    all_to_all x1, blocking collectives, to_all(): lax.all_to_all(jnp.broadcast_to(part[None], (size,) + part.shape), axis,...  8.85 us
    pallas_call x1, Pallas kernels, on_device(): pl.pallas_call(lambda *refs: dispatch_kernel(width, *refs), grid=(experts...  8.07 us
    psum x1, blocking collectives, on_device(): d_gain = lax.psum(own_gain, 'x')  7.03 us
  transfers between devices with their start and end apart: 13, of which 5 were waited for; matrix products, arithmetic and copies ran while one was open for 9% of the time, Pallas kernels for 8%

profile of v3, /device:TPU:1, one launch (start us, length us, event | category | flops | bytes accessed | tf_op | source)
XLA Modules:
  0.0 157.8 jit_solution(2521838321710944858)
XLA Ops:
  11.3 27.9 %all_to_all.33 = bf16[4,16,512]{2,1,0:T(8,128)(2,1)S(1)} all-to-all(bf16[4,16,512]{2,1,0:T(8,128)(2,1)S(1)} %get-tuple-element.25), channel_id=1, replica_groups=mesh['zh'=4,'zl'=4,'x'=4,'y'=4,'core'=2] {'zh'}, dimensions={0} | all-to-all | bytes 131072 | tf_op jit(solution)/shard_map/all_to_all | solution.py:195
  39.3 8.9 %all_to_all.34 = bf16[4,4,16,512]{3,2,1,0:T(8,128)(2,1)S(1)} all-to-all(bf16[4,4,16,512]{3,2,1,0:T(8,128)(2,1)S(1)} %broadcast_in_dim.35), channel_id=1, replica_groups=mesh['zh'=4,'zl'=4,'x'=4,'y'=4,'core'=2] {'zl'}, dimensions={0} | all-to-all | bytes 524288 | tf_op jit(solution)/shard_map/all_to_all | solution.py:164
  48.8 3.1 %collective-permute-start = (bf16[4,4,16,512]{3,2,1,0:T(8,128)(2,1)}, bf16[4,4,16,512]{3,2,1,0:T(8,128)(2,1)S(1)}, u32[]{:S(2)}, u32[]{:S(2)}) collective-permute-start(bf16[4,4,16,512]{3,2,1,0:T(8,128)(2,1)} %bitcast.36), channel_id=1, source_target_pairs={{0,8},{8,16},{16,24},{24,0},{1,9},{9,17},{17,25},{25,1},{2,10},{10... | collective-permute-start | bytes 786440 | tf_op jit(solution)/shard_map/ppermute | solution.py:171
  51.9 4.3 %collective-permute-start.1 = (bf16[4,4,16,512]{3,2,1,0:T(8,128)(2,1)}, bf16[4,4,16,512]{3,2,1,0:T(8,128)(2,1)}, u32[]{:S(2)}, u32[]{:S(2)}) collective-permute-start(bf16[4,4,16,512]{3,2,1,0:T(8,128)(2,1)} %bitcast.36), channel_id=1, source_target_pairs={{0,16},{8,24},{16,0},{24,8},{1,17},{9,25},{17,1},{25,9},{2,18},{10... | collective-permute-start | bytes 786440 | tf_op jit(solution)/shard_map/ppermute | solution.py:171
  56.3 3.1 %collective-permute-start.2 = (bf16[4,4,16,512]{3,2,1,0:T(8,128)(2,1)}, bf16[4,4,16,512]{3,2,1,0:T(8,128)(2,1)}, u32[]{:S(2)}, u32[]{:S(2)}) collective-permute-start(bf16[4,4,16,512]{3,2,1,0:T(8,128)(2,1)} %bitcast.36), channel_id=1, source_target_pairs={{0,24},{8,0},{16,8},{24,16},{1,25},{9,1},{17,9},{25,17},{2,26},{10... | collective-permute-start | bytes 786440 | tf_op jit(solution)/shard_map/ppermute | solution.py:171
  60.5 1.7 %copy-done.3 = bf16[1152,1024]{1,0:T(8,128)(2,1)S(1)} copy-done((bf16[1152,1024]{1,0:T(8,128)(2,1)S(1)}, bf16[1152,1024]{1,0:T(8,128)(2,1)}, u32[]{:S(2)}) %copy-start.3) | copy-done | bytes 2359320
  62.2 3.1 %shard_map.95 = (f32[4,4,4,16,512]{4,3,2,1,0:T(8,128)}, bf16[1024,1024]{1,0:T(8,128)(2,1)S(1)}, f32[8,128]{1,0:T(8,128)S(1)}) custom-call(bf16[8,144,1024]{2,1,0:T(8,128)(2,1)S(1)} %bitcast.37, bf16[1024,512]{1,0:T(8,128)(2,1)S(1)} %copy-done.1, f32[1,512]{1,0:T(1,128)S(1)} %bitcast.40), custom_call_target="tpu_custom_call" | custom-call | tf_op jit(solution)/shard_map/pallas_call | solution.py:16
  66.0 1.7 %bitcast_dynamic-update-slice_fusion = bf16[4,4,4,16,512]{4,3,2,1,0:T(8,128)(2,1)} fusion(bf16[4,4,4,16,512]{4,3,2,1,0:T(8,128)(2,1)} %bitcast_dynamic-update-slice_fusion.1, u32[]{:T(128)S(6)} %rem.14, bf16[4,4,16,512]{3,2,1,0:T(8,128)(2,1)} %collective-permute-done.1), kind=kLoop, calls=%fused_computation.4 | loop fusion | bytes 524292 | tf_op jit(solution)/shard_map/dynamic_update_slice | solution.py:203
  67.8 1.7 %bitcast_dynamic-update-slice_fusion.3 = bf16[4,4,4,16,512]{4,3,2,1,0:T(8,128)(2,1)} fusion(bf16[4,4,4,16,512]{4,3,2,1,0:T(8,128)(2,1)} %bitcast_dynamic-update-slice_fusion, u32[]{:T(128)S(6)} %rem.15, bf16[4,4,16,512]{3,2,1,0:T(8,128)(2,1)} %collective-permute-done.2), kind=kLoop, calls=%fused_computation.7 | loop fusion | bytes 524292 | tf_op jit(solution)/shard_map/dynamic_update_slice | solution.py:203
  69.5 4.6 %multiply_reduce_fusion = (f32[512]{0:T(512)S(1)}, f32[1024]{0:T(1024)S(1)}, f32[1024,512]{1,0:T(8,128)}) fusion(bf16[1024,512]{1,0:T(8,128)(2,1)S(1)} %copy-done.1, f32[1024]{0:T(1024)S(1)} %bitcast.41, f32[512]{0:T(512)S(1)} %copy-done.9, bf16[1024,512]{1,0:T(8,128)(2,1)} %param.7, bf16[1024,1024]{1,0:T(8,128)(2,1)S(1)} %get-tuple-element.29, ...), kind=kOutput, calls=%fused_computation | convolution fusion | flops 1078983168 | bytes 7352320 | tf_op jit(solution)/shard_map/dot_general | solution.py:228
  74.7 9.3 %all-to-all-start.2 = ((f32[8,8,128]{2,1,0:T(8,128)}), f32[8,8,128]{2,1,0:T(8,128)S(1)}, u32[]{:S(2)}, u32[]{:S(2)}) async-start(f32[8,8,128]{2,1,0:T(8,128)} %broadcast_in_dim.43), calls=%async_computation.3 | async-start | bytes 65536 | tf_op jit(solution)/shard_map/all_to_all | solution.py:164
  84.2 4.4 %all-to-all-done.2.refs_1_ = f32[8,8,128]{2,1,0:T(8,128)S(1)} async-done(((f32[8,8,128]{2,1,0:T(8,128)}), f32[8,8,128]{2,1,0:T(8,128)S(1)}, u32[]{:S(2)}, u32[]{:S(2)}) %all-to-all-start.2) | async-done | bytes 32800 | tf_op jit(solution)/shard_map/all_to_all | solution.py:164
  90.3 8.1 %shard_map.97 = bf16[8,320,512]{2,1,0:T(8,128)(2,1)S(1)} custom-call(f32[8,128]{1,0:T(8,128)S(1)} %get-tuple-element.28.refs_0_, f32[8,8,128]{2,1,0:T(8,128)S(1)} %all-to-all-done.2.refs_1_, s32[8,1024]{1,0:T(8,128)S(1)} %get-tuple-element.31.refs_2_, f32[8,1024]{1,0:T(8,128)S(1)} %get-tuple-element.32.refs_3_, f32[1024,512]{1,0:T(8,128)S(1)} %copy-done.10, ...), custom_call_target="tpu_custom_call" | custom-call | flops 15000000512 | bytes 10000000 | tf_op jit(solution)/shard_map/pallas_call | solution.py:236
  99.8 5.0 %all-to-all-start.3 = ((bf16[8,320,512]{2,1,0:T(8,128)(2,1)}), bf16[8,320,512]{2,1,0:T(8,128)(2,1)}, u32[]{:S(2)}, u32[]{:S(2)}) async-start(bf16[8,320,512]{2,1,0:T(8,128)(2,1)} %copy-done.2), calls=%async_computation.4 | async-start | bytes 5242880 | tf_op jit(solution)/shard_map/all_to_all | solution.py:256
  104.9 7.0 %psum.7.d_gain_ref = f32[1,512]{1,0:T(1,128)S(1)} all-reduce(f32[1,512]{1,0:T(1,128)S(1)} %bitcast.45), channel_id=1, replica_groups=mesh['zh'=4,'zl'=4,'x'=4,'y'=4,'core'=2] {'x'}, use_global_device_ids=true, to_apply=%region_3.0 | all-reduce | flops 512 | bytes 4096 | tf_op jit(solution)/shard_map/psum | solution.py:258
  113.0 2.2 %collective-permute-start.3 = (bf16[80,512]{1,0:T(8,128)(2,1)S(1)}, bf16[80,512]{1,0:T(8,128)(2,1)S(1)}, u32[]{:S(2)}, u32[]{:S(2)}) collective-permute-start(bf16[80,512]{1,0:T(8,128)(2,1)S(1)} %get-tuple-element.35), channel_id=1, source_target_pairs={{0,32},{32,64},{64,96},{96,0},{1,33},{33,65},{65,97},{97,1},{2,34}... | collective-permute-start | bytes 245768 | tf_op jit(solution)/shard_map/ppermute | solution.py:171
  115.2 3.8 %collective-permute-start.4 = (bf16[80,512]{1,0:T(8,128)(2,1)S(1)}, bf16[80,512]{1,0:T(8,128)(2,1)S(1)}, u32[]{:S(2)}, u32[]{:S(2)}) collective-permute-start(bf16[80,512]{1,0:T(8,128)(2,1)S(1)} %get-tuple-element.36), channel_id=1, source_target_pairs={{0,64},{32,96},{64,0},{96,32},{1,65},{33,97},{65,1},{97,33},{2,66}... | collective-permute-start | bytes 245768 | tf_op jit(solution)/shard_map/ppermute | solution.py:171
  119.0 3.0 %collective-permute-start.5 = (bf16[80,512]{1,0:T(8,128)(2,1)S(1)}, bf16[80,512]{1,0:T(8,128)(2,1)S(1)}, u32[]{:S(2)}, u32[]{:S(2)}) collective-permute-start(bf16[80,512]{1,0:T(8,128)(2,1)S(1)} %get-tuple-element.37), channel_id=1, source_target_pairs={{0,96},{32,0},{64,32},{96,64},{1,97},{33,1},{65,33},{97,65},{2,98}... | collective-permute-start | bytes 245768 | tf_op jit(solution)/shard_map/ppermute | solution.py:171
  122.0 2.4 %collective-permute-done.4.c_ref = bf16[80,512]{1,0:T(8,128)(2,1)S(1)} collective-permute-done((bf16[80,512]{1,0:T(8,128)(2,1)S(1)}, bf16[80,512]{1,0:T(8,128)(2,1)S(1)}, u32[]{:S(2)}, u32[]{:S(2)}) %collective-permute-start.4) | collective-permute-done | bytes 81952 | tf_op jit(solution)/shard_map/ppermute | solution.py:171
  126.3 2.0 %collective-permute-start.6 = (f32[24,512]{1,0:T(8,128)S(1)}, f32[24,512]{1,0:T(8,128)S(1)}, u32[]{:S(2)}, u32[]{:S(2)}) collective-permute-start(f32[24,512]{1,0:T(8,128)S(1)} %get-tuple-element.39), channel_id=1, source_target_pairs={{0,128},{128,256},{256,384},{384,0},{1,129},{129,257},{257,385},{3... | collective-permute-start | bytes 147464 | tf_op jit(solution)/shard_map/ppermute | solution.py:171
  128.3 7.0 %collective-permute-start.7 = (f32[24,512]{1,0:T(8,128)S(1)}, f32[24,512]{1,0:T(8,128)S(1)}, u32[]{:S(2)}, u32[]{:S(2)}) collective-permute-start(f32[24,512]{1,0:T(8,128)S(1)} %get-tuple-element.40), channel_id=1, source_target_pairs={{0,256},{128,384},{256,0},{384,128},{1,257},{129,385},{257,1},{385... | collective-permute-start | bytes 147464 | tf_op jit(solution)/shard_map/ppermute | solution.py:171
  135.4 2.5 %collective-permute-start.8 = (f32[24,512]{1,0:T(8,128)S(1)}, f32[24,512]{1,0:T(8,128)S(1)}, u32[]{:S(2)}, u32[]{:S(2)}) collective-permute-start(f32[24,512]{1,0:T(8,128)S(1)} %get-tuple-element.41), channel_id=1, source_target_pairs={{0,384},{128,0},{256,128},{384,256},{1,385},{129,1},{257,129},{385... | collective-permute-start | bytes 147464 | tf_op jit(solution)/shard_map/ppermute | solution.py:171
  137.9 3.6 %copy.19 = bf16[1,8,40,8,512]{4,3,1,2,0:T(8,128)(2,1)} copy(bf16[1,8,40,8,512]{4,3,2,1,0:T(8,128)(2,1)} %bitcast.27) | data formatting | bytes 5242880 | tf_op jit(solution)/shard_map/all_to_all | solution.py:256
  141.9 8.5 %collective-permute-done.8.refs_3_ = f32[24,512]{1,0:T(8,128)S(1)} collective-permute-done((f32[24,512]{1,0:T(8,128)S(1)}, f32[24,512]{1,0:T(8,128)S(1)}, u32[]{:S(2)}, u32[]{:S(2)}) %collective-permute-start.8) | collective-permute-done | bytes 49184 | tf_op jit(solution)/shard_map/ppermute | solution.py:171
  (48 shorter events, 14.7 us)
Async XLA Ops:
  7.2 53.3 %all-gather.3.cloned.1.call-start = ((), (), s32[]{:S(2)}) async-start(), calls=%async_computation.6 | async-start | bytes 2654208 | tf_op jit(solution)/shard_map/all_gather | solution.py:193
  7.2 1.2 copy-start
  8.4 0.9 copy-start.5
  10.1 50.4 %copy-start.1 = (bf16[1024,512]{1,0:T(8,128)(2,1)S(1)}, bf16[1024,512]{1,0:T(8,128)(2,1)}, u32[]{:S(2)}) copy-start(bf16[1024,512]{1,0:T(8,128)(2,1)} %refs_5_.1) | copy-start | bytes 3145732
  10.1 50.4 %copy-start.9 = (f32[512]{0:T(512)S(1)}, f32[512]{0:T(512)}, u32[]{:S(2)}) copy-start(f32[512]{0:T(512)} %param.10) | copy-start | bytes 6148
  11.2 100.6 %reduce-scatter.2.cloned.1.call-start = ((), (), s32[]{:S(2)}) async-start(), calls=%async_computation.5 | async-start | bytes 2621440 | tf_op jit(solution)/shard_map/reduce_scatter | solution.py:222
  48.8 11.7 %collective-permute-start = (bf16[4,4,16,512]{3,2,1,0:T(8,128)(2,1)}, bf16[4,4,16,512]{3,2,1,0:T(8,128)(2,1)S(1)}, u32[]{:S(2)}, u32[]{:S(2)}) collective-permute-start(bf16[4,4,16,512]{3,2,1,0:T(8,128)(2,1)} %bitcast.36), channel_id=1, source_target_pairs={{0,8},{8,16},{16,24},{24,0},{1,9},{9,17},{17,25},{25,1},{2,10},{10... | collective-permute-start | bytes 786440 | tf_op jit(solution)/shard_map/ppermute | solution.py:171
  51.9 14.1 %collective-permute-start.1 = (bf16[4,4,16,512]{3,2,1,0:T(8,128)(2,1)}, bf16[4,4,16,512]{3,2,1,0:T(8,128)(2,1)}, u32[]{:S(2)}, u32[]{:S(2)}) collective-permute-start(bf16[4,4,16,512]{3,2,1,0:T(8,128)(2,1)} %bitcast.36), channel_id=1, source_target_pairs={{0,16},{8,24},{16,0},{24,8},{1,17},{9,25},{17,1},{25,9},{2,18},{10... | collective-permute-start | bytes 786440 | tf_op jit(solution)/shard_map/ppermute | solution.py:171
  56.3 11.5 %collective-permute-start.2 = (bf16[4,4,16,512]{3,2,1,0:T(8,128)(2,1)}, bf16[4,4,16,512]{3,2,1,0:T(8,128)(2,1)}, u32[]{:S(2)}, u32[]{:S(2)}) collective-permute-start(bf16[4,4,16,512]{3,2,1,0:T(8,128)(2,1)} %bitcast.36), channel_id=1, source_target_pairs={{0,24},{8,0},{16,8},{24,16},{1,25},{9,1},{17,9},{25,17},{2,26},{10... | collective-permute-start | bytes 786440 | tf_op jit(solution)/shard_map/ppermute | solution.py:171
  59.5 1.0 copy-start.11
  60.5 1.7 %copy-start.3 = (bf16[1152,1024]{1,0:T(8,128)(2,1)S(1)}, bf16[1152,1024]{1,0:T(8,128)(2,1)}, u32[]{:S(2)}) copy-start(bf16[1152,1024]{1,0:T(8,128)(2,1)} %all-gather.3.cloned.1.call-done) | copy-start | bytes 7077892
  69.5 14.4 %copy-start.7 = (s32[1024,2]{0,1:T(2,128)S(1)}, s32[1024,2]{0,1:T(2,128)}, u32[]{:S(2)}) copy-start(s32[1024,2]{0,1:T(2,128)} %param.13) | copy-start | bytes 24580
  69.5 14.4 %copy-start.8 = (f32[1024,2]{0,1:T(2,128)S(1)}, f32[1024,2]{0,1:T(2,128)}, u32[]{:S(2)}) copy-start(f32[1024,2]{0,1:T(2,128)} %param.12) | copy-start | bytes 24580
  74.7 14.0 %all-to-all-start.2 = ((f32[8,8,128]{2,1,0:T(8,128)}), f32[8,8,128]{2,1,0:T(8,128)S(1)}, u32[]{:S(2)}, u32[]{:S(2)}) async-start(f32[8,8,128]{2,1,0:T(8,128)} %broadcast_in_dim.43), calls=%async_computation.3 | async-start | bytes 65536 | tf_op jit(solution)/shard_map/all_to_all | solution.py:164
  88.7 1.6 %copy-start.10 = (f32[1024,512]{1,0:T(8,128)S(1)}, f32[1024,512]{1,0:T(8,128)}, u32[]{:S(2)}) copy-start(f32[1024,512]{1,0:T(8,128)} %get-tuple-element.47.refs_4_) | copy-start | bytes 6291460
  98.3 1.5 copy-start.2
  99.8 38.0 %all-to-all-start.3 = ((bf16[8,320,512]{2,1,0:T(8,128)(2,1)}), bf16[8,320,512]{2,1,0:T(8,128)(2,1)}, u32[]{:S(2)}, u32[]{:S(2)}) async-start(bf16[8,320,512]{2,1,0:T(8,128)(2,1)} %copy-done.2), calls=%async_computation.4 | async-start | bytes 5242880 | tf_op jit(solution)/shard_map/all_to_all | solution.py:256
  111.9 1.0 copy-start.4
  113.0 9.0 %collective-permute-start.3 = (bf16[80,512]{1,0:T(8,128)(2,1)S(1)}, bf16[80,512]{1,0:T(8,128)(2,1)S(1)}, u32[]{:S(2)}, u32[]{:S(2)}) collective-permute-start(bf16[80,512]{1,0:T(8,128)(2,1)S(1)} %get-tuple-element.35), channel_id=1, source_target_pairs={{0,32},{32,64},{64,96},{96,0},{1,33},{33,65},{65,97},{97,1},{2,34}... | collective-permute-start | bytes 245768 | tf_op jit(solution)/shard_map/ppermute | solution.py:171
  115.2 9.3 %collective-permute-start.4 = (bf16[80,512]{1,0:T(8,128)(2,1)S(1)}, bf16[80,512]{1,0:T(8,128)(2,1)S(1)}, u32[]{:S(2)}, u32[]{:S(2)}) collective-permute-start(bf16[80,512]{1,0:T(8,128)(2,1)S(1)} %get-tuple-element.36), channel_id=1, source_target_pairs={{0,64},{32,96},{64,0},{96,32},{1,65},{33,97},{65,1},{97,33},{2,66}... | collective-permute-start | bytes 245768 | tf_op jit(solution)/shard_map/ppermute | solution.py:171
  119.0 6.6 %collective-permute-start.5 = (bf16[80,512]{1,0:T(8,128)(2,1)S(1)}, bf16[80,512]{1,0:T(8,128)(2,1)S(1)}, u32[]{:S(2)}, u32[]{:S(2)}) collective-permute-start(bf16[80,512]{1,0:T(8,128)(2,1)S(1)} %get-tuple-element.37), channel_id=1, source_target_pairs={{0,96},{32,0},{64,32},{96,64},{1,97},{33,1},{65,33},{97,65},{2,98}... | collective-permute-start | bytes 245768 | tf_op jit(solution)/shard_map/ppermute | solution.py:171
  126.3 15.2 %collective-permute-start.6 = (f32[24,512]{1,0:T(8,128)S(1)}, f32[24,512]{1,0:T(8,128)S(1)}, u32[]{:S(2)}, u32[]{:S(2)}) collective-permute-start(f32[24,512]{1,0:T(8,128)S(1)} %get-tuple-element.39), channel_id=1, source_target_pairs={{0,128},{128,256},{256,384},{384,0},{1,129},{129,257},{257,385},{3... | collective-permute-start | bytes 147464 | tf_op jit(solution)/shard_map/ppermute | solution.py:171
  128.3 13.5 %collective-permute-start.7 = (f32[24,512]{1,0:T(8,128)S(1)}, f32[24,512]{1,0:T(8,128)S(1)}, u32[]{:S(2)}, u32[]{:S(2)}) collective-permute-start(f32[24,512]{1,0:T(8,128)S(1)} %get-tuple-element.40), channel_id=1, source_target_pairs={{0,256},{128,384},{256,0},{384,128},{1,257},{129,385},{257,1},{385... | collective-permute-start | bytes 147464 | tf_op jit(solution)/shard_map/ppermute | solution.py:171
  135.4 15.0 %collective-permute-start.8 = (f32[24,512]{1,0:T(8,128)S(1)}, f32[24,512]{1,0:T(8,128)S(1)}, u32[]{:S(2)}, u32[]{:S(2)}) collective-permute-start(f32[24,512]{1,0:T(8,128)S(1)} %get-tuple-element.41), channel_id=1, source_target_pairs={{0,384},{128,0},{256,128},{384,256},{1,385},{129,1},{257,129},{385... | collective-permute-start | bytes 147464 | tf_op jit(solution)/shard_map/ppermute | solution.py:171
  (1 other events, 0.7 us)
Sparse Core Ops, SparseCore 0:
  11.4 39.0 all-gather.2
  65.4 31.7 reduce-scatter.1

commit v4 on v3

--- a/solution.py
+++ b/solution.py
@@ -7,18 +7,33 @@
 
 epsilon = 1e-05
 EXPERT = ("y", "core")
-VMEM = pl.BlockSpec(memory_space=pltpu.VMEM)
 SMEM = pl.BlockSpec(memory_space=pltpu.SMEM)
+BASE_FLOPS = 4 * 10**9
+SLOTS_FLOPS = 50 * 10**9
 PAD = 16
 
 
-def call(kernel, *operands, out, limit=32):
+def whole(shape):
+    return pl.BlockSpec(shape, lambda *at: (0,) * len(shape))
+
+
+def call(kernel, *operands, out, limit=60, scratch=(), grid=(1,), out_specs=None, flops=None):
+    cost = {}
+    if flops:
+        cost["cost_estimate"] = pl.CostEstimate(
+            flops=flops, bytes_accessed=10**7, transcendentals=0
+        )
     return pl.pallas_call(
         kernel,
-        in_specs=[SMEM if o.shape == (1,) else VMEM for o in operands],
-        out_specs=[VMEM] * len(out),
+        grid=grid,
+        in_specs=[SMEM if o.dtype == jnp.int32 and o.ndim == 1 else whole(o.shape) for o in operands],
+        out_specs=out_specs or [whole(shape) for shape, _ in out],
         out_shape=[jax.ShapeDtypeStruct(shape, kind) for shape, kind in out],
-        compiler_params=pltpu.CompilerParams(vmem_limit_bytes=limit * 2**20),
+        scratch_shapes=[pltpu.VMEM(shape, kind) for shape, kind in scratch],
+        compiler_params=pltpu.CompilerParams(
+            dimension_semantics=("arbitrary",) * len(grid), vmem_limit_bytes=limit * 2**20
+        ),
+        **cost,
     )(*operands)
 
 
@@ -67,7 +82,7 @@
     gate_ref[...] = jnp.where(first, gate_first, jnp.where(second, gate_second, 0.0))
 
 
-def value_kernel(width, gathered_ref, input_ref, gain_ref, d_value_ref, value_ref, inverse_ref):
+def value_kernel(width, gathered_ref, input_ref, gain_ref, d_value_ref, inverse_ref):
     devices, packed, features = gathered_ref.shape
     rows = packed - PAD
     group = input_ref.shape[0]
@@ -75,7 +90,6 @@
     for device in range(devices):
         part = gathered_ref[device, rows:, :].astype(jnp.float32)
         squares += jnp.sum(part, axis=0, keepdims=True)
-        value_ref[device * rows : (device + 1) * rows, :] = gathered_ref[device, 0:rows, :]
     inverse = 1.0 / jnp.sqrt(squares / width + epsilon)
     tile = group // 8
     for at in range(8):
@@ -86,7 +100,7 @@
     block = features // zh
     for high in range(zh):
         partial = lax.dot_general(
-            value_ref[:, high * block : (high + 1) * block],
+            gathered_ref[:, 0:rows, high * block : (high + 1) * block].reshape(group, block),
             normed,
             (((0,), (0,)), ((), ())),
             preferred_element_type=jnp.float32,
@@ -97,34 +111,82 @@
                 d_value_ref[x, low, high] = partial[start : start + own, :]
 
 
-def dispatch_kernel(
-    width, inverse_ref, inner_ref, slot_ref, gate_ref, base_ref, input_ref, out_ref, stream_ref
+def selected(slot_ref, rows_ref, out_ref):
+    slot = slot_ref[pl.ds(pl.program_id(0), 1), :]
+    taken = lax.broadcasted_iota(jnp.int32, (out_ref.shape[1], slot.shape[1]), 0) == slot
+    picked = jnp.dot(
+        jnp.where(taken, 1.0, 0.0).astype(jnp.bfloat16),
+        rows_ref[...],
+        preferred_element_type=jnp.float32,
+    )
+    out_ref[0] = picked.astype(jnp.bfloat16)
+
+
+def base_kernel(
+    me_ref, gathered_ref, input_ref, grad_ref, gain_ref, inverse_ref, slot_ref, *refs
 ):
-    expert = pl.program_id(0)
-    group = input_ref.shape[0]
-    capacity = out_ref.shape[1]
-
-    @pl.when(expert == 0)
+    parts, (out_ref, inner_ref, d_gain_ref, weight_ref, base_ref) = refs[:-5], refs[-5:]
+    devices, packed, _ = gathered_ref.shape
+    rows = packed - PAD
+
+    @pl.when(pl.program_id(0) == 0)
     def _():
-        inverse = inverse_ref[...]
-        inner = jnp.sum(inner_ref[...], axis=0) / width
-        factor = jnp.transpose(inner * inverse * inverse)
-        tile = group // 8
-        for at in range(8):
-            rows = pl.ds(at * tile, tile)
-            stream_ref[rows, :] = (
-                base_ref[rows, :]
-                - input_ref[rows, :].astype(jnp.float32) * factor[:, at : at + 1]
+        xs = len(parts)
+        zl, zh, own, _ = parts[0].shape
+        for x_step, part in enumerate(parts):
+            x = lax.rem(me_ref[0] + (xs - x_step), xs)
+            for low_step in range(zl):
+                low = lax.rem(me_ref[1] + (zl - low_step), zl)
+                for high in range(zh):
+                    start = pl.multiple_of(((high * zl + low) * xs + x) * own, own)
+                    weight_ref[pl.ds(start, own), :] = part[low_step, high]
+        factor = jnp.transpose(inverse_ref[...])
+        d_gain = jnp.zeros(d_gain_ref.shape, jnp.float32)
+        for at in range(0, devices, 2):
+            d_normed = jnp.dot(
+                gathered_ref[at : at + 2, 0:rows, :].reshape(2 * rows, -1),
+                weight_ref[...],
+                preferred_element_type=jnp.float32,
             )
-
-    slot = slot_ref[pl.ds(expert, 1), :]
-    gate = column(gate_ref[pl.ds(expert, 1), :])
-    rows = (gate * stream_ref[...]).astype(jnp.bfloat16)
-    taken = lax.broadcasted_iota(jnp.int32, (capacity, group), 0) == slot
-    picked = jnp.dot(
-        jnp.where(taken, 1.0, 0.0).astype(jnp.bfloat16), rows, preferred_element_type=jnp.float32
-    )
-    out_ref[0] = picked.astype(jnp.bfloat16)
+            for half in range(2):
+                tokens = slice((at + half) * rows, (at + half + 1) * rows)
+                normed = d_normed[half * rows : (half + 1) * rows, :]
+                inverse = factor[:, at + half : at + half + 1]
+                scaled = input_ref[tokens, :].astype(jnp.float32) * inverse
+                weighted = normed * gain_ref[...]
+                d_gain += jnp.sum(normed * scaled, axis=0, keepdims=True)
+                inner = jnp.sum(weighted * scaled, axis=1, keepdims=True)
+                inner = jnp.transpose(jnp.broadcast_to(inner, (rows, 8)))[0:1, :]
+                inner_ref[at + half : at + half + 1, :] = inner
+                base = grad_ref[tokens, :].astype(jnp.float32) + weighted * inverse
+                base_ref[tokens, :] = base.astype(jnp.bfloat16)
+        d_gain_ref[...] = d_gain
+
+    selected(slot_ref, base_ref, out_ref)
+
+
+def slots_kernel(width, me_ref, slot_ref, gate_ref, inverse_ref, inner_ref, gate_out, factor_out):
+    capacity = gate_out.shape[0]
+    tile = inverse_ref.shape[1]
+    factor = inner_ref[...] / width * inverse_ref[...] * inverse_ref[...]
+    slot = slot_ref[pl.ds(me_ref[0], 1), :]
+    gate = gate_ref[pl.ds(me_ref[0], 1), :]
+    gates = jnp.zeros((capacity, 1), jnp.float32)
+    factors = jnp.zeros((capacity, 1), jnp.float32)
+    for at in range(inverse_ref.shape[0]):
+        tokens = slice(at * tile, (at + 1) * tile)
+        taken = lax.broadcasted_iota(jnp.int32, (capacity, tile), 0) == slot[:, tokens]
+        gates += jnp.sum(jnp.where(taken, gate[:, tokens], 0.0), axis=1, keepdims=True)
+        factors += jnp.sum(jnp.where(taken, factor[at : at + 1, :], 0.0), axis=1, keepdims=True)
+    gate_out[...] = jnp.broadcast_to(gates, gate_out.shape)
+    factor_out[...] = jnp.broadcast_to(factors, factor_out.shape)
+
+
+def combine_kernel(gate_ref, factor_ref, base_ref, input_ref, out_ref):
+    base = base_ref[0].astype(jnp.float32)
+    inputs = input_ref[0].astype(jnp.float32)
+    stream = base - inputs * factor_ref[:, 0:1]
+    out_ref[...] = (gate_ref[:, 0:1] * stream).astype(jnp.bfloat16)
 
 
 def low_split_kernel(me_ref, d_value_ref, d_gain_ref, *outs):
@@ -159,13 +221,6 @@
     d_gain_ref[...] = total[rows : rows + 1, :] * rescale
 
 
-def to_all(part, axis):
-    size = lax.axis_size(axis)
-    return lax.all_to_all(
-        jnp.broadcast_to(part[None], (size,) + part.shape), axis, 0, 0, tiled=True
-    )
-
-
 def further(part, axis, step):
     size = lax.axis_size(axis)
     return lax.ppermute(part, axis, [(i, (i + step) % size) for i in range(size)])
@@ -184,81 +239,72 @@
     own_rows = value_grad.shape[0]
     f32, bf16 = jnp.float32, jnp.bfloat16
     gain_row = norm_gain[None]
-    me_x = lax.axis_index("x").astype(jnp.uint32)
 
     packed, copies = call(
         pack_kernel, value_grad, attn_input, value_weight,
         out=[((own_rows + PAD, features), bf16), ((zh, rows, columns), bf16)],
     )
     gathered = lax.all_gather(packed, EXPERT, axis=0)
-
-    weight = to_all(lax.all_to_all(copies, "zh", 0, 0, tiled=True), "zl")
-    weight = jnp.transpose(weight, (1, 0, 2, 3))
-    others = [further(weight, "x", step) for step in range(1, xs)]
-    gathered, others[0] = lax.optimization_barrier((gathered, others[0]))
-    every_weight = jnp.zeros((zh, zl, xs, rows, columns), bf16)
-    for step, part in enumerate([weight] + others):
-        place = lax.rem(me_x + jnp.uint32(xs - step), jnp.uint32(xs))
-        zero = jnp.uint32(0)
-        every_weight = lax.dynamic_update_slice(
-            every_weight, part[:, :, None], (zero, zero, place, zero, zero)
-        )
-    every_weight = every_weight.reshape(features, columns)
-
     slot, gate = call(
         route_kernel, routes.T, gate_logits.T,
         out=[((experts, group), jnp.int32), ((experts, group), f32)],
     )
-
-    d_value, every_value, inverse = call(
+    by_slot = ((experts, capacity, columns), bf16)
+    one_slot_block = pl.BlockSpec((1, capacity, columns), lambda e: (e, 0, 0))
+    (input_rows,) = call(
+        selected, slot, attn_input, out=[by_slot], out_specs=[one_slot_block], grid=(experts,)
+    )
+
+    weight = lax.all_to_all(copies, "zh", 0, 0, tiled=True)
+    weight, input_rows = lax.optimization_barrier((weight, input_rows))
+    input_rows = lax.all_to_all(input_rows, EXPERT, 0, 0, tiled=True)
+    weight = jnp.stack([weight] + [further(weight, "zl", step) for step in range(1, zl)])
+    weights = [weight] + [further(weight, "x", step) for step in range(1, xs)]
+    gathered, weights[1] = lax.optimization_barrier((gathered, weights[1]))
+
+    d_value, inverse = call(
         lambda *refs: value_kernel(width, *refs), gathered, attn_input, gain_row,
-        out=[
-            ((xs, zl, zh, rows, columns), f32),
-            ((group, features), bf16),
-            ((8, group // 8), f32),
-        ],
-        limit=40,
+        out=[((xs, zl, zh, rows, columns), f32), ((8, group // 8), f32)],
     )
     d_value = lax.psum_scatter(
         d_value.reshape(features, columns), "x", scatter_dimension=0, tiled=True
     )
 
-    inverse_column = inverse.reshape(group)[:, None]
-    scaled = attn_input.astype(f32) * inverse_column
-    d_normed = jnp.dot(every_value, every_weight, preferred_element_type=f32)
-    weighted = d_normed * norm_gain
-    own_inner = jnp.sum(weighted * scaled, axis=1)
-    own_gain = jnp.sum(d_normed * scaled, axis=0)
-    base = stream_grad.astype(f32) + weighted * inverse_column
-    inner = to_all(own_inner.reshape(8, group // 8), EXPERT)
-
-    whole = lambda *shape: pl.BlockSpec(shape, lambda e: (0,) * len(shape))
-    sent = pl.pallas_call(
-        lambda *refs: dispatch_kernel(width, *refs),
+    sent, inner, own_gain = call(
+        base_kernel, jnp.stack([lax.axis_index("x"), lax.axis_index("zl")]),
+        gathered, attn_input, stream_grad, gain_row, inverse, slot, *weights,
+        out=[by_slot, ((8, group // 8), f32), ((1, columns), f32)],
+        out_specs=[one_slot_block, whole((8, group // 8)), whole((1, columns))],
+        scratch=[((features, columns), bf16), ((group, columns), bf16)],
         grid=(experts,),
-        in_specs=[
-            whole(8, group // 8),
-            whole(experts, 8, group // 8),
-            whole(experts, group),
-            whole(experts, group),
-            whole(group, columns),
-            whole(group, columns),
-        ],
-        out_specs=pl.BlockSpec((1, capacity, columns), lambda e: (e, 0, 0)),
-        out_shape=jax.ShapeDtypeStruct((experts, capacity, columns), bf16),
-        scratch_shapes=[pltpu.VMEM((group, columns), f32)],
+        flops=BASE_FLOPS,
+    )
+    sent, inner, own_gain = lax.optimization_barrier((sent, inner, own_gain))
+    arrived = lax.all_to_all(sent, EXPERT, 0, 0, tiled=True)
+
+    d_gain = lax.psum(own_gain, "x")
+    inner = lax.psum(inner, EXPERT)
+    lanes = ((capacity, 128), f32)
+    slot_gate, slot_factor = call(
+        lambda *refs: slots_kernel(width, *refs), lax.axis_index(EXPERT).reshape(1),
+        slot, gate, inverse, inner, out=[lanes, lanes], flops=SLOTS_FLOPS,
+    )
+    block = pl.BlockSpec((1, capacity, columns), lambda d: (d, 0, 0))
+    dispatched = pl.pallas_call(
+        combine_kernel,
+        grid=(experts,),
+        in_specs=[whole(lanes[0]), whole(lanes[0]), block, block],
+        out_specs=pl.BlockSpec((capacity, columns), lambda d: (0, d)),
+        out_shape=jax.ShapeDtypeStruct((capacity, width), bf16),
         compiler_params=pltpu.CompilerParams(
             dimension_semantics=("arbitrary",), vmem_limit_bytes=40 * 2**20
         ),
-        cost_estimate=pl.CostEstimate(flops=15 * 10**9, bytes_accessed=10**7, transcendentals=0),
-    )(inverse, inner, slot, gate, base, attn_input)
-    sent, own_gain = lax.optimization_barrier((sent, own_gain))
-    arrived = lax.all_to_all(sent, EXPERT, split_axis=0, concat_axis=2, tiled=True)
-
-    d_gain = lax.psum(own_gain, "x")
+    )(slot_gate, slot_factor, arrived, input_rows)
+
+    d_gain, _ = lax.optimization_barrier((d_gain, slot_gate))
     part = (features // xs // zl + PAD, columns)
     parts = call(
-        low_split_kernel, lax.axis_index("zl").reshape(1), d_value, d_gain[None],
+        low_split_kernel, lax.axis_index("zl").reshape(1), d_value, d_gain,
         out=[(part, bf16)] * zl,
     )
     parts = [parts[0]] + [further(parts[k], "zl", k) for k in range(1, zl)]
@@ -272,7 +318,7 @@
         lambda *refs: finish_kernel(rescale, *refs), *parts,
         out=[((rows, columns), bf16), ((1, columns), f32)],
     )
-    return (d_value, d_gain.reshape(columns), arrived)
+    return (d_value, d_gain.reshape(columns), dispatched[None])
 
 
 def solution(mesh):

time: 159 us -> 171 us (1.075); the launches traced: 158 us -> 168 us
  starting transfers between devices: 45.4 us -> 73.1 us
  Pallas kernels: 14 us -> 39.8 us
  blocking collectives: 43.8 us -> 24.5 us
  local copies, waits for them, and re-layouts: 18.9 us -> 3.09 us
  matrix products: 4.55 us -> 0 us
  waiting for transfers between devices: 16.9 us -> 12.4 us
    all_to_all x2 -> x0, blocking collectives: 36.8 us -> none  [the longest x1 27.9 us: on_device(): weight = to_all(lax.all_to_all(copies, 'zh', 0, 0, tiled=True), 'zl')]
    pallas_call x7 -> x10, Pallas kernels: 14 us -> 39.8 us  [the longest x9 33.3 us: call(): pl.pallas_call(kernel, grid=grid, in_specs=[SMEM if o.dtype == jnp.int32...]
    psum x0 -> x1, blocking collectives: none -> 15 us  [on_device(): inner = lax.psum(inner, EXPERT)]
    ppermute x9 -> x12, starting transfers between devices: 31.1 us -> 45.3 us  [further(): lax.ppermute(part, axis, [(i, (i + step) % size) for i in range(size)])]
    all_to_all x2 -> x3, starting transfers between devices: 14.3 us -> 27.7 us  [the longest x1 15.6 us: on_device(): weight = lax.all_to_all(copies, 'zh', 0, 0, tiled=True)]
    unnamed x24, local copies, waits for them, and re-layouts: 9.66 us -> 3.09 us
    dot_general x1 -> x0, matrix products: 4.55 us -> none  [on_device(): d_normed = jnp.dot(every_value, every_weight, preferred_element_type=f32)]
    all_to_all x2 -> x0, local copies, waits for them, and re-layouts: 4.3 us -> none  [the longest x1 3.6 us: on_device(): lax.all_to_all(sent, EXPERT, split_axis=0, concat_axis=2, tiled=True)]
  transfers between devices with their start and end apart: 13 -> 17, of which waited for: 5 -> 5; matrix products, arithmetic and copies ran while one was open for 9% -> 0% of each run, Pallas kernels for 8% -> 21%
where the time goes in v4:
time: 171 us; the launch traced here: 168 us
  starting transfers between devices  73.1 us (43%)
  Pallas kernels  39.8 us (23%)
  blocking collectives  24.5 us (14%)
  between operations  14.3 us (8%)
  waiting for transfers between devices  12.4 us (7%)
  local copies, waits for them, and re-layouts  3.09 us (2%)
    ppermute x12, starting transfers between devices, further(): lax.ppermute(part, axis, [(i, (i + step) % size) for i in range(size)])  45.3 us
    pallas_call x9, Pallas kernels, call(): pl.pallas_call(kernel, grid=grid, in_specs=[SMEM if o.dtype == jnp.int32...  33.3 us
    all_to_all x1, starting transfers between devices, on_device(): weight = lax.all_to_all(copies, 'zh', 0, 0, tiled=True)  15.6 us
    psum x1, blocking collectives, on_device(): inner = lax.psum(inner, EXPERT)  15 us
    psum x1, blocking collectives, on_device(): d_gain = lax.psum(own_gain, 'x')  9.56 us
    ppermute x12, waiting for transfers between devices, further(): lax.ppermute(part, axis, [(i, (i + step) % size) for i in range(size)])  8.24 us
    pallas_call x1, Pallas kernels, on_device(): pl.pallas_call(combine_kernel, grid=(experts,), in_specs=[whole(lanes[0])...  6.47 us
    all_to_all x1, starting transfers between devices, on_device(): input_rows = lax.all_to_all(input_rows, EXPERT, 0, 0, tiled=True)  6.06 us
  transfers between devices with their start and end apart: 17, of which 5 were waited for; matrix products, arithmetic and copies ran while one was open for 0% of the time, Pallas kernels for 21%

profile of v4, /device:TPU:1, one launch (start us, length us, event | category | flops | bytes accessed | tf_op | source)
XLA Modules:
  0.0 167.9 jit_solution(15415437115745959087)
XLA Ops:
  7.2 2.4 %shard_map.94 = (bf16[144,1024]{1,0:T(8,128)(2,1)}, bf16[4,16,512]{2,1,0:T(8,128)(2,1)}) custom-call(bf16[128,1024]{1,0:T(8,128)(2,1)} %value_ref.1, bf16[1024,512]{1,0:T(8,128)(2,1)} %input_ref.3, bf16[16,512]{1,0:T(8,128)(2,1)} %weight_ref.1), custom_call_target="tpu_custom_call" | custom-call | tf_op jit(solution)/shard_map/pallas_call | solution.py:26
  9.6 15.6 %all-to-all-start = ((bf16[4,16,512]{2,1,0:T(8,128)(2,1)}), bf16[4,16,512]{2,1,0:T(8,128)(2,1)S(1)}, u32[]{:S(2)}, u32[]{:S(2)}) async-start(bf16[4,16,512]{2,1,0:T(8,128)(2,1)} %get-tuple-element.30), calls=%async_computation | async-start | bytes 131072 | tf_op jit(solution)/shard_map/all_to_all | solution.py:258
  26.9 6.7 %shard_map.96 = bf16[8,320,512]{2,1,0:T(8,128)(2,1)} custom-call(s32[8,1024]{1,0:T(8,128)} %get-tuple-element.31.slot_ref.refs_1_, bf16[1024,512]{1,0:T(8,128)(2,1)} %input_ref.3), custom_call_target="tpu_custom_call" | custom-call | tf_op jit(solution)/shard_map/pallas_call | solution.py:26
  33.6 4.1 %all-to-all-done = bf16[4,16,512]{2,1,0:T(8,128)(2,1)S(1)} async-done(((bf16[4,16,512]{2,1,0:T(8,128)(2,1)}), bf16[4,16,512]{2,1,0:T(8,128)(2,1)S(1)}, u32[]{:S(2)}, u32[]{:S(2)}) %all-to-all-start) | async-done | bytes 65568 | tf_op jit(solution)/shard_map/all_to_all | solution.py:258
  37.8 6.1 %all-to-all-start.2 = ((bf16[8,320,512]{2,1,0:T(8,128)(2,1)}), bf16[8,320,512]{2,1,0:T(8,128)(2,1)S(1)}, u32[]{:S(2)}, u32[]{:S(2)}) async-start(bf16[8,320,512]{2,1,0:T(8,128)(2,1)} %shard_map.96), calls=%async_computation.3 | async-start | bytes 5242880 | tf_op jit(solution)/shard_map/all_to_all | solution.py:260
  43.8 3.5 %collective-permute-start.2 = (bf16[4,16,512]{2,1,0:T(8,128)(2,1)S(1)}, bf16[4,16,512]{2,1,0:T(8,128)(2,1)S(1)}, u32[]{:S(2)}, u32[]{:S(2)}) collective-permute-start(bf16[4,16,512]{2,1,0:T(8,128)(2,1)S(1)} %all-to-all-done), channel_id=1, source_target_pairs={{0,96},{32,0},{64,32},{96,64},{1,97},{33,1},{65,33},{97,65},{2,98}... | collective-permute-start | bytes 196616 | tf_op jit(solution)/shard_map/ppermute | solution.py:226
  47.4 3.1 %collective-permute-start.1 = (bf16[4,16,512]{2,1,0:T(8,128)(2,1)S(1)}, bf16[4,16,512]{2,1,0:T(8,128)(2,1)S(1)}, u32[]{:S(2)}, u32[]{:S(2)}) collective-permute-start(bf16[4,16,512]{2,1,0:T(8,128)(2,1)S(1)} %all-to-all-done), channel_id=1, source_target_pairs={{0,64},{32,96},{64,0},{96,32},{1,65},{33,97},{65,1},{97,33},{2,66}... | collective-permute-start | bytes 196616 | tf_op jit(solution)/shard_map/ppermute | solution.py:226
  50.5 2.6 %collective-permute-start = (bf16[4,16,512]{2,1,0:T(8,128)(2,1)S(1)}, bf16[4,16,512]{2,1,0:T(8,128)(2,1)S(1)}, u32[]{:S(2)}, u32[]{:S(2)}) collective-permute-start(bf16[4,16,512]{2,1,0:T(8,128)(2,1)S(1)} %all-to-all-done), channel_id=1, source_target_pairs={{0,32},{32,64},{64,96},{96,0},{1,33},{33,65},{65,97},{97,1},{2,34}... | collective-permute-start | bytes 196616 | tf_op jit(solution)/shard_map/ppermute | solution.py:226
  53.1 2.2 %collective-permute-done.1 = bf16[4,16,512]{2,1,0:T(8,128)(2,1)S(1)} collective-permute-done((bf16[4,16,512]{2,1,0:T(8,128)(2,1)S(1)}, bf16[4,16,512]{2,1,0:T(8,128)(2,1)S(1)}, u32[]{:S(2)}, u32[]{:S(2)}) %collective-permute-start.1) | collective-permute-done | bytes 65568 | tf_op jit(solution)/shard_map/ppermute | solution.py:226
  57.3 3.1 %collective-permute-start.3 = (bf16[4,4,16,512]{3,2,1,0:T(8,128)(2,1)S(1)}, bf16[4,4,16,512]{3,2,1,0:T(8,128)(2,1)S(1)}, u32[]{:S(2)}, u32[]{:S(2)}) collective-permute-start(bf16[4,4,16,512]{3,2,1,0:T(8,128)(2,1)S(1)} %pad_maximum_fusion.refs_0_), channel_id=1, source_target_pairs={{0,8},{8,16},{16,24},{24,0},{1,9},{9,17},{17,25},{25,1},{2,10},{10... | collective-permute-start | bytes 786440 | tf_op jit(solution)/shard_map/ppermute | solution.py:226
  60.5 4.4 %collective-permute-start.4 = (bf16[4,4,16,512]{3,2,1,0:T(8,128)(2,1)S(1)}, bf16[4,4,16,512]{3,2,1,0:T(8,128)(2,1)S(1)}, u32[]{:S(2)}, u32[]{:S(2)}) collective-permute-start(bf16[4,4,16,512]{3,2,1,0:T(8,128)(2,1)S(1)} %pad_maximum_fusion.refs_0_), channel_id=1, source_target_pairs={{0,16},{8,24},{16,0},{24,8},{1,17},{9,25},{17,1},{25,9},{2,18},{10... | collective-permute-start | bytes 786440 | tf_op jit(solution)/shard_map/ppermute | solution.py:226
  64.8 3.1 %collective-permute-start.5 = (bf16[4,4,16,512]{3,2,1,0:T(8,128)(2,1)S(1)}, bf16[4,4,16,512]{3,2,1,0:T(8,128)(2,1)}, u32[]{:S(2)}, u32[]{:S(2)}) collective-permute-start(bf16[4,4,16,512]{3,2,1,0:T(8,128)(2,1)S(1)} %pad_maximum_fusion.refs_0_), channel_id=1, source_target_pairs={{0,24},{8,0},{16,8},{24,16},{1,25},{9,1},{17,9},{25,17},{2,26},{10... | collective-permute-start | bytes 786440 | tf_op jit(solution)/shard_map/ppermute | solution.py:226
  68.6 5.2 %shard_map.97 = (f32[4,4,4,16,512]{4,3,2,1,0:T(8,128)}, f32[8,128]{1,0:T(8,128)}) custom-call(bf16[8,144,1024]{2,1,0:T(8,128)(2,1)} %bitcast.16, bf16[1024,512]{1,0:T(8,128)(2,1)} %input_ref.3, f32[1,512]{1,0:T(1,128)} %bitcast.25), custom_call_target="tpu_custom_call" | custom-call | tf_op jit(solution)/shard_map/pallas_call | solution.py:26
  75.2 10.1 %shard_map.98 = (bf16[8,320,512]{2,1,0:T(8,128)(2,1)}, f32[8,128]{1,0:T(8,128)}, f32[1,512]{1,0:T(1,128)}) custom-call(s32[2]{0:T(128)} %pad_add_fusion.me_ref, bf16[8,144,1024]{2,1,0:T(8,128)(2,1)} %bitcast.17, bf16[1024,512]{1,0:T(8,128)(2,1)} %input_ref.3, bf16[1024,512]{1,0:T(8,128)(2,1)} %grad_ref.1, f32[1,512]{1,0:T(1,128)} %bitcast.26, ...), custom_call_target="tpu_custom_call" | custom-call | flops 4000000000 | bytes 10000000 | tf_op jit(solution)/shard_map/pallas_call | solution.py:26
  85.3 15.0 %psum.15.refs_4_ = f32[8,128]{1,0:T(8,128)} all-reduce(f32[8,128]{1,0:T(8,128)} %get-tuple-element.39), channel_id=1, replica_groups=mesh['zh'=4,'zl'=4,'x'=4,'y'=4,'core'=2] {'y','core'}, use_global_device_ids=true, to_apply=%region_2.0 | all-reduce | flops 1024 | bytes 8192 | tf_op jit(solution)/shard_map/psum | solution.py:286
  100.3 6.0 %all-to-all-start.1 = ((bf16[8,320,512]{2,1,0:T(8,128)(2,1)}), bf16[8,320,512]{2,1,0:T(8,128)(2,1)}, u32[]{:S(2)}, u32[]{:S(2)}) async-start(bf16[8,320,512]{2,1,0:T(8,128)(2,1)} %get-tuple-element.53), calls=%async_computation.2 | async-start | bytes 5242880 | tf_op jit(solution)/shard_map/all_to_all | solution.py:283
  106.3 2.2 %shard_map.99 = (f32[320,128]{1,0:T(8,128)}, f32[320,128]{1,0:T(8,128)}) custom-call(s32[1]{0:T(128)} %bitcast.12.refs_0_, s32[8,1024]{1,0:T(8,128)} %get-tuple-element.31.slot_ref.refs_1_, f32[8,1024]{1,0:T(8,128)} %get-tuple-element.38.refs_2_, f32[8,128]{1,0:T(8,128)} %get-tuple-element.35.inverse_ref.refs_3_, f32[8,128]{1,0:T(8,128)} %psum.15.refs_4_), custom_call_target="tpu_custom_call" | custom-call | flops 49999998976 | bytes 10000000 | tf_op jit(solution)/shard_map/pallas_call | solution.py:26
  108.5 9.6 %psum.14.d_gain_ref = f32[1,512]{1,0:T(1,128)} all-reduce(f32[1,512]{1,0:T(1,128)S(1)} %copy-done.9), channel_id=1, replica_groups=mesh['zh'=4,'zl'=4,'x'=4,'y'=4,'core'=2] {'x'}, use_global_device_ids=true, to_apply=%region_1.0 | all-reduce | flops 512 | bytes 4096 | tf_op jit(solution)/shard_map/psum | solution.py:285
  123.9 5.1 %collective-permute-start.8 = (bf16[80,512]{1,0:T(8,128)(2,1)}, bf16[80,512]{1,0:T(8,128)(2,1)S(1)}, u32[]{:S(2)}, u32[]{:S(2)}) collective-permute-start(bf16[80,512]{1,0:T(8,128)(2,1)} %get-tuple-element.45), channel_id=1, source_target_pairs={{0,96},{32,0},{64,32},{96,64},{1,97},{33,1},{65,33},{97,65},{2,98}... | collective-permute-start | bytes 245768 | tf_op jit(solution)/shard_map/ppermute | solution.py:226
  129.0 2.7 %collective-permute-done.8.d_ref = bf16[80,512]{1,0:T(8,128)(2,1)S(1)} collective-permute-done((bf16[80,512]{1,0:T(8,128)(2,1)}, bf16[80,512]{1,0:T(8,128)(2,1)S(1)}, u32[]{:S(2)}, u32[]{:S(2)}) %collective-permute-start.8) | collective-permute-done | bytes 81952 | tf_op jit(solution)/shard_map/ppermute | solution.py:226
  134.1 2.6 %collective-permute-start.9 = (f32[24,512]{1,0:T(8,128)}, f32[24,512]{1,0:T(8,128)S(1)}, u32[]{:S(2)}, u32[]{:S(2)}) collective-permute-start(f32[24,512]{1,0:T(8,128)} %get-tuple-element.47), channel_id=1, source_target_pairs={{0,128},{128,256},{256,384},{384,0},{1,129},{129,257},{257,385},{3... | collective-permute-start | bytes 147464 | tf_op jit(solution)/shard_map/ppermute | solution.py:226
  136.7 6.9 %collective-permute-start.10 = (f32[24,512]{1,0:T(8,128)}, f32[24,512]{1,0:T(8,128)S(1)}, u32[]{:S(2)}, u32[]{:S(2)}) collective-permute-start(f32[24,512]{1,0:T(8,128)} %get-tuple-element.48), channel_id=1, source_target_pairs={{0,256},{128,384},{256,0},{384,128},{1,257},{129,385},{257,1},{385... | collective-permute-start | bytes 147464 | tf_op jit(solution)/shard_map/ppermute | solution.py:226
  143.6 7.0 %collective-permute-start.11 = (f32[24,512]{1,0:T(8,128)}, f32[24,512]{1,0:T(8,128)S(1)}, u32[]{:S(2)}, u32[]{:S(2)}) collective-permute-start(f32[24,512]{1,0:T(8,128)} %get-tuple-element.49), channel_id=1, source_target_pairs={{0,384},{128,0},{256,128},{384,256},{1,385},{129,1},{257,129},{385... | collective-permute-start | bytes 147464 | tf_op jit(solution)/shard_map/ppermute | solution.py:226
  152.4 6.5 %shard_map.103 = bf16[320,4096]{1,0:T(8,128)(2,1)} custom-call(f32[320,128]{1,0:T(8,128)S(1)} %copy-done, f32[320,128]{1,0:T(8,128)S(1)} %copy-done.1, bf16[8,320,512]{2,1,0:T(8,128)(2,1)} %all-to-all-done.1.base_ref, bf16[8,320,512]{2,1,0:T(8,128)(2,1)S(1)} %all-to-all-done.2.input_ref), custom_call_target="tpu_custom_call" | custom-call | tf_op jit(solution)/shard_map/pallas_call | solution.py:293
  (50 shorter events, 17.9 us)
Async XLA Ops:
  7.2 61.4 %all-gather.3.cloned.1.call-start = ((), (), s32[]{:S(2)}) async-start(), calls=%async_computation.5 | async-start | bytes 2654208 | tf_op jit(solution)/shard_map/all_gather | solution.py:247
  9.6 28.1 %all-to-all-start = ((bf16[4,16,512]{2,1,0:T(8,128)(2,1)}), bf16[4,16,512]{2,1,0:T(8,128)(2,1)S(1)}, u32[]{:S(2)}, u32[]{:S(2)}) async-start(bf16[4,16,512]{2,1,0:T(8,128)(2,1)} %get-tuple-element.30), calls=%async_computation | async-start | bytes 131072 | tf_op jit(solution)/shard_map/all_to_all | solution.py:258
  37.8 62.5 %all-to-all-start.2 = ((bf16[8,320,512]{2,1,0:T(8,128)(2,1)}), bf16[8,320,512]{2,1,0:T(8,128)(2,1)S(1)}, u32[]{:S(2)}, u32[]{:S(2)}) async-start(bf16[8,320,512]{2,1,0:T(8,128)(2,1)} %shard_map.96), calls=%async_computation.3 | async-start | bytes 5242880 | tf_op jit(solution)/shard_map/all_to_all | solution.py:260
  43.8 74.3 %reduce-scatter.2.cloned.1.call-start = ((), (), s32[]{:S(2)}) async-start(), calls=%async_computation.4 | async-start | bytes 2621440 | tf_op jit(solution)/shard_map/reduce_scatter | solution.py:269
  43.8 9.3 %collective-permute-start.2 = (bf16[4,16,512]{2,1,0:T(8,128)(2,1)S(1)}, bf16[4,16,512]{2,1,0:T(8,128)(2,1)S(1)}, u32[]{:S(2)}, u32[]{:S(2)}) collective-permute-start(bf16[4,16,512]{2,1,0:T(8,128)(2,1)S(1)} %all-to-all-done), channel_id=1, source_target_pairs={{0,96},{32,0},{64,32},{96,64},{1,97},{33,1},{65,33},{97,65},{2,98}... | collective-permute-start | bytes 196616 | tf_op jit(solution)/shard_map/ppermute | solution.py:226
  47.4 8.0 %collective-permute-start.1 = (bf16[4,16,512]{2,1,0:T(8,128)(2,1)S(1)}, bf16[4,16,512]{2,1,0:T(8,128)(2,1)S(1)}, u32[]{:S(2)}, u32[]{:S(2)}) collective-permute-start(bf16[4,16,512]{2,1,0:T(8,128)(2,1)S(1)} %all-to-all-done), channel_id=1, source_target_pairs={{0,64},{32,96},{64,0},{96,32},{1,65},{33,97},{65,1},{97,33},{2,66}... | collective-permute-start | bytes 196616 | tf_op jit(solution)/shard_map/ppermute | solution.py:226
  50.5 6.8 %collective-permute-start = (bf16[4,16,512]{2,1,0:T(8,128)(2,1)S(1)}, bf16[4,16,512]{2,1,0:T(8,128)(2,1)S(1)}, u32[]{:S(2)}, u32[]{:S(2)}) collective-permute-start(bf16[4,16,512]{2,1,0:T(8,128)(2,1)S(1)} %all-to-all-done), channel_id=1, source_target_pairs={{0,32},{32,64},{64,96},{96,0},{1,33},{33,65},{65,97},{97,1},{2,34}... | collective-permute-start | bytes 196616 | tf_op jit(solution)/shard_map/ppermute | solution.py:226
  57.3 16.4 %copy-start.2 = (bf16[4,4,16,512]{3,2,1,0:T(8,128)(2,1)}, bf16[4,4,16,512]{3,2,1,0:T(8,128)(2,1)S(1)}, u32[]{:S(2)}) copy-start(bf16[4,4,16,512]{3,2,1,0:T(8,128)(2,1)S(1)} %pad_maximum_fusion.refs_0_) | copy-start | bytes 786436
  57.3 11.2 %collective-permute-start.3 = (bf16[4,4,16,512]{3,2,1,0:T(8,128)(2,1)S(1)}, bf16[4,4,16,512]{3,2,1,0:T(8,128)(2,1)S(1)}, u32[]{:S(2)}, u32[]{:S(2)}) collective-permute-start(bf16[4,4,16,512]{3,2,1,0:T(8,128)(2,1)S(1)} %pad_maximum_fusion.refs_0_), channel_id=1, source_target_pairs={{0,8},{8,16},{16,24},{24,0},{1,9},{9,17},{17,25},{25,1},{2,10},{10... | collective-permute-start | bytes 786440 | tf_op jit(solution)/shard_map/ppermute | solution.py:226
  60.5 13.3 %collective-permute-start.4 = (bf16[4,4,16,512]{3,2,1,0:T(8,128)(2,1)S(1)}, bf16[4,4,16,512]{3,2,1,0:T(8,128)(2,1)S(1)}, u32[]{:S(2)}, u32[]{:S(2)}) collective-permute-start(bf16[4,4,16,512]{3,2,1,0:T(8,128)(2,1)S(1)} %pad_maximum_fusion.refs_0_), channel_id=1, source_target_pairs={{0,16},{8,24},{16,0},{24,8},{1,17},{9,25},{17,1},{25,9},{2,18},{10... | collective-permute-start | bytes 786440 | tf_op jit(solution)/shard_map/ppermute | solution.py:226
  64.8 10.4 %collective-permute-start.5 = (bf16[4,4,16,512]{3,2,1,0:T(8,128)(2,1)S(1)}, bf16[4,4,16,512]{3,2,1,0:T(8,128)(2,1)}, u32[]{:S(2)}, u32[]{:S(2)}) collective-permute-start(bf16[4,4,16,512]{3,2,1,0:T(8,128)(2,1)S(1)} %pad_maximum_fusion.refs_0_), channel_id=1, source_target_pairs={{0,24},{8,0},{16,8},{24,16},{1,25},{9,1},{17,9},{25,17},{2,26},{10... | collective-permute-start | bytes 786440 | tf_op jit(solution)/shard_map/ppermute | solution.py:226
  68.6 5.2 %copy-start.10 = (bf16[4,4,16,512]{3,2,1,0:T(8,128)(2,1)}, bf16[4,4,16,512]{3,2,1,0:T(8,128)(2,1)S(1)}, u32[]{:S(2)}) copy-start(bf16[4,4,16,512]{3,2,1,0:T(8,128)(2,1)S(1)} %collective-permute-done.3.refs_1_) | copy-start | bytes 786436
  73.8 1.4 copy-start.11
  100.3 50.3 %all-to-all-start.1 = ((bf16[8,320,512]{2,1,0:T(8,128)(2,1)}), bf16[8,320,512]{2,1,0:T(8,128)(2,1)}, u32[]{:S(2)}, u32[]{:S(2)}) async-start(bf16[8,320,512]{2,1,0:T(8,128)(2,1)} %get-tuple-element.53), calls=%async_computation.2 | async-start | bytes 5242880 | tf_op jit(solution)/shard_map/all_to_all | solution.py:283
  106.3 2.2 %copy-start.9 = (f32[1,512]{1,0:T(1,128)S(1)}, f32[1,512]{1,0:T(1,128)}, u32[]{:S(2)}) copy-start(f32[1,512]{1,0:T(1,128)} %get-tuple-element.37) | copy-start | bytes 6148
  119.9 9.0 %collective-permute-start.6 = (bf16[80,512]{1,0:T(8,128)(2,1)}, bf16[80,512]{1,0:T(8,128)(2,1)S(1)}, u32[]{:S(2)}, u32[]{:S(2)}) collective-permute-start(bf16[80,512]{1,0:T(8,128)(2,1)} %get-tuple-element.43), channel_id=1, source_target_pairs={{0,32},{32,64},{64,96},{96,0},{1,33},{33,65},{65,97},{97,1},{2,34}... | collective-permute-start | bytes 245768 | tf_op jit(solution)/shard_map/ppermute | solution.py:226
  121.8 7.1 %collective-permute-start.7 = (bf16[80,512]{1,0:T(8,128)(2,1)}, bf16[80,512]{1,0:T(8,128)(2,1)S(1)}, u32[]{:S(2)}, u32[]{:S(2)}) collective-permute-start(bf16[80,512]{1,0:T(8,128)(2,1)} %get-tuple-element.44), channel_id=1, source_target_pairs={{0,64},{32,96},{64,0},{96,32},{1,65},{33,97},{65,1},{97,33},{2,66}... | collective-permute-start | bytes 245768 | tf_op jit(solution)/shard_map/ppermute | solution.py:226
  123.9 7.8 %collective-permute-start.8 = (bf16[80,512]{1,0:T(8,128)(2,1)}, bf16[80,512]{1,0:T(8,128)(2,1)S(1)}, u32[]{:S(2)}, u32[]{:S(2)}) collective-permute-start(bf16[80,512]{1,0:T(8,128)(2,1)} %get-tuple-element.45), channel_id=1, source_target_pairs={{0,96},{32,0},{64,32},{96,64},{1,97},{33,1},{65,33},{97,65},{2,98}... | collective-permute-start | bytes 245768 | tf_op jit(solution)/shard_map/ppermute | solution.py:226
  128.9 2.7 %copy-start.3 = (bf16[80,512]{1,0:T(8,128)(2,1)}, bf16[80,512]{1,0:T(8,128)(2,1)S(1)}, u32[]{:S(2)}) copy-start(bf16[80,512]{1,0:T(8,128)(2,1)S(1)} %collective-permute-done.6.b_ref) | copy-start | bytes 245764
  129.0 2.7 %copy-start.4 = (bf16[80,512]{1,0:T(8,128)(2,1)}, bf16[80,512]{1,0:T(8,128)(2,1)S(1)}, u32[]{:S(2)}) copy-start(bf16[80,512]{1,0:T(8,128)(2,1)S(1)} %collective-permute-done.7.c_ref) | copy-start | bytes 245764
  134.1 24.8 %collective-permute-start.9 = (f32[24,512]{1,0:T(8,128)}, f32[24,512]{1,0:T(8,128)S(1)}, u32[]{:S(2)}, u32[]{:S(2)}) collective-permute-start(f32[24,512]{1,0:T(8,128)} %get-tuple-element.47), channel_id=1, source_target_pairs={{0,128},{128,256},{256,384},{384,0},{1,129},{129,257},{257,385},{3... | collective-permute-start | bytes 147464 | tf_op jit(solution)/shard_map/ppermute | solution.py:226
  136.7 22.2 %collective-permute-start.10 = (f32[24,512]{1,0:T(8,128)}, f32[24,512]{1,0:T(8,128)S(1)}, u32[]{:S(2)}, u32[]{:S(2)}) collective-permute-start(f32[24,512]{1,0:T(8,128)} %get-tuple-element.48), channel_id=1, source_target_pairs={{0,256},{128,384},{256,0},{384,128},{1,257},{129,385},{257,1},{385... | collective-permute-start | bytes 147464 | tf_op jit(solution)/shard_map/ppermute | solution.py:226
  143.6 15.3 %collective-permute-start.11 = (f32[24,512]{1,0:T(8,128)}, f32[24,512]{1,0:T(8,128)S(1)}, u32[]{:S(2)}, u32[]{:S(2)}) collective-permute-start(f32[24,512]{1,0:T(8,128)} %get-tuple-element.49), channel_id=1, source_target_pairs={{0,384},{128,0},{256,128},{384,256},{1,385},{129,1},{257,129},{385... | collective-permute-start | bytes 147464 | tf_op jit(solution)/shard_map/ppermute | solution.py:226
  150.6 0.9 copy-start
  (5 other events, 3.4 us)
Sparse Core Ops, SparseCore 0:
  10.7 41.0 all-gather.2
  73.9 34.0 reduce-scatter.1

commit v5 on v3

v5 whole, which is shorter than its diff:
```python
import jax
import jax.numpy as jnp
from jax import lax
from jax.experimental import pallas as pl
from jax.experimental.pallas import tpu as pltpu
from jax.sharding import Mesh, PartitionSpec as P

epsilon = 1e-05
EXPERT = ("y", "core")
SMEM = pl.BlockSpec(memory_space=pltpu.SMEM)
PAD = 16
NORMED_FLOPS = 4 * 10**9
DISPATCH_FLOPS = 20 * 10**9


def whole(shape):
    return pl.BlockSpec(shape, lambda *at: (0,) * len(shape))


def call(
    kernel, *operands, out, limit=60, grid=1, scratch=(), in_specs=None, out_specs=None, flops=None
):
    cost = {}
    if flops:
        cost["cost_estimate"] = pl.CostEstimate(
            flops=flops, bytes_accessed=10**7, transcendentals=0
        )
    return pl.pallas_call(
        kernel,
        grid=(grid,),
        in_specs=in_specs or [SMEM if o.shape == (1,) else whole(o.shape) for o in operands],
        out_specs=out_specs or [whole(shape) for shape, _ in out],
        out_shape=[jax.ShapeDtypeStruct(shape, kind) for shape, kind in out],
        scratch_shapes=[pltpu.VMEM(shape, kind) for shape, kind in scratch],
        compiler_params=pltpu.CompilerParams(
            dimension_semantics=("arbitrary",), vmem_limit_bytes=limit * 2**20
        ),
        **cost,
    )(*operands)


def column(row):
    return jnp.transpose(jnp.broadcast_to(row, (8, row.shape[1])))[:, 0:1]


def pieces(row):
    high = row.astype(jnp.bfloat16).astype(jnp.float32)
    middle = (row - high).astype(jnp.bfloat16).astype(jnp.float32)
    low = row - high - middle
    at = lax.broadcasted_iota(jnp.int32, (PAD, row.shape[1]), 0)
    rows = jnp.where(at == 0, high, jnp.where(at == 1, middle, jnp.where(at == 2, low, 0.0)))
    return rows.astype(jnp.bfloat16)


def pack_kernel(value_ref, input_ref, weight_ref, packed_ref, copies_ref):
    rows = value_ref.shape[0]
    inputs = input_ref[...].astype(jnp.float32)
    squares = jnp.sum(inputs * inputs, axis=1, keepdims=True)
    row = jnp.transpose(jnp.broadcast_to(squares, (squares.shape[0], 8)))[0:1, :]
    packed_ref[0:rows, :] = value_ref[...]
    packed_ref[rows:, :] = pieces(row)
    for peer in range(copies_ref.shape[0]):
        copies_ref[peer] = weight_ref[...]


def route_kernel(routes_ref, logits_ref, slot_ref, gate_ref):
    experts, group = slot_ref.shape
    expert = lax.broadcasted_iota(jnp.int32, (experts, group), 0)
    first = routes_ref[0:1, :] == expert
    second = routes_ref[1:2, :] == expert
    named = jnp.where(first | second, 1.0, 0.0)
    earlier = lax.broadcasted_iota(jnp.int32, (group, group), 0) < lax.broadcasted_iota(
        jnp.int32, (group, group), 1
    )
    count = jnp.dot(
        named.astype(jnp.bfloat16),
        jnp.where(earlier, 1.0, 0.0).astype(jnp.bfloat16),
        preferred_element_type=jnp.float32,
    )
    slot_ref[...] = jnp.where(named > 0.0, count, -1.0).astype(jnp.int32)
    low, high = logits_ref[0:1, :], logits_ref[1:2, :]
    gate_first = 1.0 / (1.0 + jnp.exp(high - low))
    gate_second = 1.0 / (1.0 + jnp.exp(low - high))
    gate_ref[...] = jnp.where(first, gate_first, jnp.where(second, gate_second, 0.0))


def value_kernel(
    width, squares_ref, value_ref, input_ref, gain_ref, d_value_ref, inverse_ref, normed_ref
):
    group = input_ref.shape[0]

    @pl.when(pl.program_id(0) == 0)
    def _():
        squares = jnp.zeros((1, group), jnp.float32)
        for device in range(squares_ref.shape[0]):
            part = squares_ref[device].astype(jnp.float32)
            squares += jnp.sum(part, axis=0, keepdims=True)
        inverse = 1.0 / jnp.sqrt(squares / width + epsilon)
        tile = group // 8
        for at in range(8):
            inverse_ref[at : at + 1, :] = inverse[:, at * tile : (at + 1) * tile]
        scaled = input_ref[...].astype(jnp.float32) * column(inverse)
        normed_ref[...] = (scaled * gain_ref[...]).astype(jnp.bfloat16)

    xs, zl, _, own, _ = d_value_ref.shape
    partial = lax.dot_general(
        value_ref[...].reshape(group, -1),
        normed_ref[...],
        (((0,), (0,)), ((), ())),
        preferred_element_type=jnp.float32,
    )
    for low in range(zl):
        for x in range(xs):
            start = (low * xs + x) * own
            d_value_ref[x, low, 0] = partial[start : start + own, :]


def normed_kernel(
    me_ref, value_ref, input_ref, grad_ref, gain_ref, inverse_ref, *refs
):
    parts, (base_ref, inner_ref, d_gain_ref, weight_ref) = refs[:-4], refs[-4:]
    step = pl.program_id(0)

    @pl.when(step == 0)
    def _():
        xs = len(parts)
        zl, zh, own, _ = parts[0].shape
        for x_step, part in enumerate(parts):
            x = lax.rem(me_ref[0] + (xs - x_step), xs)
            for low in range(zl):
                for high in range(zh):
                    start = pl.multiple_of(((high * zl + low) * xs + x) * own, own)
                    weight_ref[pl.ds(start, own), :] = part[low, high]
        d_gain_ref[...] = jnp.zeros(d_gain_ref.shape, jnp.float32)

    devices, rows, features = value_ref.shape
    d_normed = jnp.dot(
        value_ref[...].reshape(devices * rows, features),
        weight_ref[...],
        preferred_element_type=jnp.float32,
    )
    d_gain = d_gain_ref[...]
    for at in range(devices):
        tokens = slice(at * rows, (at + 1) * rows)
        inverse = column(inverse_ref[pl.ds(step * devices + at, 1), :])
        normed = d_normed[tokens, :]
        scaled = input_ref[tokens, :].astype(jnp.float32) * inverse
        weighted = normed * gain_ref[...]
        d_gain += jnp.sum(normed * scaled, axis=0, keepdims=True)
        inner = jnp.sum(weighted * scaled, axis=1, keepdims=True)
        inner = jnp.transpose(jnp.broadcast_to(inner, (rows, 8)))[0:1, :]
        for peer in range(inner_ref.shape[0]):
            inner_ref[peer, pl.ds(step * devices + at, 1), :] = inner
        base_ref[tokens, :] = grad_ref[tokens, :].astype(jnp.float32) + weighted * inverse
    d_gain_ref[...] = d_gain


def dispatch_kernel(
    width, inverse_ref, inner_ref, slot_ref, gate_ref, base_ref, input_ref, out_ref, stream_ref
):
    step = pl.program_id(0)
    group = input_ref.shape[0]
    experts, capacity, _ = out_ref.shape

    @pl.when(step == 0)
    def _():
        inverse = inverse_ref[...]
        inner = jnp.sum(inner_ref[...], axis=0) / width
        factor = jnp.transpose(inner * inverse * inverse)
        tile = group // 8
        for at in range(8):
            rows = pl.ds(at * tile, tile)
            stream = (
                base_ref[rows, :]
                - input_ref[rows, :].astype(jnp.float32) * factor[:, at : at + 1]
            )
            stream_ref[rows, :] = stream.astype(jnp.bfloat16)

    for at in range(experts):
        slot = slot_ref[pl.ds(step * experts + at, 1), :]
        gate = gate_ref[pl.ds(step * experts + at, 1), :]
        taken = lax.broadcasted_iota(jnp.int32, (capacity, group), 0) == slot
        gates = jnp.sum(jnp.where(taken, gate, 0.0), axis=1, keepdims=True)
        picked = jnp.dot(
            jnp.where(taken, 1.0, 0.0).astype(jnp.bfloat16),
            stream_ref[...],
            preferred_element_type=jnp.float32,
        )
        out_ref[at] = (gates * picked).astype(jnp.bfloat16)


def low_split_kernel(me_ref, d_value_ref, d_gain_ref, *outs):
    count = len(outs)
    rows = d_value_ref.shape[0] // count
    behind = pieces(d_gain_ref[...])
    for k, out in enumerate(outs):
        start = pl.multiple_of(lax.rem(me_ref[0] + k, count) * rows, rows)
        out[0:rows, :] = d_value_ref[pl.ds(start, rows), :].astype(jnp.bfloat16)
        out[rows:, :] = behind


def high_split_kernel(me_ref, a_ref, b_ref, c_ref, d_ref, sum_ref, *outs):
    count = len(outs)
    total = a_ref[...].astype(jnp.float32)
    for ref in (b_ref, c_ref, d_ref):
        total += ref[...].astype(jnp.float32)
    sum_ref[...] = total
    rows = total.shape[0] - PAD
    gain = jnp.sum(total[rows:, :], axis=0, keepdims=True)
    own = rows // count
    for k, out in enumerate(outs):
        start = pl.multiple_of(lax.rem(me_ref[0] + k, count) * own, own)
        out[0:own, :] = sum_ref[pl.ds(start, own), :]
        out[own:, :] = jnp.broadcast_to(gain, (8, gain.shape[1]))


def finish_kernel(rescale, a_ref, b_ref, c_ref, d_ref, d_value_ref, d_gain_ref):
    total = (a_ref[...] + b_ref[...]) + (c_ref[...] + d_ref[...])
    rows = d_value_ref.shape[0]
    d_value_ref[...] = (total[0:rows, :] * rescale).astype(jnp.bfloat16)
    d_gain_ref[...] = total[rows : rows + 1, :] * rescale


def to_all(part, axis):
    size = lax.axis_size(axis)
    return lax.all_to_all(
        jnp.broadcast_to(part[None], (size,) + part.shape), axis, 0, 0, tiled=True
    )


def further(part, axis, step):
    size = lax.axis_size(axis)
    return lax.ppermute(part, axis, [(i, (i + step) % size) for i in range(size)])


def on_device(stream_grad, value_grad, attn_input, norm_gain, value_weight, gate_logits, routes):
    group, columns = attn_input.shape
    experts = lax.axis_size(EXPERT)
    zh, zl, xs = lax.axis_size("zh"), lax.axis_size("zl"), lax.axis_size("x")
    width = columns * experts
    tokens_all = group * zh * zl * xs
    rescale = float(tokens_all) ** (-0.5)
    capacity = min(group, 5 * group // (2 * experts))
    rows = value_weight.shape[0]
    features = rows * zh * zl * xs
    own_rows = value_grad.shape[0]
    f32, bf16 = jnp.float32, jnp.bfloat16
    gain_row = norm_gain[None]

    packed, copies = call(
        pack_kernel, value_grad, attn_input, value_weight,
        out=[((own_rows + PAD, features), bf16), ((zh, rows, columns), bf16)],
    )
    gathered = lax.all_gather(packed, EXPERT, axis=0)

    weight = to_all(lax.all_to_all(copies, "zh", 0, 0, tiled=True), "zl")
    weights = [weight] + [further(weight, "x", step) for step in range(1, xs)]
    gathered, weights[1] = lax.optimization_barrier((gathered, weights[1]))

    slot, gate = call(
        route_kernel, routes.T, gate_logits.T,
        out=[((experts, group), jnp.int32), ((experts, group), f32)],
    )

    block = features // zh
    d_value, inverse = call(
        lambda *refs: value_kernel(width, *refs), gathered, gathered, attn_input, gain_row,
        out=[((xs, zl, zh, rows, columns), f32), ((8, group // 8), f32)],
        in_specs=[
            pl.BlockSpec((experts, PAD, features), lambda i: (0, own_rows // PAD, 0)),
            pl.BlockSpec((experts, own_rows, block), lambda i: (0, 0, i)),
            whole((group, columns)),
            whole((1, columns)),
        ],
        out_specs=[
            pl.BlockSpec((xs, zl, 1, rows, columns), lambda i: (0, 0, i, 0, 0)),
            whole((8, group // 8)),
        ],
        scratch=[((group, columns), bf16)],
        grid=zh,
    )
    d_value = lax.psum_scatter(
        d_value.reshape(features, columns), "x", scatter_dimension=0, tiled=True
    )

    two = pl.BlockSpec((2 * own_rows, columns), lambda i: (i, 0))
    base, inner, own_gain = call(
        normed_kernel, lax.axis_index("x").reshape(1), gathered, attn_input, stream_grad,
        gain_row, inverse, *weights,
        out=[((group, columns), f32), ((experts, 8, group // 8), f32), ((1, columns), f32)],
        in_specs=[
            SMEM,
            pl.BlockSpec((2, own_rows, features), lambda i: (i, 0, 0)),
            two,
            two,
            whole((1, columns)),
            whole((8, group // 8)),
        ]
        + [whole(part.shape) for part in weights],
        out_specs=[two, whole((experts, 8, group // 8)), whole((1, columns))],
        scratch=[((features, columns), bf16)],
        grid=experts // 2,
        limit=40,
        flops=NORMED_FLOPS,
    )
    inner = lax.all_to_all(inner, EXPERT, 0, 0, tiled=True)

    (sent,) = call(
        lambda *refs: dispatch_kernel(width, *refs),
        inverse, inner, slot, gate, base, attn_input,
        out=[((experts, capacity, columns), bf16)],
        out_specs=[pl.BlockSpec((experts // 4, capacity, columns), lambda e: (e, 0, 0))],
        scratch=[((group, columns), bf16)],
        grid=4,
        flops=DISPATCH_FLOPS,
    )
    sent, own_gain = lax.optimization_barrier((sent, own_gain))
    arrived = lax.all_to_all(sent, EXPERT, split_axis=0, concat_axis=2, tiled=True)

    d_gain = lax.psum(own_gain, "x")
    part = (features // xs // zl + PAD, columns)
    parts = call(
        low_split_kernel, lax.axis_index("zl").reshape(1), d_value, d_gain,
        out=[(part, bf16)] * zl, limit=8,
    )
    parts = [parts[0]] + [further(parts[k], "zl", k) for k in range(1, zl)]
    part = (rows + 8, columns)
    _, *parts = call(
        high_split_kernel, lax.axis_index("zh").reshape(1), *parts,
        out=[(parts[0].shape, f32)] + [(part, f32)] * zh, limit=8,
    )
    parts = [parts[0]] + [further(parts[k], "zh", k) for k in range(1, zh)]
    d_value, d_gain = call(
        lambda *refs: finish_kernel(rescale, *refs), *parts,
        out=[((rows, columns), bf16), ((1, columns), f32)], limit=8,
    )
    return (d_value, d_gain.reshape(columns), arrived)


def solution(mesh):
    split = Mesh(mesh.devices.reshape(4, 4, 4, 4, 2), ("zh", "zl", "x", "y", "core"))
    dp = ("zh", "zl", "x")
    return jax.shard_map(
        on_device,
        mesh=split,
        in_specs=(
            P(dp, EXPERT),
            P(dp + EXPERT, None),
            P(dp, EXPERT),
            P(EXPERT),
            P(dp, EXPERT),
            P(dp, None),
            P(dp, None),
        ),
        out_specs=(P(dp, EXPERT), P(EXPERT), P(EXPERT, dp, None)),
        check_vma=False,
    )
```

time: 159 us -> 154 us (0.969)
  local copies, waits for them, and re-layouts: 18.9 us -> 8.44 us
  Pallas kernels: 14 us -> 22.9 us
  matrix products: 4.55 us -> 0 us
    pallas_call x7 -> x8, Pallas kernels: 14 us -> 22.9 us  [call(): pl.pallas_call(kernel, grid=(grid,), in_specs=in_specs or [SMEM if o.shap...]
    dot_general x1 -> x0, matrix products: 4.55 us -> none  [on_device(): d_normed = jnp.dot(every_value, every_weight, preferred_element_type=f32)]
    dynamic_update_slice x4 -> x0, local copies, waits for them, and re-layouts: 4.21 us -> none  [on_device(): lax.dynamic_update_slice(every_weight, part[:, :, None], (zero, zero, pla...]
    unnamed x24 -> x20, local copies, waits for them, and re-layouts: 9.66 us -> 6.56 us
    ppermute x9, waiting for transfers between devices: 12.5 us -> 15 us  [further(): lax.ppermute(part, axis, [(i, (i + step) % size) for i in range(size)])]
    all_to_all x1, local copies, waits for them, and re-layouts: 3.6 us -> 1.86 us  [on_device(): lax.all_to_all(sent, EXPERT, split_axis=0, concat_axis=2, tiled=True)]
  transfers between devices with their start and end apart: 13 -> 13, of which waited for: 5 -> 6; matrix products, arithmetic and copies ran while one was open for 9% -> 1% of each run, Pallas kernels for 8% -> 13%
where the time goes in v5:
time: 154 us; the launch traced here: 153 us
  blocking collectives  45.1 us (29%)
  starting transfers between devices  44.7 us (29%)
  Pallas kernels  22.9 us (15%)
  waiting for transfers between devices  18.1 us (12%)
  between operations  14.2 us (9%)
  local copies, waits for them, and re-layouts  8.44 us (5%)
    ppermute x9, starting transfers between devices, further(): lax.ppermute(part, axis, [(i, (i + step) % size) for i in range(size)])  31.1 us
    all_to_all x1, blocking collectives, on_device(): weight = to_all(lax.all_to_all(copies, 'zh', 0, 0, tiled=True), 'zl')  28.1 us
    pallas_call x8, Pallas kernels, call(): pl.pallas_call(kernel, grid=(grid,), in_specs=in_specs or [SMEM if o.shap...  22.9 us
    ppermute x9, waiting for transfers between devices, further(): lax.ppermute(part, axis, [(i, (i + step) % size) for i in range(size)])  15 us
    all_to_all x1, blocking collectives, to_all(): lax.all_to_all(jnp.broadcast_to(part[None], (size,) + part.shape), axis,...  9.33 us
    all_to_all x1, starting transfers between devices, on_device(): inner = lax.all_to_all(inner, EXPERT, 0, 0, tiled=True)  9.33 us
    psum x1, blocking collectives, on_device(): d_gain = lax.psum(own_gain, 'x')  7.6 us
    unnamed x20, local copies, waits for them, and re-layouts  6.56 us
  transfers between devices with their start and end apart: 13, of which 6 were waited for; matrix products, arithmetic and copies ran while one was open for 1% of the time, Pallas kernels for 13%

profile of v5, /device:TPU:1, one launch (start us, length us, event | category | flops | bytes accessed | tf_op | source)
XLA Modules:
  0.0 153.4 jit_solution(2883239038617972337)
XLA Ops:
  7.2 2.4 %shard_map.94 = (bf16[144,1024]{1,0:T(8,128)(2,1)}, bf16[4,16,512]{2,1,0:T(8,128)(2,1)}) custom-call(bf16[128,1024]{1,0:T(8,128)(2,1)} %value_ref.1, bf16[1024,512]{1,0:T(8,128)(2,1)} %refs_5_.1, bf16[16,512]{1,0:T(8,128)(2,1)} %weight_ref.1), custom_call_target="tpu_custom_call" | custom-call | tf_op jit(solution)/shard_map/pallas_call | solution.py:28
  9.7 28.1 %all_to_all.33 = bf16[4,16,512]{2,1,0:T(8,128)(2,1)S(1)} all-to-all(bf16[4,16,512]{2,1,0:T(8,128)(2,1)} %get-tuple-element.27), channel_id=1, replica_groups=mesh['zh'=4,'zl'=4,'x'=4,'y'=4,'core'=2] {'zh'}, dimensions={0} | all-to-all | bytes 131072 | tf_op jit(solution)/shard_map/all_to_all | solution.py:256
  37.8 9.3 %all_to_all.34.refs_0_ = bf16[4,4,16,512]{3,2,1,0:T(8,128)(2,1)} all-to-all(bf16[4,4,16,512]{3,2,1,0:T(8,128)(2,1)S(1)} %broadcast_in_dim.4), channel_id=1, replica_groups=mesh['zh'=4,'zl'=4,'x'=4,'y'=4,'core'=2] {'zl'}, dimensions={0} | all-to-all | bytes 524288 | tf_op jit(solution)/shard_map/all_to_all | solution.py:226
  47.2 3.1 %collective-permute-start = (bf16[4,4,16,512]{3,2,1,0:T(8,128)(2,1)}, bf16[4,4,16,512]{3,2,1,0:T(8,128)(2,1)S(1)}, u32[]{:S(2)}, u32[]{:S(2)}) collective-permute-start(bf16[4,4,16,512]{3,2,1,0:T(8,128)(2,1)} %all_to_all.34.refs_0_), channel_id=1, source_target_pairs={{0,8},{8,16},{16,24},{24,0},{1,9},{9,17},{17,25},{25,1},{2,10},{10... | collective-permute-start | bytes 786440 | tf_op jit(solution)/shard_map/ppermute | solution.py:233
  50.3 4.4 %collective-permute-start.1 = (bf16[4,4,16,512]{3,2,1,0:T(8,128)(2,1)}, bf16[4,4,16,512]{3,2,1,0:T(8,128)(2,1)}, u32[]{:S(2)}, u32[]{:S(2)}) collective-permute-start(bf16[4,4,16,512]{3,2,1,0:T(8,128)(2,1)} %all_to_all.34.refs_0_), channel_id=1, source_target_pairs={{0,16},{8,24},{16,0},{24,8},{1,17},{9,25},{17,1},{25,9},{2,18},{10... | collective-permute-start | bytes 786440 | tf_op jit(solution)/shard_map/ppermute | solution.py:233
  54.6 3.1 %collective-permute-start.2 = (bf16[4,4,16,512]{3,2,1,0:T(8,128)(2,1)}, bf16[4,4,16,512]{3,2,1,0:T(8,128)(2,1)}, u32[]{:S(2)}, u32[]{:S(2)}) collective-permute-start(bf16[4,4,16,512]{3,2,1,0:T(8,128)(2,1)} %all_to_all.34.refs_0_), channel_id=1, source_target_pairs={{0,24},{8,0},{16,8},{24,16},{1,25},{9,1},{17,9},{25,17},{2,26},{10... | collective-permute-start | bytes 786440 | tf_op jit(solution)/shard_map/ppermute | solution.py:233
  58.5 5.9 %shard_map.95 = (f32[4,4,4,16,512]{4,3,2,1,0:T(8,128)}, f32[8,128]{1,0:T(8,128)}) custom-call(bf16[8,144,1024]{2,1,0:T(8,128)(2,1)} %bitcast.14, bf16[8,144,1024]{2,1,0:T(8,128)(2,1)} %bitcast.15, bf16[1024,512]{1,0:T(8,128)(2,1)} %refs_5_.1, f32[1,512]{1,0:T(1,128)} %bitcast.17), custom_call_target="tpu_custom_call" | custom-call | tf_op jit(solution)/shard_map/pallas_call | solution.py:28
  67.5 4.7 %shard_map.96 = (f32[1024,512]{1,0:T(8,128)S(1)}, f32[8,8,128]{2,1,0:T(8,128)}, f32[1,512]{1,0:T(1,128)S(1)}) custom-call(s32[1]{0:T(128)} %bitcast.5.me_ref, bf16[8,144,1024]{2,1,0:T(8,128)(2,1)S(1)} %bitcast.16, bf16[1024,512]{1,0:T(8,128)(2,1)S(1)} %copy-done.1, bf16[1024,512]{1,0:T(8,128)(2,1)S(1)} %copy-done.4, f32[1,512]{1,0:T(1,128)S(1)} %bitcast.18, ...), custom_call_target="tpu_custom_call" | custom-call | flops 4000000000 | bytes 10000000 | tf_op jit(solution)/shard_map/pallas_call | solution.py:28
  73.6 9.3 %all-to-all-start.2 = ((f32[8,8,128]{2,1,0:T(8,128)}), f32[8,8,128]{2,1,0:T(8,128)S(1)}, u32[]{:S(2)}, u32[]{:S(2)}) async-start(f32[8,8,128]{2,1,0:T(8,128)} %get-tuple-element.32), calls=%async_computation.3 | async-start | bytes 65536 | tf_op jit(solution)/shard_map/all_to_all | solution.py:306
  82.9 1.6 %shard_map.97 = (s32[8,1024]{1,0:T(8,128)}, f32[8,1024]{1,0:T(8,128)}) custom-call(s32[2,1024]{1,0:T(2,128)} %bitcast.22, f32[2,1024]{1,0:T(2,128)} %bitcast.23), custom_call_target="tpu_custom_call" | custom-call | tf_op jit(solution)/shard_map/pallas_call | solution.py:28
  84.5 3.1 %all-to-all-done.2.refs_1_ = f32[8,8,128]{2,1,0:T(8,128)S(1)} async-done(((f32[8,8,128]{2,1,0:T(8,128)}), f32[8,8,128]{2,1,0:T(8,128)S(1)}, u32[]{:S(2)}, u32[]{:S(2)}) %all-to-all-start.2) | async-done | bytes 32800 | tf_op jit(solution)/shard_map/all_to_all | solution.py:306
  88.2 6.9 %shard_map.98 = bf16[8,320,512]{2,1,0:T(8,128)(2,1)} custom-call(f32[8,128]{1,0:T(8,128)} %get-tuple-element.30.inverse_ref.refs_0_, f32[8,8,128]{2,1,0:T(8,128)} %copy-done.9, s32[8,1024]{1,0:T(8,128)} %get-tuple-element.33.refs_2_, f32[8,1024]{1,0:T(8,128)} %get-tuple-element.34.refs_3_, f32[1024,512]{1,0:T(8,128)} %copy-done.8, bf16[1024,512]{1,0:T(8,128)(2,1)} %refs_5_.1), custom_call_target="tpu_custom_call" | custom-call | flops 20000000000 | bytes 10000000 | tf_op jit(solution)/shard_map/pallas_call | solution.py:28
  95.2 4.2 %all-to-all-start.3 = ((bf16[8,320,512]{2,1,0:T(8,128)(2,1)}), bf16[8,320,512]{2,1,0:T(8,128)(2,1)S(1)}, u32[]{:S(2)}, u32[]{:S(2)}) async-start(bf16[8,320,512]{2,1,0:T(8,128)(2,1)} %shard_map.98), calls=%async_computation.4 | async-start | bytes 5242880 | tf_op jit(solution)/shard_map/all_to_all | solution.py:318
  99.4 7.6 %psum.7.d_gain_ref = f32[1,512]{1,0:T(1,128)S(1)} all-reduce(f32[1,512]{1,0:T(1,128)S(1)} %get-tuple-element.37), channel_id=1, replica_groups=mesh['zh'=4,'zl'=4,'x'=4,'y'=4,'core'=2] {'x'}, use_global_device_ids=true, to_apply=%region_1.0 | all-reduce | flops 512 | bytes 4096 | tf_op jit(solution)/shard_map/psum | solution.py:320
  108.1 2.7 %collective-permute-start.3 = (bf16[80,512]{1,0:T(8,128)(2,1)S(1)}, bf16[80,512]{1,0:T(8,128)(2,1)S(1)}, u32[]{:S(2)}, u32[]{:S(2)}) collective-permute-start(bf16[80,512]{1,0:T(8,128)(2,1)S(1)} %get-tuple-element.39), channel_id=1, source_target_pairs={{0,32},{32,64},{64,96},{96,0},{1,33},{33,65},{65,97},{97,1},{2,34}... | collective-permute-start | bytes 245768 | tf_op jit(solution)/shard_map/ppermute | solution.py:233
  110.8 3.6 %collective-permute-start.4 = (bf16[80,512]{1,0:T(8,128)(2,1)S(1)}, bf16[80,512]{1,0:T(8,128)(2,1)S(1)}, u32[]{:S(2)}, u32[]{:S(2)}) collective-permute-start(bf16[80,512]{1,0:T(8,128)(2,1)S(1)} %get-tuple-element.40), channel_id=1, source_target_pairs={{0,64},{32,96},{64,0},{96,32},{1,65},{33,97},{65,1},{97,33},{2,66}... | collective-permute-start | bytes 245768 | tf_op jit(solution)/shard_map/ppermute | solution.py:233
  114.4 2.7 %collective-permute-start.5 = (bf16[80,512]{1,0:T(8,128)(2,1)S(1)}, bf16[80,512]{1,0:T(8,128)(2,1)S(1)}, u32[]{:S(2)}, u32[]{:S(2)}) collective-permute-start(bf16[80,512]{1,0:T(8,128)(2,1)S(1)} %get-tuple-element.41), channel_id=1, source_target_pairs={{0,96},{32,0},{64,32},{96,64},{1,97},{33,1},{65,33},{97,65},{2,98}... | collective-permute-start | bytes 245768 | tf_op jit(solution)/shard_map/ppermute | solution.py:233
  117.1 3.1 %collective-permute-done.4.c_ref = bf16[80,512]{1,0:T(8,128)(2,1)S(1)} collective-permute-done((bf16[80,512]{1,0:T(8,128)(2,1)S(1)}, bf16[80,512]{1,0:T(8,128)(2,1)S(1)}, u32[]{:S(2)}, u32[]{:S(2)}) %collective-permute-start.4) | collective-permute-done | bytes 81952 | tf_op jit(solution)/shard_map/ppermute | solution.py:233
  121.9 1.9 %collective-permute-start.6 = (f32[24,512]{1,0:T(8,128)S(1)}, f32[24,512]{1,0:T(8,128)S(1)}, u32[]{:S(2)}, u32[]{:S(2)}) collective-permute-start(f32[24,512]{1,0:T(8,128)S(1)} %get-tuple-element.43), channel_id=1, source_target_pairs={{0,128},{128,256},{256,384},{384,0},{1,129},{129,257},{257,385},{3... | collective-permute-start | bytes 147464 | tf_op jit(solution)/shard_map/ppermute | solution.py:233
  123.8 7.1 %collective-permute-start.7 = (f32[24,512]{1,0:T(8,128)S(1)}, f32[24,512]{1,0:T(8,128)S(1)}, u32[]{:S(2)}, u32[]{:S(2)}) collective-permute-start(f32[24,512]{1,0:T(8,128)S(1)} %get-tuple-element.44), channel_id=1, source_target_pairs={{0,256},{128,384},{256,0},{384,128},{1,257},{129,385},{257,1},{385... | collective-permute-start | bytes 147464 | tf_op jit(solution)/shard_map/ppermute | solution.py:233
  131.0 2.5 %collective-permute-start.8 = (f32[24,512]{1,0:T(8,128)S(1)}, f32[24,512]{1,0:T(8,128)S(1)}, u32[]{:S(2)}, u32[]{:S(2)}) collective-permute-start(f32[24,512]{1,0:T(8,128)S(1)} %get-tuple-element.45), channel_id=1, source_target_pairs={{0,384},{128,0},{256,128},{384,256},{1,385},{129,1},{257,129},{385... | collective-permute-start | bytes 147464 | tf_op jit(solution)/shard_map/ppermute | solution.py:233
  133.5 1.9 %copy.11 = bf16[1,8,40,8,512]{4,3,1,2,0:T(8,128)(2,1)} copy(bf16[1,8,40,8,512]{4,3,2,1,0:T(8,128)(2,1)S(1)} %bitcast.19) | data formatting | bytes 5242880 | tf_op jit(solution)/shard_map/all_to_all | solution.py:318
  135.3 2.0 %collective-permute-done.7.refs_2_ = f32[24,512]{1,0:T(8,128)S(1)} collective-permute-done((f32[24,512]{1,0:T(8,128)S(1)}, f32[24,512]{1,0:T(8,128)S(1)}, u32[]{:S(2)}, u32[]{:S(2)}) %collective-permute-start.7) | collective-permute-done | bytes 49184 | tf_op jit(solution)/shard_map/ppermute | solution.py:233
  137.4 8.6 %collective-permute-done.8.refs_3_ = f32[24,512]{1,0:T(8,128)S(1)} collective-permute-done((f32[24,512]{1,0:T(8,128)S(1)}, f32[24,512]{1,0:T(8,128)S(1)}, u32[]{:S(2)}, u32[]{:S(2)}) %collective-permute-start.8) | collective-permute-done | bytes 49184 | tf_op jit(solution)/shard_map/ppermute | solution.py:233
  (37 shorter events, 9.3 us)
Async XLA Ops:
  7.2 51.3 %all-gather.3.cloned.1.call-start = ((), (), s32[]{:S(2)}) async-start(), calls=%async_computation.6 | async-start | bytes 2654208 | tf_op jit(solution)/shard_map/all_gather | solution.py:254
  9.6 97.4 %reduce-scatter.2.cloned.1.call-start = ((), (), s32[]{:S(2)}) async-start(), calls=%async_computation.5 | async-start | bytes 2621440 | tf_op jit(solution)/shard_map/reduce_scatter | solution.py:282
  47.2 10.6 %collective-permute-start = (bf16[4,4,16,512]{3,2,1,0:T(8,128)(2,1)}, bf16[4,4,16,512]{3,2,1,0:T(8,128)(2,1)S(1)}, u32[]{:S(2)}, u32[]{:S(2)}) collective-permute-start(bf16[4,4,16,512]{3,2,1,0:T(8,128)(2,1)} %all_to_all.34.refs_0_), channel_id=1, source_target_pairs={{0,8},{8,16},{16,24},{24,0},{1,9},{9,17},{17,25},{25,1},{2,10},{10... | collective-permute-start | bytes 786440 | tf_op jit(solution)/shard_map/ppermute | solution.py:233
  50.3 14.1 %collective-permute-start.1 = (bf16[4,4,16,512]{3,2,1,0:T(8,128)(2,1)}, bf16[4,4,16,512]{3,2,1,0:T(8,128)(2,1)}, u32[]{:S(2)}, u32[]{:S(2)}) collective-permute-start(bf16[4,4,16,512]{3,2,1,0:T(8,128)(2,1)} %all_to_all.34.refs_0_), channel_id=1, source_target_pairs={{0,16},{8,24},{16,0},{24,8},{1,17},{9,25},{17,1},{25,9},{2,18},{10... | collective-permute-start | bytes 786440 | tf_op jit(solution)/shard_map/ppermute | solution.py:233
  54.6 10.0 %collective-permute-start.2 = (bf16[4,4,16,512]{3,2,1,0:T(8,128)(2,1)}, bf16[4,4,16,512]{3,2,1,0:T(8,128)(2,1)}, u32[]{:S(2)}, u32[]{:S(2)}) collective-permute-start(bf16[4,4,16,512]{3,2,1,0:T(8,128)(2,1)} %all_to_all.34.refs_0_), channel_id=1, source_target_pairs={{0,24},{8,0},{16,8},{24,16},{1,25},{9,1},{17,9},{25,17},{2,26},{10... | collective-permute-start | bytes 786440 | tf_op jit(solution)/shard_map/ppermute | solution.py:233
  57.7 0.7 copy-start.5
  58.5 6.2 %copy-start = (bf16[1152,1024]{1,0:T(8,128)(2,1)S(1)}, bf16[1152,1024]{1,0:T(8,128)(2,1)}, u32[]{:S(2)}) copy-start(bf16[1152,1024]{1,0:T(8,128)(2,1)} %all-gather.3.cloned.1.call-done) | copy-start | bytes 7077892
  58.5 6.2 %copy-start.1 = (bf16[1024,512]{1,0:T(8,128)(2,1)S(1)}, bf16[1024,512]{1,0:T(8,128)(2,1)}, u32[]{:S(2)}) copy-start(bf16[1024,512]{1,0:T(8,128)(2,1)} %refs_5_.1) | copy-start | bytes 3145732
  58.5 6.2 %copy-start.3 = (f32[512]{0:T(512)S(1)}, f32[512]{0:T(512)}, u32[]{:S(2)}) copy-start(f32[512]{0:T(512)} %param.10) | copy-start | bytes 6148
  64.7 1.2 copy-start.4
  65.9 0.9 copy-start.6
  66.8 0.7 copy-start.7
  72.2 1.4 copy-start.8
  73.6 14.1 %all-to-all-start.2 = ((f32[8,8,128]{2,1,0:T(8,128)}), f32[8,8,128]{2,1,0:T(8,128)S(1)}, u32[]{:S(2)}, u32[]{:S(2)}) async-start(f32[8,8,128]{2,1,0:T(8,128)} %get-tuple-element.32), calls=%async_computation.3 | async-start | bytes 65536 | tf_op jit(solution)/shard_map/all_to_all | solution.py:306
  87.6 0.6 copy-start.9
  95.2 38.3 %all-to-all-start.3 = ((bf16[8,320,512]{2,1,0:T(8,128)(2,1)}), bf16[8,320,512]{2,1,0:T(8,128)(2,1)S(1)}, u32[]{:S(2)}, u32[]{:S(2)}) async-start(bf16[8,320,512]{2,1,0:T(8,128)(2,1)} %shard_map.98), calls=%async_computation.4 | async-start | bytes 5242880 | tf_op jit(solution)/shard_map/all_to_all | solution.py:318
  107.0 1.0 copy-start.2
  108.1 9.0 %collective-permute-start.3 = (bf16[80,512]{1,0:T(8,128)(2,1)S(1)}, bf16[80,512]{1,0:T(8,128)(2,1)S(1)}, u32[]{:S(2)}, u32[]{:S(2)}) collective-permute-start(bf16[80,512]{1,0:T(8,128)(2,1)S(1)} %get-tuple-element.39), channel_id=1, source_target_pairs={{0,32},{32,64},{64,96},{96,0},{1,33},{33,65},{65,97},{97,1},{2,34}... | collective-permute-start | bytes 245768 | tf_op jit(solution)/shard_map/ppermute | solution.py:233
  110.8 9.4 %collective-permute-start.4 = (bf16[80,512]{1,0:T(8,128)(2,1)S(1)}, bf16[80,512]{1,0:T(8,128)(2,1)S(1)}, u32[]{:S(2)}, u32[]{:S(2)}) collective-permute-start(bf16[80,512]{1,0:T(8,128)(2,1)S(1)} %get-tuple-element.40), channel_id=1, source_target_pairs={{0,64},{32,96},{64,0},{96,32},{1,65},{33,97},{65,1},{97,33},{2,66}... | collective-permute-start | bytes 245768 | tf_op jit(solution)/shard_map/ppermute | solution.py:233
  114.4 6.8 %collective-permute-start.5 = (bf16[80,512]{1,0:T(8,128)(2,1)S(1)}, bf16[80,512]{1,0:T(8,128)(2,1)S(1)}, u32[]{:S(2)}, u32[]{:S(2)}) collective-permute-start(bf16[80,512]{1,0:T(8,128)(2,1)S(1)} %get-tuple-element.41), channel_id=1, source_target_pairs={{0,96},{32,0},{64,32},{96,64},{1,97},{33,1},{65,33},{97,65},{2,98}... | collective-permute-start | bytes 245768 | tf_op jit(solution)/shard_map/ppermute | solution.py:233
  121.9 13.4 %collective-permute-start.6 = (f32[24,512]{1,0:T(8,128)S(1)}, f32[24,512]{1,0:T(8,128)S(1)}, u32[]{:S(2)}, u32[]{:S(2)}) collective-permute-start(f32[24,512]{1,0:T(8,128)S(1)} %get-tuple-element.43), channel_id=1, source_target_pairs={{0,128},{128,256},{256,384},{384,0},{1,129},{129,257},{257,385},{3... | collective-permute-start | bytes 147464 | tf_op jit(solution)/shard_map/ppermute | solution.py:233
  123.8 13.5 %collective-permute-start.7 = (f32[24,512]{1,0:T(8,128)S(1)}, f32[24,512]{1,0:T(8,128)S(1)}, u32[]{:S(2)}, u32[]{:S(2)}) collective-permute-start(f32[24,512]{1,0:T(8,128)S(1)} %get-tuple-element.44), channel_id=1, source_target_pairs={{0,256},{128,384},{256,0},{384,128},{1,257},{129,385},{257,1},{385... | collective-permute-start | bytes 147464 | tf_op jit(solution)/shard_map/ppermute | solution.py:233
  131.0 15.0 %collective-permute-start.8 = (f32[24,512]{1,0:T(8,128)S(1)}, f32[24,512]{1,0:T(8,128)S(1)}, u32[]{:S(2)}, u32[]{:S(2)}) collective-permute-start(f32[24,512]{1,0:T(8,128)S(1)} %get-tuple-element.45), channel_id=1, source_target_pairs={{0,384},{128,0},{256,128},{384,256},{1,385},{129,1},{257,129},{385... | collective-permute-start | bytes 147464 | tf_op jit(solution)/shard_map/ppermute | solution.py:233
Sparse Core Ops, SparseCore 0:
  10.7 39.0 all-gather.2
  64.5 32.8 reduce-scatter.1

commit v6 on v5

--- a/solution.py
+++ b/solution.py
@@ -7,8 +7,11 @@
 
 epsilon = 1e-05
 EXPERT = ("y", "core")
+ANY = pl.BlockSpec(memory_space=pl.ANY)
 SMEM = pl.BlockSpec(memory_space=pltpu.SMEM)
 PAD = 16
+VALUE_LIMIT = 62
+NORMED_LIMIT = 52
 NORMED_FLOPS = 4 * 10**9
 DISPATCH_FLOPS = 20 * 10**9
 
@@ -31,7 +34,7 @@
         in_specs=in_specs or [SMEM if o.shape == (1,) else whole(o.shape) for o in operands],
         out_specs=out_specs or [whole(shape) for shape, _ in out],
         out_shape=[jax.ShapeDtypeStruct(shape, kind) for shape, kind in out],
-        scratch_shapes=[pltpu.VMEM(shape, kind) for shape, kind in scratch],
+        scratch_shapes=scratch,
         compiler_params=pltpu.CompilerParams(
             dimension_semantics=("arbitrary",), vmem_limit_bytes=limit * 2**20
         ),
@@ -85,58 +88,84 @@
 
 
 def value_kernel(
-    width, squares_ref, value_ref, input_ref, gain_ref, d_value_ref, inverse_ref, normed_ref
+    width, gathered_ref, whole_input_ref, gain_ref, d_value_ref, inverse_ref,
+    squares_ref, input_ref, value_ref, normed_ref, partial_ref, sems,
 ):
+    devices, rows, features = value_ref.shape
     group = input_ref.shape[0]
-
-    @pl.when(pl.program_id(0) == 0)
-    def _():
-        squares = jnp.zeros((1, group), jnp.float32)
-        for device in range(squares_ref.shape[0]):
-            part = squares_ref[device].astype(jnp.float32)
-            squares += jnp.sum(part, axis=0, keepdims=True)
-        inverse = 1.0 / jnp.sqrt(squares / width + epsilon)
-        tile = group // 8
-        for at in range(8):
-            inverse_ref[at : at + 1, :] = inverse[:, at * tile : (at + 1) * tile]
-        scaled = input_ref[...].astype(jnp.float32) * column(inverse)
-        normed_ref[...] = (scaled * gain_ref[...]).astype(jnp.bfloat16)
-
-    xs, zl, _, own, _ = d_value_ref.shape
-    partial = lax.dot_general(
-        value_ref[...].reshape(group, -1),
-        normed_ref[...],
-        (((0,), (0,)), ((), ())),
-        preferred_element_type=jnp.float32,
-    )
-    for low in range(zl):
-        for x in range(xs):
-            start = (low * xs + x) * own
-            d_value_ref[x, low, 0] = partial[start : start + own, :]
+    get_squares = pltpu.make_async_copy(
+        gathered_ref.at[:, pl.ds(rows, PAD), :], squares_ref, sems.at[0]
+    )
+    get_value = pltpu.make_async_copy(
+        gathered_ref.at[:, pl.ds(0, rows), :], value_ref, sems.at[1]
+    )
+    get_input = pltpu.make_async_copy(whole_input_ref, input_ref, sems.at[2])
+    get_squares.start()
+    get_input.start()
+    get_value.start()
+    get_squares.wait()
+    squares = jnp.zeros((1, group), jnp.float32)
+    for device in range(devices):
+        part = squares_ref[device].astype(jnp.float32)
+        squares += jnp.sum(part, axis=0, keepdims=True)
+    inverse = 1.0 / jnp.sqrt(squares / width + epsilon)
+    tile = group // 8
+    for at in range(8):
+        inverse_ref[at : at + 1, :] = inverse[:, at * tile : (at + 1) * tile]
+    get_input.wait()
+    scaled = input_ref[...].astype(jnp.float32) * column(inverse)
+    normed_ref[...] = (scaled * gain_ref[...]).astype(jnp.bfloat16)
+
+    zh, xs, zl, own, _ = partial_ref.shape
+    block = features // zh
+    get_value.wait()
+    puts = []
+    for high in range(zh):
+        partial = lax.dot_general(
+            value_ref[:, :, high * block : (high + 1) * block].reshape(group, block),
+            normed_ref[...],
+            (((0,), (0,)), ((), ())),
+            preferred_element_type=jnp.float32,
+        )
+        for low in range(zl):
+            for x in range(xs):
+                start = (low * xs + x) * own
+                partial_ref[high, x, low] = partial[start : start + own, :]
+        put = pltpu.make_async_copy(
+            partial_ref.at[high], d_value_ref.at[:, :, high], sems.at[3 + high]
+        )
+        put.start()
+        puts.append(put)
+    for put in puts:
+        put.wait()
 
 
 def normed_kernel(
     me_ref, value_ref, input_ref, grad_ref, gain_ref, inverse_ref, *refs
 ):
-    parts, (base_ref, inner_ref, d_gain_ref, weight_ref) = refs[:-4], refs[-4:]
+    parts, (base_ref, inner_ref, d_gain_ref, weight_ref, sems) = refs[:-5], refs[-5:]
     step = pl.program_id(0)
 
     @pl.when(step == 0)
     def _():
-        xs = len(parts)
-        zl, zh, own, _ = parts[0].shape
+        xs, zl = len(parts), parts[0].shape[0]
+        gets = []
         for x_step, part in enumerate(parts):
             x = lax.rem(me_ref[0] + (xs - x_step), xs)
             for low in range(zl):
-                for high in range(zh):
-                    start = pl.multiple_of(((high * zl + low) * xs + x) * own, own)
-                    weight_ref[pl.ds(start, own), :] = part[low, high]
+                get = pltpu.make_async_copy(
+                    part.at[low], weight_ref.at[:, low, x], sems.at[x_step, low]
+                )
+                get.start()
+                gets.append(get)
         d_gain_ref[...] = jnp.zeros(d_gain_ref.shape, jnp.float32)
+        for get in gets:
+            get.wait()
 
     devices, rows, features = value_ref.shape
     d_normed = jnp.dot(
         value_ref[...].reshape(devices * rows, features),
-        weight_ref[...],
+        weight_ref[...].reshape(features, -1),
         preferred_element_type=jnp.float32,
     )
     d_gain = d_gain_ref[...]
@@ -199,23 +228,20 @@
         out[rows:, :] = behind
 
 
-def high_split_kernel(me_ref, a_ref, b_ref, c_ref, d_ref, sum_ref, *outs):
-    count = len(outs)
+def high_split_kernel(a_ref, b_ref, c_ref, d_ref, out_ref):
     total = a_ref[...].astype(jnp.float32)
     for ref in (b_ref, c_ref, d_ref):
         total += ref[...].astype(jnp.float32)
-    sum_ref[...] = total
     rows = total.shape[0] - PAD
     gain = jnp.sum(total[rows:, :], axis=0, keepdims=True)
-    own = rows // count
-    for k, out in enumerate(outs):
-        start = pl.multiple_of(lax.rem(me_ref[0] + k, count) * own, own)
-        out[0:own, :] = sum_ref[pl.ds(start, own), :]
-        out[own:, :] = jnp.broadcast_to(gain, (8, gain.shape[1]))
-
-
-def finish_kernel(rescale, a_ref, b_ref, c_ref, d_ref, d_value_ref, d_gain_ref):
-    total = (a_ref[...] + b_ref[...]) + (c_ref[...] + d_ref[...])
+    own = rows // out_ref.shape[0]
+    for at in range(out_ref.shape[0]):
+        out_ref[at, 0:own, :] = total[at * own : (at + 1) * own, :]
+        out_ref[at, own:, :] = jnp.broadcast_to(gain, (8, gain.shape[1]))
+
+
+def finish_kernel(rescale, parts_ref, d_value_ref, d_gain_ref):
+    total = jnp.sum(parts_ref[...], axis=0)
     rows = d_value_ref.shape[0]
     d_value_ref[...] = (total[0:rows, :] * rescale).astype(jnp.bfloat16)
     d_gain_ref[...] = total[rows : rows + 1, :] * rescale
@@ -262,22 +288,20 @@
         out=[((experts, group), jnp.int32), ((experts, group), f32)],
     )
 
-    block = features // zh
     d_value, inverse = call(
-        lambda *refs: value_kernel(width, *refs), gathered, gathered, attn_input, gain_row,
+        lambda *refs: value_kernel(width, *refs), gathered, attn_input, gain_row,
         out=[((xs, zl, zh, rows, columns), f32), ((8, group // 8), f32)],
-        in_specs=[
-            pl.BlockSpec((experts, PAD, features), lambda i: (0, own_rows // PAD, 0)),
-            pl.BlockSpec((experts, own_rows, block), lambda i: (0, 0, i)),
-            whole((group, columns)),
-            whole((1, columns)),
+        in_specs=[ANY, ANY, whole((1, columns))],
+        out_specs=[ANY, whole((8, group // 8))],
+        scratch=[
+            pltpu.VMEM((experts, PAD, features), bf16),
+            pltpu.VMEM((group, columns), bf16),
+            pltpu.VMEM((experts, own_rows, features), bf16),
+            pltpu.VMEM((group, columns), bf16),
+            pltpu.VMEM((zh, xs, zl, rows, columns), f32),
+            pltpu.SemaphoreType.DMA((3 + zh,)),
         ],
-        out_specs=[
-            pl.BlockSpec((xs, zl, 1, rows, columns), lambda i: (0, 0, i, 0, 0)),
-            whole((8, group // 8)),
-        ],
-        scratch=[((group, columns), bf16)],
-        grid=zh,
+        limit=VALUE_LIMIT,
     )
     d_value = lax.psum_scatter(
         d_value.reshape(features, columns), "x", scatter_dimension=0, tiled=True
@@ -296,11 +320,14 @@
             whole((1, columns)),
             whole((8, group // 8)),
         ]
-        + [whole(part.shape) for part in weights],
+        + [ANY] * xs,
         out_specs=[two, whole((experts, 8, group // 8)), whole((1, columns))],
-        scratch=[((features, columns), bf16)],
+        scratch=[
+            pltpu.VMEM((zh, zl, xs, rows, columns), bf16),
+            pltpu.SemaphoreType.DMA((xs, zl)),
+        ],
         grid=experts // 2,
-        limit=40,
+        limit=NORMED_LIMIT,
         flops=NORMED_FLOPS,
     )
     inner = lax.all_to_all(inner, EXPERT, 0, 0, tiled=True)
@@ -310,7 +337,7 @@
         inverse, inner, slot, gate, base, attn_input,
         out=[((experts, capacity, columns), bf16)],
         out_specs=[pl.BlockSpec((experts // 4, capacity, columns), lambda e: (e, 0, 0))],
-        scratch=[((group, columns), bf16)],
+        scratch=[pltpu.VMEM((group, columns), bf16)],
         grid=4,
         flops=DISPATCH_FLOPS,
     )
@@ -324,14 +351,12 @@
         out=[(part, bf16)] * zl, limit=8,
     )
     parts = [parts[0]] + [further(parts[k], "zl", k) for k in range(1, zl)]
-    part = (rows + 8, columns)
-    _, *parts = call(
-        high_split_kernel, lax.axis_index("zh").reshape(1), *parts,
-        out=[(parts[0].shape, f32)] + [(part, f32)] * zh, limit=8,
-    )
-    parts = [parts[0]] + [further(parts[k], "zh", k) for k in range(1, zh)]
+    (parts,) = call(
+        high_split_kernel, *parts, out=[((zh, rows + 8, columns), f32)], limit=8,
+    )
+    parts = lax.all_to_all(parts, "zh", 0, 0, tiled=True)
     d_value, d_gain = call(
-        lambda *refs: finish_kernel(rescale, *refs), *parts,
+        lambda *refs: finish_kernel(rescale, *refs), parts,
         out=[((rows, columns), bf16), ((1, columns), f32)], limit=8,
     )
     return (d_value, d_gain.reshape(columns), arrived)

time: 154 us -> 156 us (1.013)
  the two profiles are of different devices: /device:TPU:1 before, /device:TPU:32 now
where the time goes in v6:
time: 156 us; the launch traced here: 155 us
  blocking collectives  48.3 us (31%)
  waiting for transfers between devices  32.7 us (21%)
  starting transfers between devices  32.1 us (21%)
  Pallas kernels  23.6 us (15%)
  between operations  14.2 us (9%)
  local copies, waits for them, and re-layouts  4.2 us (3%)
    all_to_all x1, blocking collectives, on_device(): weight = to_all(lax.all_to_all(copies, 'zh', 0, 0, tiled=True), 'zl')  28.3 us
    pallas_call x8, Pallas kernels, call(): pl.pallas_call(kernel, grid=(grid,), in_specs=in_specs or [SMEM if o.shap...  23.6 us
    ppermute x6, starting transfers between devices, further(): lax.ppermute(part, axis, [(i, (i + step) % size) for i in range(size)])  20.6 us
    all_to_all x1, waiting for transfers between devices, on_device(): parts = lax.all_to_all(parts, 'zh', 0, 0, tiled=True)  16.5 us
    psum x1, blocking collectives, on_device(): d_gain = lax.psum(own_gain, 'x')  10.2 us
    all_to_all x1, blocking collectives, to_all(): lax.all_to_all(jnp.broadcast_to(part[None], (size,) + part.shape), axis,...  9.76 us
    all_to_all x1, waiting for transfers between devices, on_device(): lax.all_to_all(sent, EXPERT, split_axis=0, concat_axis=2, tiled=True)  7.35 us
    ppermute x6, waiting for transfers between devices, further(): lax.ppermute(part, axis, [(i, (i + step) % size) for i in range(size)])  4.97 us
  transfers between devices with their start and end apart: 11, of which 6 were waited for; matrix products, arithmetic and copies ran while one was open for 1% of the time, Pallas kernels for 13%

profile of v6, /device:TPU:32, one launch (start us, length us, event | category | flops | bytes accessed | tf_op | source)
XLA Modules:
  0.0 155.1 jit_solution(16126993694498768263)
XLA Ops:
  7.2 2.4 %shard_map.94 = (bf16[144,1024]{1,0:T(8,128)(2,1)}, bf16[4,16,512]{2,1,0:T(8,128)(2,1)}) custom-call(bf16[128,1024]{1,0:T(8,128)(2,1)} %value_ref.1, bf16[1024,512]{1,0:T(8,128)(2,1)} %refs_5_.1, bf16[16,512]{1,0:T(8,128)(2,1)} %weight_ref.1), custom_call_target="tpu_custom_call" | custom-call | tf_op jit(solution)/shard_map/pallas_call | solution.py:31
  9.7 28.3 %all_to_all.38 = bf16[4,16,512]{2,1,0:T(8,128)(2,1)S(1)} all-to-all(bf16[4,16,512]{2,1,0:T(8,128)(2,1)} %get-tuple-element.23), channel_id=1, replica_groups=mesh['zh'=4,'zl'=4,'x'=4,'y'=4,'core'=2] {'zh'}, dimensions={0} | all-to-all | bytes 131072 | tf_op jit(solution)/shard_map/all_to_all | solution.py:282
  37.9 9.8 %all_to_all.39.refs_0_ = bf16[4,4,16,512]{3,2,1,0:T(8,128)(2,1)S(1)} all-to-all(bf16[4,4,16,512]{3,2,1,0:T(8,128)(2,1)S(1)} %broadcast_in_dim.4), channel_id=1, replica_groups=mesh['zh'=4,'zl'=4,'x'=4,'y'=4,'core'=2] {'zl'}, dimensions={0} | all-to-all | bytes 524288 | tf_op jit(solution)/shard_map/all_to_all | solution.py:252
  47.7 3.4 %collective-permute-start = (bf16[4,4,16,512]{3,2,1,0:T(8,128)(2,1)S(1)}, bf16[4,4,16,512]{3,2,1,0:T(8,128)(2,1)S(1)}, u32[]{:S(2)}, u32[]{:S(2)}) collective-permute-start(bf16[4,4,16,512]{3,2,1,0:T(8,128)(2,1)S(1)} %all_to_all.39.refs_0_), channel_id=1, source_target_pairs={{0,8},{8,16},{16,24},{24,0},{1,9},{9,17},{17,25},{25,1},{2,10},{10... | collective-permute-start | bytes 786440 | tf_op jit(solution)/shard_map/ppermute | solution.py:259
  51.1 4.6 %collective-permute-start.1 = (bf16[4,4,16,512]{3,2,1,0:T(8,128)(2,1)S(1)}, bf16[4,4,16,512]{3,2,1,0:T(8,128)(2,1)S(1)}, u32[]{:S(2)}, u32[]{:S(2)}) collective-permute-start(bf16[4,4,16,512]{3,2,1,0:T(8,128)(2,1)S(1)} %all_to_all.39.refs_0_), channel_id=1, source_target_pairs={{0,16},{8,24},{16,0},{24,8},{1,17},{9,25},{17,1},{25,9},{2,18},{10... | collective-permute-start | bytes 786440 | tf_op jit(solution)/shard_map/ppermute | solution.py:259
  55.7 3.3 %collective-permute-start.2 = (bf16[4,4,16,512]{3,2,1,0:T(8,128)(2,1)S(1)}, bf16[4,4,16,512]{3,2,1,0:T(8,128)(2,1)S(1)}, u32[]{:S(2)}, u32[]{:S(2)}) collective-permute-start(bf16[4,4,16,512]{3,2,1,0:T(8,128)(2,1)S(1)} %all_to_all.39.refs_0_), channel_id=1, source_target_pairs={{0,24},{8,0},{16,8},{24,16},{1,25},{9,1},{17,9},{25,17},{2,26},{10... | collective-permute-start | bytes 786440 | tf_op jit(solution)/shard_map/ppermute | solution.py:259
  60.0 5.6 %shard_map.95 = (f32[4,4,4,16,512]{4,3,2,1,0:T(8,128)}, f32[8,128]{1,0:T(8,128)}) custom-call(bf16[8,144,1024]{2,1,0:T(8,128)(2,1)} %bitcast.17, bf16[1024,512]{1,0:T(8,128)(2,1)} %refs_5_.1, f32[1,512]{1,0:T(1,128)} %bitcast.13), custom_call_target="tpu_custom_call" | custom-call | tf_op jit(solution)/shard_map/pallas_call | solution.py:31
  66.3 5.8 %shard_map.96 = (f32[1024,512]{1,0:T(8,128)}, f32[8,8,128]{2,1,0:T(8,128)}, f32[1,512]{1,0:T(1,128)S(1)}) custom-call(s32[1]{0:T(128)} %bitcast.4.me_ref, bf16[8,144,1024]{2,1,0:T(8,128)(2,1)} %bitcast.18, bf16[1024,512]{1,0:T(8,128)(2,1)} %refs_5_.1, bf16[1024,512]{1,0:T(8,128)(2,1)} %grad_ref.1, f32[1,512]{1,0:T(1,128)S(1)} %bitcast.14, ...), custom_call_target="tpu_custom_call" | custom-call | flops 4000000000 | bytes 10000000 | tf_op jit(solution)/shard_map/pallas_call | solution.py:31
  72.1 4.4 %all-to-all-start.2 = ((f32[8,8,128]{2,1,0:T(8,128)}), f32[8,8,128]{2,1,0:T(8,128)S(1)}, u32[]{:S(2)}, u32[]{:S(2)}) async-start(f32[8,8,128]{2,1,0:T(8,128)} %get-tuple-element.28), calls=%async_computation.3 | async-start | bytes 65536 | tf_op jit(solution)/shard_map/all_to_all | solution.py:333
  76.5 1.7 %shard_map.97 = (s32[8,1024]{1,0:T(8,128)}, f32[8,1024]{1,0:T(8,128)}) custom-call(s32[2,1024]{1,0:T(2,128)} %bitcast.20, f32[2,1024]{1,0:T(2,128)} %bitcast.21), custom_call_target="tpu_custom_call" | custom-call | tf_op jit(solution)/shard_map/pallas_call | solution.py:31
  78.2 3.8 %all-to-all-done.2.refs_1_ = f32[8,8,128]{2,1,0:T(8,128)S(1)} async-done(((f32[8,8,128]{2,1,0:T(8,128)}), f32[8,8,128]{2,1,0:T(8,128)S(1)}, u32[]{:S(2)}, u32[]{:S(2)}) %all-to-all-start.2) | async-done | bytes 32800 | tf_op jit(solution)/shard_map/all_to_all | solution.py:333
  82.6 6.9 %shard_map.98 = bf16[8,320,512]{2,1,0:T(8,128)(2,1)} custom-call(f32[8,128]{1,0:T(8,128)} %get-tuple-element.26.inverse_ref.refs_0_, f32[8,8,128]{2,1,0:T(8,128)} %copy-done.3, s32[8,1024]{1,0:T(8,128)} %get-tuple-element.29.refs_2_, f32[8,1024]{1,0:T(8,128)} %get-tuple-element.30.refs_3_, f32[1024,512]{1,0:T(8,128)} %get-tuple-element.31.refs_4_, ...), custom_call_target="tpu_custom_call" | custom-call | flops 20000000000 | bytes 10000000 | tf_op jit(solution)/shard_map/pallas_call | solution.py:31
  89.5 3.6 %all-to-all-start.4 = ((bf16[8,320,512]{2,1,0:T(8,128)(2,1)}), bf16[8,320,512]{2,1,0:T(8,128)(2,1)S(1)}, u32[]{:S(2)}, u32[]{:S(2)}) async-start(bf16[8,320,512]{2,1,0:T(8,128)(2,1)} %shard_map.98), calls=%async_computation.5 | async-start | bytes 5242880 | tf_op jit(solution)/shard_map/all_to_all | solution.py:345
  93.1 10.2 %psum.7.d_gain_ref = f32[1,512]{1,0:T(1,128)S(1)} all-reduce(f32[1,512]{1,0:T(1,128)S(1)} %get-tuple-element.33), channel_id=1, replica_groups=mesh['zh'=4,'zl'=4,'x'=4,'y'=4,'core'=2] {'x'}, use_global_device_ids=true, to_apply=%region_1.0 | all-reduce | flops 512 | bytes 4096 | tf_op jit(solution)/shard_map/psum | solution.py:347
  103.4 1.0 copy-done
  104.4 2.3 %collective-permute-start.3 = (bf16[80,512]{1,0:T(8,128)(2,1)S(1)}, bf16[80,512]{1,0:T(8,128)(2,1)S(1)}, u32[]{:S(2)}, u32[]{:S(2)}) collective-permute-start(bf16[80,512]{1,0:T(8,128)(2,1)S(1)} %get-tuple-element.35), channel_id=1, source_target_pairs={{0,32},{32,64},{64,96},{96,0},{1,33},{33,65},{65,97},{97,1},{2,34}... | collective-permute-start | bytes 245768 | tf_op jit(solution)/shard_map/ppermute | solution.py:259
  106.7 4.7 %collective-permute-start.4 = (bf16[80,512]{1,0:T(8,128)(2,1)S(1)}, bf16[80,512]{1,0:T(8,128)(2,1)S(1)}, u32[]{:S(2)}, u32[]{:S(2)}) collective-permute-start(bf16[80,512]{1,0:T(8,128)(2,1)S(1)} %get-tuple-element.36), channel_id=1, source_target_pairs={{0,64},{32,96},{64,0},{96,32},{1,65},{33,97},{65,1},{97,33},{2,66}... | collective-permute-start | bytes 245768 | tf_op jit(solution)/shard_map/ppermute | solution.py:259
  111.4 2.2 %collective-permute-start.5 = (bf16[80,512]{1,0:T(8,128)(2,1)S(1)}, bf16[80,512]{1,0:T(8,128)(2,1)S(1)}, u32[]{:S(2)}, u32[]{:S(2)}) collective-permute-start(bf16[80,512]{1,0:T(8,128)(2,1)S(1)} %get-tuple-element.37), channel_id=1, source_target_pairs={{0,96},{32,0},{64,32},{96,64},{1,97},{33,1},{65,33},{97,65},{2,98}... | collective-permute-start | bytes 245768 | tf_op jit(solution)/shard_map/ppermute | solution.py:259
  113.7 1.2 collective-permute-done.4.c_ref
  114.9 2.9 %collective-permute-done.5.d_ref = bf16[80,512]{1,0:T(8,128)(2,1)S(1)} collective-permute-done((bf16[80,512]{1,0:T(8,128)(2,1)S(1)}, bf16[80,512]{1,0:T(8,128)(2,1)S(1)}, u32[]{:S(2)}, u32[]{:S(2)}) %collective-permute-start.5) | collective-permute-done | bytes 81952 | tf_op jit(solution)/shard_map/ppermute | solution.py:259
  118.5 7.4 %all-to-all-done.4 = bf16[8,320,512]{2,1,0:T(8,128)(2,1)S(1)} async-done(((bf16[8,320,512]{2,1,0:T(8,128)(2,1)}), bf16[8,320,512]{2,1,0:T(8,128)(2,1)S(1)}, u32[]{:S(2)}, u32[]{:S(2)}) %all-to-all-start.4) | async-done | bytes 2621472 | tf_op jit(solution)/shard_map/all_to_all | solution.py:345
  125.8 3.4 %all-to-all-start.3 = ((f32[4,24,512]{2,1,0:T(8,128)}), f32[4,24,512]{2,1,0:T(8,128)S(1)}, u32[]{:S(2)}, u32[]{:S(2)}) async-start(f32[4,24,512]{2,1,0:T(8,128)} %shard_map.100), calls=%async_computation.4 | async-start | bytes 393216 | tf_op jit(solution)/shard_map/all_to_all | solution.py:357
  129.2 1.9 %copy.11 = bf16[1,8,40,8,512]{4,3,1,2,0:T(8,128)(2,1)} copy(bf16[1,8,40,8,512]{4,3,2,1,0:T(8,128)(2,1)S(1)} %bitcast.15) | data formatting | bytes 5242880 | tf_op jit(solution)/shard_map/all_to_all | solution.py:345
  131.1 16.5 %all-to-all-done.3.refs_0_ = f32[4,24,512]{2,1,0:T(8,128)S(1)} async-done(((f32[4,24,512]{2,1,0:T(8,128)}), f32[4,24,512]{2,1,0:T(8,128)S(1)}, u32[]{:S(2)}, u32[]{:S(2)}) %all-to-all-start.3) | async-done | bytes 196640 | tf_op jit(solution)/shard_map/all_to_all | solution.py:357
  (21 shorter events, 3.7 us)
Async XLA Ops:
  7.2 52.8 %all-gather.3.cloned.1.call-start = ((), (), s32[]{:S(2)}) async-start(), calls=%async_computation.7 | async-start | bytes 2654208 | tf_op jit(solution)/shard_map/all_gather | solution.py:280
  9.6 93.7 %reduce-scatter.2.cloned.1.call-start = ((), (), s32[]{:S(2)}) async-start(), calls=%async_computation.6 | async-start | bytes 2621440 | tf_op jit(solution)/shard_map/reduce_scatter | solution.py:306
  47.7 12.3 %collective-permute-start = (bf16[4,4,16,512]{3,2,1,0:T(8,128)(2,1)S(1)}, bf16[4,4,16,512]{3,2,1,0:T(8,128)(2,1)S(1)}, u32[]{:S(2)}, u32[]{:S(2)}) collective-permute-start(bf16[4,4,16,512]{3,2,1,0:T(8,128)(2,1)S(1)} %all_to_all.39.refs_0_), channel_id=1, source_target_pairs={{0,8},{8,16},{16,24},{24,0},{1,9},{9,17},{17,25},{25,1},{2,10},{10... | collective-permute-start | bytes 786440 | tf_op jit(solution)/shard_map/ppermute | solution.py:259
  51.1 14.5 %collective-permute-start.1 = (bf16[4,4,16,512]{3,2,1,0:T(8,128)(2,1)S(1)}, bf16[4,4,16,512]{3,2,1,0:T(8,128)(2,1)S(1)}, u32[]{:S(2)}, u32[]{:S(2)}) collective-permute-start(bf16[4,4,16,512]{3,2,1,0:T(8,128)(2,1)S(1)} %all_to_all.39.refs_0_), channel_id=1, source_target_pairs={{0,16},{8,24},{16,0},{24,8},{1,17},{9,25},{17,1},{25,9},{2,18},{10... | collective-permute-start | bytes 786440 | tf_op jit(solution)/shard_map/ppermute | solution.py:259
  55.7 9.8 %collective-permute-start.2 = (bf16[4,4,16,512]{3,2,1,0:T(8,128)(2,1)S(1)}, bf16[4,4,16,512]{3,2,1,0:T(8,128)(2,1)S(1)}, u32[]{:S(2)}, u32[]{:S(2)}) collective-permute-start(bf16[4,4,16,512]{3,2,1,0:T(8,128)(2,1)S(1)} %all_to_all.39.refs_0_), channel_id=1, source_target_pairs={{0,24},{8,0},{16,8},{24,16},{1,25},{9,1},{17,9},{25,17},{2,26},{10... | collective-permute-start | bytes 786440 | tf_op jit(solution)/shard_map/ppermute | solution.py:259
  60.0 5.6 %copy-start.1 = (f32[512]{0:T(512)S(1)}, f32[512]{0:T(512)}, u32[]{:S(2)}) copy-start(f32[512]{0:T(512)} %param.10) | copy-start | bytes 6148
  65.6 0.7 copy-start.2
  72.1 9.9 %all-to-all-start.2 = ((f32[8,8,128]{2,1,0:T(8,128)}), f32[8,8,128]{2,1,0:T(8,128)S(1)}, u32[]{:S(2)}, u32[]{:S(2)}) async-start(f32[8,8,128]{2,1,0:T(8,128)} %get-tuple-element.28), calls=%async_computation.3 | async-start | bytes 65536 | tf_op jit(solution)/shard_map/all_to_all | solution.py:333
  82.0 0.6 copy-start.3
  89.5 36.4 %all-to-all-start.4 = ((bf16[8,320,512]{2,1,0:T(8,128)(2,1)}), bf16[8,320,512]{2,1,0:T(8,128)(2,1)S(1)}, u32[]{:S(2)}, u32[]{:S(2)}) async-start(bf16[8,320,512]{2,1,0:T(8,128)(2,1)} %shard_map.98), calls=%async_computation.5 | async-start | bytes 5242880 | tf_op jit(solution)/shard_map/all_to_all | solution.py:345
  103.4 1.0 copy-start
  104.4 9.2 %collective-permute-start.3 = (bf16[80,512]{1,0:T(8,128)(2,1)S(1)}, bf16[80,512]{1,0:T(8,128)(2,1)S(1)}, u32[]{:S(2)}, u32[]{:S(2)}) collective-permute-start(bf16[80,512]{1,0:T(8,128)(2,1)S(1)} %get-tuple-element.35), channel_id=1, source_target_pairs={{0,32},{32,64},{64,96},{96,0},{1,33},{33,65},{65,97},{97,1},{2,34}... | collective-permute-start | bytes 245768 | tf_op jit(solution)/shard_map/ppermute | solution.py:259
  106.7 8.2 %collective-permute-start.4 = (bf16[80,512]{1,0:T(8,128)(2,1)S(1)}, bf16[80,512]{1,0:T(8,128)(2,1)S(1)}, u32[]{:S(2)}, u32[]{:S(2)}) collective-permute-start(bf16[80,512]{1,0:T(8,128)(2,1)S(1)} %get-tuple-element.36), channel_id=1, source_target_pairs={{0,64},{32,96},{64,0},{96,32},{1,65},{33,97},{65,1},{97,33},{2,66}... | collective-permute-start | bytes 245768 | tf_op jit(solution)/shard_map/ppermute | solution.py:259
  111.4 6.3 %collective-permute-start.5 = (bf16[80,512]{1,0:T(8,128)(2,1)S(1)}, bf16[80,512]{1,0:T(8,128)(2,1)S(1)}, u32[]{:S(2)}, u32[]{:S(2)}) collective-permute-start(bf16[80,512]{1,0:T(8,128)(2,1)S(1)} %get-tuple-element.37), channel_id=1, source_target_pairs={{0,96},{32,0},{64,32},{96,64},{1,97},{33,1},{65,33},{97,65},{2,98}... | collective-permute-start | bytes 245768 | tf_op jit(solution)/shard_map/ppermute | solution.py:259
  125.8 21.8 %all-to-all-start.3 = ((f32[4,24,512]{2,1,0:T(8,128)}), f32[4,24,512]{2,1,0:T(8,128)S(1)}, u32[]{:S(2)}, u32[]{:S(2)}) async-start(f32[4,24,512]{2,1,0:T(8,128)} %shard_map.100), calls=%async_computation.4 | async-start | bytes 393216 | tf_op jit(solution)/shard_map/all_to_all | solution.py:357
Sparse Core Ops, SparseCore 0:
  10.7 37.4 all-gather.2
  65.7 28.7 reduce-scatter.1

commit v7 on v6

--- a/solution.py
+++ b/solution.py
@@ -8,6 +8,7 @@
 epsilon = 1e-05
 EXPERT = ("y", "core")
 ANY = pl.BlockSpec(memory_space=pl.ANY)
+HBM = pl.BlockSpec(memory_space=pltpu.HBM)
 SMEM = pl.BlockSpec(memory_space=pltpu.SMEM)
 PAD = 16
 VALUE_LIMIT = 62
@@ -141,15 +142,17 @@
 
 
 def normed_kernel(
-    me_ref, value_ref, input_ref, grad_ref, gain_ref, inverse_ref, *refs
+    me_ref, value_ref, input_ref, grad_ref, gain_ref, given_ref, *refs
 ):
-    parts, (base_ref, inner_ref, d_gain_ref, weight_ref, sems) = refs[:-5], refs[-5:]
+    parts = refs[:-7]
+    base_ref, inner_ref, d_gain_ref, inverse_ref, weight_ref, sems, sem = refs[-7:]
     step = pl.program_id(0)
 
     @pl.when(step == 0)
     def _():
         xs, zl = len(parts), parts[0].shape[0]
-        gets = []
+        gets = [pltpu.make_async_copy(given_ref, inverse_ref, sem)]
+        gets[0].start()
         for x_step, part in enumerate(parts):
             x = lax.rem(me_ref[0] + (xs - x_step), xs)
             for low in range(zl):
@@ -218,7 +221,11 @@
         out_ref[at] = (gates * picked).astype(jnp.bfloat16)
 
 
-def low_split_kernel(me_ref, d_value_ref, d_gain_ref, *outs):
+def low_split_kernel(me_ref, given_ref, d_gain_ref, *refs):
+    outs, (d_value_ref, sem) = refs[:-2], refs[-2:]
+    get = pltpu.make_async_copy(given_ref, d_value_ref, sem)
+    get.start()
+    get.wait()
     count = len(outs)
     rows = d_value_ref.shape[0] // count
     behind = pieces(d_gain_ref[...])
@@ -232,19 +239,36 @@
     total = a_ref[...].astype(jnp.float32)
     for ref in (b_ref, c_ref, d_ref):
         total += ref[...].astype(jnp.float32)
+    count, own, _ = out_ref.shape
+    columns = total.shape[1]
     rows = total.shape[0] - PAD
     gain = jnp.sum(total[rows:, :], axis=0, keepdims=True)
-    own = rows // out_ref.shape[0]
-    for at in range(out_ref.shape[0]):
-        out_ref[at, 0:own, :] = total[at * own : (at + 1) * own, :]
-        out_ref[at, own:, :] = jnp.broadcast_to(gain, (8, gain.shape[1]))
+    parts = pieces(gain).astype(jnp.float32)
+    blocks = columns // 128
+    at = lax.broadcasted_iota(jnp.int32, (own, 128), 0)
+    behind = jnp.zeros((own, 128), jnp.float32)
+    for part in range(3):
+        for block in range(blocks):
+            row = parts[part : part + 1, block * 128 : (block + 1) * 128]
+            behind = jnp.where(at == part * blocks + block, row, behind)
+    for to in range(count):
+        out_ref[to, :, 0:columns] = total[to * own : (to + 1) * own, :].astype(jnp.bfloat16)
+        out_ref[to, :, columns:] = behind.astype(jnp.bfloat16)
 
 
 def finish_kernel(rescale, parts_ref, d_value_ref, d_gain_ref):
-    total = jnp.sum(parts_ref[...], axis=0)
-    rows = d_value_ref.shape[0]
-    d_value_ref[...] = (total[0:rows, :] * rescale).astype(jnp.bfloat16)
-    d_gain_ref[...] = total[rows : rows + 1, :] * rescale
+    total = parts_ref[0].astype(jnp.float32)
+    for at in range(1, parts_ref.shape[0]):
+        total += parts_ref[at].astype(jnp.float32)
+    columns = d_value_ref.shape[1]
+    d_value_ref[...] = (total[:, 0:columns] * rescale).astype(jnp.bfloat16)
+    blocks = columns // 128
+    for block in range(blocks):
+        gain = total[block : block + 1, columns:]
+        for part in (1, 2):
+            row = part * blocks + block
+            gain += total[row : row + 1, columns:]
+        d_gain_ref[:, block * 128 : (block + 1) * 128] = gain * rescale
 
 
 def to_all(part, axis):
@@ -307,26 +331,28 @@
         d_value.reshape(features, columns), "x", scatter_dimension=0, tiled=True
     )
 
-    two = pl.BlockSpec((2 * own_rows, columns), lambda i: (i, 0))
+    half = pl.BlockSpec((group // 2, columns), lambda i: (i, 0))
     base, inner, own_gain = call(
         normed_kernel, lax.axis_index("x").reshape(1), gathered, attn_input, stream_grad,
         gain_row, inverse, *weights,
         out=[((group, columns), f32), ((experts, 8, group // 8), f32), ((1, columns), f32)],
         in_specs=[
             SMEM,
-            pl.BlockSpec((2, own_rows, features), lambda i: (i, 0, 0)),
-            two,
-            two,
+            pl.BlockSpec((experts // 2, own_rows, features), lambda i: (i, 0, 0)),
+            half,
+            half,
             whole((1, columns)),
-            whole((8, group // 8)),
+            HBM,
         ]
         + [ANY] * xs,
-        out_specs=[two, whole((experts, 8, group // 8)), whole((1, columns))],
+        out_specs=[half, whole((experts, 8, group // 8)), whole((1, columns))],
         scratch=[
+            pltpu.VMEM((8, group // 8), f32),
             pltpu.VMEM((zh, zl, xs, rows, columns), bf16),
             pltpu.SemaphoreType.DMA((xs, zl)),
+            pltpu.SemaphoreType.DMA(()),
         ],
-        grid=experts // 2,
+        grid=2,
         limit=NORMED_LIMIT,
         flops=NORMED_FLOPS,
     )
@@ -349,10 +375,12 @@
     parts = call(
         low_split_kernel, lax.axis_index("zl").reshape(1), d_value, d_gain,
         out=[(part, bf16)] * zl, limit=8,
+        in_specs=[SMEM, HBM, whole((1, columns))],
+        scratch=[pltpu.VMEM((features // xs, columns), f32), pltpu.SemaphoreType.DMA(())],
     )
     parts = [parts[0]] + [further(parts[k], "zl", k) for k in range(1, zl)]
     (parts,) = call(
-        high_split_kernel, *parts, out=[((zh, rows + 8, columns), f32)], limit=8,
+        high_split_kernel, *parts, out=[((zh, rows, columns + 128), bf16)], limit=8,
     )
     parts = lax.all_to_all(parts, "zh", 0, 0, tiled=True)
     d_value, d_gain = call(

time: 156 us -> 151 us (0.968)
  the two profiles are of different devices: /device:TPU:32 before, /device:TPU:1 now
where the time goes in v7:
time: 151 us; the launch traced here: 150 us
  blocking collectives  45.9 us (30%)
  starting transfers between devices  35.4 us (23%)
  waiting for transfers between devices  27.1 us (18%)
  Pallas kernels  22.9 us (15%)
  between operations  14.2 us (9%)
  local copies, waits for them, and re-layouts  4.21 us (3%)
    all_to_all x1, blocking collectives, on_device(): weight = to_all(lax.all_to_all(copies, 'zh', 0, 0, tiled=True), 'zl')  28.1 us
    pallas_call x8, Pallas kernels, call(): pl.pallas_call(kernel, grid=(grid,), in_specs=in_specs or [SMEM if o.shap...  22.9 us
    ppermute x6, starting transfers between devices, further(): lax.ppermute(part, axis, [(i, (i + step) % size) for i in range(size)])  19.5 us
    all_to_all x1, waiting for transfers between devices, on_device(): parts = lax.all_to_all(parts, 'zh', 0, 0, tiled=True)  10.5 us
    all_to_all x1, blocking collectives, to_all(): lax.all_to_all(jnp.broadcast_to(part[None], (size,) + part.shape), axis,...  9.11 us
    all_to_all x1, waiting for transfers between devices, on_device(): lax.all_to_all(sent, EXPERT, split_axis=0, concat_axis=2, tiled=True)  9.06 us
    psum x1, blocking collectives, on_device(): d_gain = lax.psum(own_gain, 'x')  8.62 us
    all_to_all x1, starting transfers between devices, on_device(): inner = lax.all_to_all(inner, EXPERT, 0, 0, tiled=True)  8.31 us
  transfers between devices with their start and end apart: 11, of which 6 were waited for; matrix products, arithmetic and copies ran while one was open for 1% of the time, Pallas kernels for 13%

profile of v7, /device:TPU:1, one launch (start us, length us, event | category | flops | bytes accessed | tf_op | source)
XLA Modules:
  0.0 149.6 jit_solution(9093270763619739458)
XLA Ops:
  7.2 2.4 %shard_map.94 = (bf16[144,1024]{1,0:T(8,128)(2,1)}, bf16[4,16,512]{2,1,0:T(8,128)(2,1)}) custom-call(bf16[128,1024]{1,0:T(8,128)(2,1)} %value_ref.1, bf16[1024,512]{1,0:T(8,128)(2,1)} %refs_5_.1, bf16[16,512]{1,0:T(8,128)(2,1)} %weight_ref.1), custom_call_target="tpu_custom_call" | custom-call | tf_op jit(solution)/shard_map/pallas_call | solution.py:32
  9.7 28.1 %all_to_all.38 = bf16[4,16,512]{2,1,0:T(8,128)(2,1)S(1)} all-to-all(bf16[4,16,512]{2,1,0:T(8,128)(2,1)} %get-tuple-element.23), channel_id=1, replica_groups=mesh['zh'=4,'zl'=4,'x'=4,'y'=4,'core'=2] {'zh'}, dimensions={0} | all-to-all | bytes 131072 | tf_op jit(solution)/shard_map/all_to_all | solution.py:306
  37.8 9.1 %all_to_all.39.refs_0_ = bf16[4,4,16,512]{3,2,1,0:T(8,128)(2,1)S(1)} all-to-all(bf16[4,4,16,512]{3,2,1,0:T(8,128)(2,1)S(1)} %broadcast_in_dim.4), channel_id=1, replica_groups=mesh['zh'=4,'zl'=4,'x'=4,'y'=4,'core'=2] {'zl'}, dimensions={0} | all-to-all | bytes 524288 | tf_op jit(solution)/shard_map/all_to_all | solution.py:276
  46.9 3.1 %collective-permute-start = (bf16[4,4,16,512]{3,2,1,0:T(8,128)(2,1)S(1)}, bf16[4,4,16,512]{3,2,1,0:T(8,128)(2,1)S(1)}, u32[]{:S(2)}, u32[]{:S(2)}) collective-permute-start(bf16[4,4,16,512]{3,2,1,0:T(8,128)(2,1)S(1)} %all_to_all.39.refs_0_), channel_id=1, source_target_pairs={{0,8},{8,16},{16,24},{24,0},{1,9},{9,17},{17,25},{25,1},{2,10},{10... | collective-permute-start | bytes 786440 | tf_op jit(solution)/shard_map/ppermute | solution.py:283
  50.1 4.3 %collective-permute-start.1 = (bf16[4,4,16,512]{3,2,1,0:T(8,128)(2,1)S(1)}, bf16[4,4,16,512]{3,2,1,0:T(8,128)(2,1)S(1)}, u32[]{:S(2)}, u32[]{:S(2)}) collective-permute-start(bf16[4,4,16,512]{3,2,1,0:T(8,128)(2,1)S(1)} %all_to_all.39.refs_0_), channel_id=1, source_target_pairs={{0,16},{8,24},{16,0},{24,8},{1,17},{9,25},{17,1},{25,9},{2,18},{10... | collective-permute-start | bytes 786440 | tf_op jit(solution)/shard_map/ppermute | solution.py:283
  54.4 3.1 %collective-permute-start.2 = (bf16[4,4,16,512]{3,2,1,0:T(8,128)(2,1)S(1)}, bf16[4,4,16,512]{3,2,1,0:T(8,128)(2,1)S(1)}, u32[]{:S(2)}, u32[]{:S(2)}) collective-permute-start(bf16[4,4,16,512]{3,2,1,0:T(8,128)(2,1)S(1)} %all_to_all.39.refs_0_), channel_id=1, source_target_pairs={{0,24},{8,0},{16,8},{24,16},{1,25},{9,1},{17,9},{25,17},{2,26},{10... | collective-permute-start | bytes 786440 | tf_op jit(solution)/shard_map/ppermute | solution.py:283
  57.6 5.6 %shard_map.95 = (f32[4,4,4,16,512]{4,3,2,1,0:T(8,128)}, f32[8,128]{1,0:T(8,128)}) custom-call(bf16[8,144,1024]{2,1,0:T(8,128)(2,1)} %bitcast.17, bf16[1024,512]{1,0:T(8,128)(2,1)} %refs_5_.1, f32[1,512]{1,0:T(1,128)} %bitcast.13), custom_call_target="tpu_custom_call" | custom-call | tf_op jit(solution)/shard_map/pallas_call | solution.py:32
  63.2 0.9 collective-permute-done.2.refs_3_
  64.8 5.0 %shard_map.96 = (f32[1024,512]{1,0:T(8,128)}, f32[8,8,128]{2,1,0:T(8,128)}, f32[1,512]{1,0:T(1,128)S(1)}) custom-call(s32[1]{0:T(128)} %bitcast.4.me_ref, bf16[8,144,1024]{2,1,0:T(8,128)(2,1)} %bitcast.18, bf16[1024,512]{1,0:T(8,128)(2,1)} %refs_5_.1, bf16[1024,512]{1,0:T(8,128)(2,1)} %grad_ref.1, f32[1,512]{1,0:T(1,128)S(1)} %bitcast.14, ...), custom_call_target="tpu_custom_call" | custom-call | flops 4000000000 | bytes 10000000 | tf_op jit(solution)/shard_map/pallas_call | solution.py:32
  69.8 8.3 %all-to-all-start.2 = ((f32[8,8,128]{2,1,0:T(8,128)}), f32[8,8,128]{2,1,0:T(8,128)S(1)}, u32[]{:S(2)}, u32[]{:S(2)}) async-start(f32[8,8,128]{2,1,0:T(8,128)} %get-tuple-element.28), calls=%async_computation.3 | async-start | bytes 65536 | tf_op jit(solution)/shard_map/all_to_all | solution.py:359
  78.1 1.7 %shard_map.97 = (s32[8,1024]{1,0:T(8,128)}, f32[8,1024]{1,0:T(8,128)}) custom-call(s32[2,1024]{1,0:T(2,128)} %bitcast.20, f32[2,1024]{1,0:T(2,128)} %bitcast.21), custom_call_target="tpu_custom_call" | custom-call | tf_op jit(solution)/shard_map/pallas_call | solution.py:32
  79.7 3.1 %all-to-all-done.2.refs_1_ = f32[8,8,128]{2,1,0:T(8,128)S(1)} async-done(((f32[8,8,128]{2,1,0:T(8,128)}), f32[8,8,128]{2,1,0:T(8,128)S(1)}, u32[]{:S(2)}, u32[]{:S(2)}) %all-to-all-start.2) | async-done | bytes 32800 | tf_op jit(solution)/shard_map/all_to_all | solution.py:359
  83.5 6.9 %shard_map.98 = bf16[8,320,512]{2,1,0:T(8,128)(2,1)} custom-call(f32[8,128]{1,0:T(8,128)} %get-tuple-element.26.given_ref.refs_0_, f32[8,8,128]{2,1,0:T(8,128)} %copy-done.3, s32[8,1024]{1,0:T(8,128)} %get-tuple-element.29.refs_2_, f32[8,1024]{1,0:T(8,128)} %get-tuple-element.30.refs_3_, f32[1024,512]{1,0:T(8,128)} %get-tuple-element.31.refs_4_, ...), custom_call_target="tpu_custom_call" | custom-call | flops 20000000000 | bytes 10000000 | tf_op jit(solution)/shard_map/pallas_call | solution.py:32
  90.4 4.2 %all-to-all-start.4 = ((bf16[8,320,512]{2,1,0:T(8,128)(2,1)}), bf16[8,320,512]{2,1,0:T(8,128)(2,1)S(1)}, u32[]{:S(2)}, u32[]{:S(2)}) async-start(bf16[8,320,512]{2,1,0:T(8,128)(2,1)} %shard_map.98), calls=%async_computation.5 | async-start | bytes 5242880 | tf_op jit(solution)/shard_map/all_to_all | solution.py:371
  94.6 8.6 %psum.7.d_gain_ref = f32[1,512]{1,0:T(1,128)S(1)} all-reduce(f32[1,512]{1,0:T(1,128)S(1)} %get-tuple-element.33), channel_id=1, replica_groups=mesh['zh'=4,'zl'=4,'x'=4,'y'=4,'core'=2] {'x'}, use_global_device_ids=true, to_apply=%region_1.0 | all-reduce | flops 512 | bytes 4096 | tf_op jit(solution)/shard_map/psum | solution.py:373
  103.2 1.0 copy-done
  104.3 2.8 %collective-permute-start.3 = (bf16[80,512]{1,0:T(8,128)(2,1)S(1)}, bf16[80,512]{1,0:T(8,128)(2,1)S(1)}, u32[]{:S(2)}, u32[]{:S(2)}) collective-permute-start(bf16[80,512]{1,0:T(8,128)(2,1)S(1)} %get-tuple-element.35), channel_id=1, source_target_pairs={{0,32},{32,64},{64,96},{96,0},{1,33},{33,65},{65,97},{97,1},{2,34}... | collective-permute-start | bytes 245768 | tf_op jit(solution)/shard_map/ppermute | solution.py:283
  107.1 3.2 %collective-permute-start.4 = (bf16[80,512]{1,0:T(8,128)(2,1)S(1)}, bf16[80,512]{1,0:T(8,128)(2,1)S(1)}, u32[]{:S(2)}, u32[]{:S(2)}) collective-permute-start(bf16[80,512]{1,0:T(8,128)(2,1)S(1)} %get-tuple-element.36), channel_id=1, source_target_pairs={{0,64},{32,96},{64,0},{96,32},{1,65},{33,97},{65,1},{97,33},{2,66}... | collective-permute-start | bytes 245768 | tf_op jit(solution)/shard_map/ppermute | solution.py:283
  110.3 3.0 %collective-permute-start.5 = (bf16[80,512]{1,0:T(8,128)(2,1)S(1)}, bf16[80,512]{1,0:T(8,128)(2,1)S(1)}, u32[]{:S(2)}, u32[]{:S(2)}) collective-permute-start(bf16[80,512]{1,0:T(8,128)(2,1)S(1)} %get-tuple-element.37), channel_id=1, source_target_pairs={{0,96},{32,0},{64,32},{96,64},{1,97},{33,1},{65,33},{97,65},{2,98}... | collective-permute-start | bytes 245768 | tf_op jit(solution)/shard_map/ppermute | solution.py:283
  113.4 3.2 %collective-permute-done.4.c_ref = bf16[80,512]{1,0:T(8,128)(2,1)S(1)} collective-permute-done((bf16[80,512]{1,0:T(8,128)(2,1)S(1)}, bf16[80,512]{1,0:T(8,128)(2,1)S(1)}, u32[]{:S(2)}, u32[]{:S(2)}) %collective-permute-start.4) | collective-permute-done | bytes 81952 | tf_op jit(solution)/shard_map/ppermute | solution.py:283
  117.5 9.1 %all-to-all-done.4 = bf16[8,320,512]{2,1,0:T(8,128)(2,1)S(1)} async-done(((bf16[8,320,512]{2,1,0:T(8,128)(2,1)}), bf16[8,320,512]{2,1,0:T(8,128)(2,1)S(1)}, u32[]{:S(2)}, u32[]{:S(2)}) %all-to-all-start.4) | async-done | bytes 2621472 | tf_op jit(solution)/shard_map/all_to_all | solution.py:371
  126.5 3.3 %all-to-all-start.3 = ((bf16[4,16,640]{2,1,0:T(8,128)(2,1)}), bf16[4,16,640]{2,1,0:T(8,128)(2,1)S(1)}, u32[]{:S(2)}, u32[]{:S(2)}) async-start(bf16[4,16,640]{2,1,0:T(8,128)(2,1)} %shard_map.100), calls=%async_computation.4 | async-start | bytes 163840 | tf_op jit(solution)/shard_map/all_to_all | solution.py:385
  129.8 1.9 %copy.11 = bf16[1,8,40,8,512]{4,3,1,2,0:T(8,128)(2,1)} copy(bf16[1,8,40,8,512]{4,3,2,1,0:T(8,128)(2,1)S(1)} %bitcast.15) | data formatting | bytes 5242880 | tf_op jit(solution)/shard_map/all_to_all | solution.py:371
  131.7 10.5 %all-to-all-done.3.refs_0_ = bf16[4,16,640]{2,1,0:T(8,128)(2,1)S(1)} async-done(((bf16[4,16,640]{2,1,0:T(8,128)(2,1)}), bf16[4,16,640]{2,1,0:T(8,128)(2,1)S(1)}, u32[]{:S(2)}, u32[]{:S(2)}) %all-to-all-start.3) | async-done | bytes 81952 | tf_op jit(solution)/shard_map/all_to_all | solution.py:385
  (21 shorter events, 3.1 us)
Async XLA Ops:
  7.2 50.4 %all-gather.3.cloned.1.call-start = ((), (), s32[]{:S(2)}) async-start(), calls=%async_computation.7 | async-start | bytes 2654208 | tf_op jit(solution)/shard_map/all_gather | solution.py:304
  9.6 93.6 %reduce-scatter.2.cloned.1.call-start = ((), (), s32[]{:S(2)}) async-start(), calls=%async_computation.6 | async-start | bytes 2621440 | tf_op jit(solution)/shard_map/reduce_scatter | solution.py:330
  46.9 10.6 %collective-permute-start = (bf16[4,4,16,512]{3,2,1,0:T(8,128)(2,1)S(1)}, bf16[4,4,16,512]{3,2,1,0:T(8,128)(2,1)S(1)}, u32[]{:S(2)}, u32[]{:S(2)}) collective-permute-start(bf16[4,4,16,512]{3,2,1,0:T(8,128)(2,1)S(1)} %all_to_all.39.refs_0_), channel_id=1, source_target_pairs={{0,8},{8,16},{16,24},{24,0},{1,9},{9,17},{17,25},{25,1},{2,10},{10... | collective-permute-start | bytes 786440 | tf_op jit(solution)/shard_map/ppermute | solution.py:283
  50.1 13.1 %collective-permute-start.1 = (bf16[4,4,16,512]{3,2,1,0:T(8,128)(2,1)S(1)}, bf16[4,4,16,512]{3,2,1,0:T(8,128)(2,1)S(1)}, u32[]{:S(2)}, u32[]{:S(2)}) collective-permute-start(bf16[4,4,16,512]{3,2,1,0:T(8,128)(2,1)S(1)} %all_to_all.39.refs_0_), channel_id=1, source_target_pairs={{0,16},{8,24},{16,0},{24,8},{1,17},{9,25},{17,1},{25,9},{2,18},{10... | collective-permute-start | bytes 786440 | tf_op jit(solution)/shard_map/ppermute | solution.py:283
  54.4 9.7 %collective-permute-start.2 = (bf16[4,4,16,512]{3,2,1,0:T(8,128)(2,1)S(1)}, bf16[4,4,16,512]{3,2,1,0:T(8,128)(2,1)S(1)}, u32[]{:S(2)}, u32[]{:S(2)}) collective-permute-start(bf16[4,4,16,512]{3,2,1,0:T(8,128)(2,1)S(1)} %all_to_all.39.refs_0_), channel_id=1, source_target_pairs={{0,24},{8,0},{16,8},{24,16},{1,25},{9,1},{17,9},{25,17},{2,26},{10... | collective-permute-start | bytes 786440 | tf_op jit(solution)/shard_map/ppermute | solution.py:283
  57.5 6.5 %copy-start.1 = (f32[512]{0:T(512)S(1)}, f32[512]{0:T(512)}, u32[]{:S(2)}) copy-start(f32[512]{0:T(512)} %param.10) | copy-start | bytes 6148
  64.1 0.7 copy-start.2
  69.8 13.1 %all-to-all-start.2 = ((f32[8,8,128]{2,1,0:T(8,128)}), f32[8,8,128]{2,1,0:T(8,128)S(1)}, u32[]{:S(2)}, u32[]{:S(2)}) async-start(f32[8,8,128]{2,1,0:T(8,128)} %get-tuple-element.28), calls=%async_computation.3 | async-start | bytes 65536 | tf_op jit(solution)/shard_map/all_to_all | solution.py:359
  82.9 0.6 copy-start.3
  90.4 36.2 %all-to-all-start.4 = ((bf16[8,320,512]{2,1,0:T(8,128)(2,1)}), bf16[8,320,512]{2,1,0:T(8,128)(2,1)S(1)}, u32[]{:S(2)}, u32[]{:S(2)}) async-start(bf16[8,320,512]{2,1,0:T(8,128)(2,1)} %shard_map.98), calls=%async_computation.5 | async-start | bytes 5242880 | tf_op jit(solution)/shard_map/all_to_all | solution.py:371
  103.2 1.0 copy-start
  104.3 9.0 %collective-permute-start.3 = (bf16[80,512]{1,0:T(8,128)(2,1)S(1)}, bf16[80,512]{1,0:T(8,128)(2,1)S(1)}, u32[]{:S(2)}, u32[]{:S(2)}) collective-permute-start(bf16[80,512]{1,0:T(8,128)(2,1)S(1)} %get-tuple-element.35), channel_id=1, source_target_pairs={{0,32},{32,64},{64,96},{96,0},{1,33},{33,65},{65,97},{97,1},{2,34}... | collective-permute-start | bytes 245768 | tf_op jit(solution)/shard_map/ppermute | solution.py:283
  107.1 9.4 %collective-permute-start.4 = (bf16[80,512]{1,0:T(8,128)(2,1)S(1)}, bf16[80,512]{1,0:T(8,128)(2,1)S(1)}, u32[]{:S(2)}, u32[]{:S(2)}) collective-permute-start(bf16[80,512]{1,0:T(8,128)(2,1)S(1)} %get-tuple-element.36), channel_id=1, source_target_pairs={{0,64},{32,96},{64,0},{96,32},{1,65},{33,97},{65,1},{97,33},{2,66}... | collective-permute-start | bytes 245768 | tf_op jit(solution)/shard_map/ppermute | solution.py:283
  110.3 6.5 %collective-permute-start.5 = (bf16[80,512]{1,0:T(8,128)(2,1)S(1)}, bf16[80,512]{1,0:T(8,128)(2,1)S(1)}, u32[]{:S(2)}, u32[]{:S(2)}) collective-permute-start(bf16[80,512]{1,0:T(8,128)(2,1)S(1)} %get-tuple-element.37), channel_id=1, source_target_pairs={{0,96},{32,0},{64,32},{96,64},{1,97},{33,1},{65,33},{97,65},{2,98}... | collective-permute-start | bytes 245768 | tf_op jit(solution)/shard_map/ppermute | solution.py:283
  126.5 15.6 %all-to-all-start.3 = ((bf16[4,16,640]{2,1,0:T(8,128)(2,1)}), bf16[4,16,640]{2,1,0:T(8,128)(2,1)S(1)}, u32[]{:S(2)}, u32[]{:S(2)}) async-start(bf16[4,16,640]{2,1,0:T(8,128)(2,1)} %shard_map.100), calls=%async_computation.4 | async-start | bytes 163840 | tf_op jit(solution)/shard_map/all_to_all | solution.py:385
Sparse Core Ops, SparseCore 0:
  10.7 39.0 all-gather.2
  63.3 32.3 reduce-scatter.1

commit v8 on v7

--- a/solution.py
+++ b/solution.py
@@ -13,6 +13,7 @@
 PAD = 16
 VALUE_LIMIT = 62
 NORMED_LIMIT = 52
+DISPATCH_LIMIT = 52
 NORMED_FLOPS = 4 * 10**9
 DISPATCH_FLOPS = 20 * 10**9
 
@@ -188,29 +189,36 @@
 
 
 def dispatch_kernel(
-    width, inverse_ref, inner_ref, slot_ref, gate_ref, base_ref, input_ref, out_ref, stream_ref
+    width, inverse_ref, inner_ref, slot_ref, gate_ref, given_ref, input_ref, out_ref,
+    base_ref, stream_ref, rows_ref, sems, get_sems,
 ):
-    step = pl.program_id(0)
     group = input_ref.shape[0]
     experts, capacity, _ = out_ref.shape
-
-    @pl.when(step == 0)
-    def _():
-        inverse = inverse_ref[...]
-        inner = jnp.sum(inner_ref[...], axis=0) / width
-        factor = jnp.transpose(inner * inverse * inverse)
-        tile = group // 8
-        for at in range(8):
-            rows = pl.ds(at * tile, tile)
-            stream = (
-                base_ref[rows, :]
-                - input_ref[rows, :].astype(jnp.float32) * factor[:, at : at + 1]
-            )
-            stream_ref[rows, :] = stream.astype(jnp.bfloat16)
-
-    for at in range(experts):
-        slot = slot_ref[pl.ds(step * experts + at, 1), :]
-        gate = gate_ref[pl.ds(step * experts + at, 1), :]
+    quarter = group // 4
+    gets = []
+    for at in range(4):
+        rows = pl.ds(at * quarter, quarter)
+        get = pltpu.make_async_copy(given_ref.at[rows, :], base_ref.at[rows, :], get_sems.at[at])
+        get.start()
+        gets.append(get)
+    inverse = inverse_ref[...]
+    inner = jnp.sum(inner_ref[...], axis=0) / width
+    factor = jnp.transpose(inner * inverse * inverse)
+    tile = group // 8
+    for at in range(8):
+        rows = slice(at * tile, (at + 1) * tile)
+        if at % 2 == 0:
+            gets[at // 2].wait()
+        stream = (
+            base_ref[rows, :]
+            - input_ref[rows, :].astype(jnp.float32) * factor[:, at : at + 1]
+        )
+        stream_ref[rows, :] = stream.astype(jnp.bfloat16)
+
+    puts = []
+    for expert in range(experts):
+        slot = slot_ref[expert : expert + 1, :]
+        gate = gate_ref[expert : expert + 1, :]
         taken = lax.broadcasted_iota(jnp.int32, (capacity, group), 0) == slot
         gates = jnp.sum(jnp.where(taken, gate, 0.0), axis=1, keepdims=True)
         picked = jnp.dot(
@@ -218,7 +226,12 @@
             stream_ref[...],
             preferred_element_type=jnp.float32,
         )
-        out_ref[at] = (gates * picked).astype(jnp.bfloat16)
+        rows_ref[expert] = (gates * picked).astype(jnp.bfloat16)
+        put = pltpu.make_async_copy(rows_ref.at[expert], out_ref.at[expert], sems.at[expert])
+        put.start()
+        puts.append(put)
+    for put in puts:
+        put.wait()
 
 
 def low_split_kernel(me_ref, given_ref, d_gain_ref, *refs):
@@ -310,6 +323,7 @@
     slot, gate = call(
         route_kernel, routes.T, gate_logits.T,
         out=[((experts, group), jnp.int32), ((experts, group), f32)],
+        limit=24,
     )
 
     d_value, inverse = call(
@@ -362,9 +376,23 @@
         lambda *refs: dispatch_kernel(width, *refs),
         inverse, inner, slot, gate, base, attn_input,
         out=[((experts, capacity, columns), bf16)],
-        out_specs=[pl.BlockSpec((experts // 4, capacity, columns), lambda e: (e, 0, 0))],
-        scratch=[pltpu.VMEM((group, columns), bf16)],
-        grid=4,
+        in_specs=[
+            whole((8, group // 8)),
+            whole((experts, 8, group // 8)),
+            whole((experts, group)),
+            whole((experts, group)),
+            ANY,
+            whole((group, columns)),
+        ],
+        out_specs=[ANY],
+        scratch=[
+            pltpu.VMEM((group, columns), f32),
+            pltpu.VMEM((group, columns), bf16),
+            pltpu.VMEM((experts, capacity, columns), bf16),
+            pltpu.SemaphoreType.DMA((experts,)),
+            pltpu.SemaphoreType.DMA((4,)),
+        ],
+        limit=DISPATCH_LIMIT,
         flops=DISPATCH_FLOPS,
     )
     sent, own_gain = lax.optimization_barrier((sent, own_gain))

time: 151 us -> 150 us (level)
  Pallas kernels: 22.9 us -> 20.2 us
    pallas_call x8, Pallas kernels: 22.9 us -> 20.2 us  [call(): pl.pallas_call(kernel, grid=(grid,), in_specs=in_specs or [SMEM if o.shap...]
    all_to_all x1, local copies, waits for them, and re-layouts: 1.86 us -> 3.6 us  [on_device(): lax.all_to_all(sent, EXPERT, split_axis=0, concat_axis=2, tiled=True)]
    all_to_all x1, waiting for transfers between devices: 10.5 us -> 8.76 us  [on_device(): parts = lax.all_to_all(parts, 'zh', 0, 0, tiled=True)]
  transfers between devices with their start and end apart: 11 -> 11, of which waited for: 6 -> 6; matrix products, arithmetic and copies ran while one was open for 1% -> 2% of each run, Pallas kernels for 13% -> 12%
where the time goes in v8:
time: 150 us; the launch traced here: 149 us
  blocking collectives  46.1 us (31%)
  starting transfers between devices  36.2 us (24%)
  waiting for transfers between devices  26.6 us (18%)
  Pallas kernels  20.2 us (13%)
  between operations  14.2 us (9%)
  local copies, waits for them, and re-layouts  5.36 us (4%)
    all_to_all x1, blocking collectives, on_device(): weight = to_all(lax.all_to_all(copies, 'zh', 0, 0, tiled=True), 'zl')  28.1 us
    pallas_call x8, Pallas kernels, call(): pl.pallas_call(kernel, grid=(grid,), in_specs=in_specs or [SMEM if o.shap...  20.2 us
    ppermute x6, starting transfers between devices, further(): lax.ppermute(part, axis, [(i, (i + step) % size) for i in range(size)])  19.5 us
    all_to_all x1, blocking collectives, to_all(): lax.all_to_all(jnp.broadcast_to(part[None], (size,) + part.shape), axis,...  9.11 us
    psum x1, blocking collectives, on_device(): d_gain = lax.psum(own_gain, 'x')  8.86 us
    all_to_all x1, waiting for transfers between devices, on_device(): parts = lax.all_to_all(parts, 'zh', 0, 0, tiled=True)  8.76 us
    all_to_all x1, waiting for transfers between devices, on_device(): lax.all_to_all(sent, EXPERT, split_axis=0, concat_axis=2, tiled=True)  8.36 us
    all_to_all x1, starting transfers between devices, on_device(): inner = lax.all_to_all(inner, EXPERT, 0, 0, tiled=True)  8.25 us
  transfers between devices with their start and end apart: 11, of which 6 were waited for; matrix products, arithmetic and copies ran while one was open for 2% of the time, Pallas kernels for 12%

profile of v8, /device:TPU:1, one launch (start us, length us, event | category | flops | bytes accessed | tf_op | source)
XLA Modules:
  0.0 148.7 jit_solution(5175094770465730093)
XLA Ops:
  7.2 2.4 %shard_map.94 = (bf16[144,1024]{1,0:T(8,128)(2,1)}, bf16[4,16,512]{2,1,0:T(8,128)(2,1)}) custom-call(bf16[128,1024]{1,0:T(8,128)(2,1)} %value_ref.1, bf16[1024,512]{1,0:T(8,128)(2,1)} %refs_5_.1, bf16[16,512]{1,0:T(8,128)(2,1)} %weight_ref.1), custom_call_target="tpu_custom_call" | custom-call | tf_op jit(solution)/shard_map/pallas_call | solution.py:33
  9.7 28.1 %all_to_all.38 = bf16[4,16,512]{2,1,0:T(8,128)(2,1)S(1)} all-to-all(bf16[4,16,512]{2,1,0:T(8,128)(2,1)} %get-tuple-element.23), channel_id=1, replica_groups=mesh['zh'=4,'zl'=4,'x'=4,'y'=4,'core'=2] {'zh'}, dimensions={0} | all-to-all | bytes 131072 | tf_op jit(solution)/shard_map/all_to_all | solution.py:319
  37.8 9.1 %all_to_all.39.refs_0_ = bf16[4,4,16,512]{3,2,1,0:T(8,128)(2,1)S(1)} all-to-all(bf16[4,4,16,512]{3,2,1,0:T(8,128)(2,1)S(1)} %broadcast_in_dim.4), channel_id=1, replica_groups=mesh['zh'=4,'zl'=4,'x'=4,'y'=4,'core'=2] {'zl'}, dimensions={0} | all-to-all | bytes 524288 | tf_op jit(solution)/shard_map/all_to_all | solution.py:289
  46.9 3.1 %collective-permute-start = (bf16[4,4,16,512]{3,2,1,0:T(8,128)(2,1)S(1)}, bf16[4,4,16,512]{3,2,1,0:T(8,128)(2,1)S(1)}, u32[]{:S(2)}, u32[]{:S(2)}) collective-permute-start(bf16[4,4,16,512]{3,2,1,0:T(8,128)(2,1)S(1)} %all_to_all.39.refs_0_), channel_id=1, source_target_pairs={{0,8},{8,16},{16,24},{24,0},{1,9},{9,17},{17,25},{25,1},{2,10},{10... | collective-permute-start | bytes 786440 | tf_op jit(solution)/shard_map/ppermute | solution.py:296
  50.1 4.3 %collective-permute-start.1 = (bf16[4,4,16,512]{3,2,1,0:T(8,128)(2,1)S(1)}, bf16[4,4,16,512]{3,2,1,0:T(8,128)(2,1)S(1)}, u32[]{:S(2)}, u32[]{:S(2)}) collective-permute-start(bf16[4,4,16,512]{3,2,1,0:T(8,128)(2,1)S(1)} %all_to_all.39.refs_0_), channel_id=1, source_target_pairs={{0,16},{8,24},{16,0},{24,8},{1,17},{9,25},{17,1},{25,9},{2,18},{10... | collective-permute-start | bytes 786440 | tf_op jit(solution)/shard_map/ppermute | solution.py:296
  54.4 3.1 %collective-permute-start.2 = (bf16[4,4,16,512]{3,2,1,0:T(8,128)(2,1)S(1)}, bf16[4,4,16,512]{3,2,1,0:T(8,128)(2,1)S(1)}, u32[]{:S(2)}, u32[]{:S(2)}) collective-permute-start(bf16[4,4,16,512]{3,2,1,0:T(8,128)(2,1)S(1)} %all_to_all.39.refs_0_), channel_id=1, source_target_pairs={{0,24},{8,0},{16,8},{24,16},{1,25},{9,1},{17,9},{25,17},{2,26},{10... | collective-permute-start | bytes 786440 | tf_op jit(solution)/shard_map/ppermute | solution.py:296
  57.6 5.5 %shard_map.95 = (f32[4,4,4,16,512]{4,3,2,1,0:T(8,128)}, f32[8,128]{1,0:T(8,128)}) custom-call(bf16[8,144,1024]{2,1,0:T(8,128)(2,1)} %bitcast.18, bf16[1024,512]{1,0:T(8,128)(2,1)} %refs_5_.1, f32[1,512]{1,0:T(1,128)} %bitcast.15), custom_call_target="tpu_custom_call" | custom-call | tf_op jit(solution)/shard_map/pallas_call | solution.py:33
  63.1 1.0 collective-permute-done.2.refs_3_
  64.8 5.1 %shard_map.96 = (f32[1024,512]{1,0:T(8,128)}, f32[8,8,128]{2,1,0:T(8,128)}, f32[1,512]{1,0:T(1,128)S(1)}) custom-call(s32[1]{0:T(128)} %bitcast.4.me_ref, bf16[8,144,1024]{2,1,0:T(8,128)(2,1)} %bitcast.19, bf16[1024,512]{1,0:T(8,128)(2,1)} %refs_5_.1, bf16[1024,512]{1,0:T(8,128)(2,1)} %grad_ref.1, f32[1,512]{1,0:T(1,128)S(1)} %bitcast.16, ...), custom_call_target="tpu_custom_call" | custom-call | flops 4000000000 | bytes 10000000 | tf_op jit(solution)/shard_map/pallas_call | solution.py:33
  69.9 8.3 %all-to-all-start.2 = ((f32[8,8,128]{2,1,0:T(8,128)}), f32[8,8,128]{2,1,0:T(8,128)S(1)}, u32[]{:S(2)}, u32[]{:S(2)}) async-start(f32[8,8,128]{2,1,0:T(8,128)} %get-tuple-element.28), calls=%async_computation.3 | async-start | bytes 65536 | tf_op jit(solution)/shard_map/all_to_all | solution.py:373
  78.5 4.4 %all-to-all-done.2.refs_1_ = f32[8,8,128]{2,1,0:T(8,128)S(1)} async-done(((f32[8,8,128]{2,1,0:T(8,128)}), f32[8,8,128]{2,1,0:T(8,128)S(1)}, u32[]{:S(2)}, u32[]{:S(2)}) %all-to-all-start.2) | async-done | bytes 32800 | tf_op jit(solution)/shard_map/all_to_all | solution.py:373
  82.9 5.5 %shard_map.98 = bf16[8,320,512]{2,1,0:T(8,128)(2,1)} custom-call(f32[8,128]{1,0:T(8,128)S(1)} %copy-done.6, f32[8,8,128]{2,1,0:T(8,128)S(1)} %all-to-all-done.2.refs_1_, s32[8,1024]{1,0:T(8,128)S(1)} %get-tuple-element.29.refs_2_, f32[8,1024]{1,0:T(8,128)S(1)} %get-tuple-element.30.refs_3_, f32[1024,512]{1,0:T(8,128)} %get-tuple-element.31.refs_4_, ...), custom_call_target="tpu_custom_call" | custom-call | flops 20000000000 | bytes 10000000 | tf_op jit(solution)/shard_map/pallas_call | solution.py:33
  88.5 5.0 %all-to-all-start.4 = ((bf16[8,320,512]{2,1,0:T(8,128)(2,1)}), bf16[8,320,512]{2,1,0:T(8,128)(2,1)}, u32[]{:S(2)}, u32[]{:S(2)}) async-start(bf16[8,320,512]{2,1,0:T(8,128)(2,1)} %shard_map.98), calls=%async_computation.5 | async-start | bytes 5242880 | tf_op jit(solution)/shard_map/all_to_all | solution.py:399
  93.5 8.9 %psum.7.d_gain_ref = f32[1,512]{1,0:T(1,128)S(1)} all-reduce(f32[1,512]{1,0:T(1,128)S(1)} %get-tuple-element.33), channel_id=1, replica_groups=mesh['zh'=4,'zl'=4,'x'=4,'y'=4,'core'=2] {'x'}, use_global_device_ids=true, to_apply=%region_1.0 | all-reduce | flops 512 | bytes 4096 | tf_op jit(solution)/shard_map/psum | solution.py:401
  102.4 1.0 copy-done.1
  103.5 2.9 %collective-permute-start.3 = (bf16[80,512]{1,0:T(8,128)(2,1)S(1)}, bf16[80,512]{1,0:T(8,128)(2,1)S(1)}, u32[]{:S(2)}, u32[]{:S(2)}) collective-permute-start(bf16[80,512]{1,0:T(8,128)(2,1)S(1)} %get-tuple-element.35), channel_id=1, source_target_pairs={{0,32},{32,64},{64,96},{96,0},{1,33},{33,65},{65,97},{97,1},{2,34}... | collective-permute-start | bytes 245768 | tf_op jit(solution)/shard_map/ppermute | solution.py:296
  106.3 3.1 %collective-permute-start.4 = (bf16[80,512]{1,0:T(8,128)(2,1)S(1)}, bf16[80,512]{1,0:T(8,128)(2,1)S(1)}, u32[]{:S(2)}, u32[]{:S(2)}) collective-permute-start(bf16[80,512]{1,0:T(8,128)(2,1)S(1)} %get-tuple-element.36), channel_id=1, source_target_pairs={{0,64},{32,96},{64,0},{96,32},{1,65},{33,97},{65,1},{97,33},{2,66}... | collective-permute-start | bytes 245768 | tf_op jit(solution)/shard_map/ppermute | solution.py:296
  109.5 3.0 %collective-permute-start.5 = (bf16[80,512]{1,0:T(8,128)(2,1)S(1)}, bf16[80,512]{1,0:T(8,128)(2,1)S(1)}, u32[]{:S(2)}, u32[]{:S(2)}) collective-permute-start(bf16[80,512]{1,0:T(8,128)(2,1)S(1)} %get-tuple-element.37), channel_id=1, source_target_pairs={{0,96},{32,0},{64,32},{96,64},{1,97},{33,1},{65,33},{97,65},{2,98}... | collective-permute-start | bytes 245768 | tf_op jit(solution)/shard_map/ppermute | solution.py:296
  112.5 3.5 %collective-permute-done.4.c_ref = bf16[80,512]{1,0:T(8,128)(2,1)S(1)} collective-permute-done((bf16[80,512]{1,0:T(8,128)(2,1)S(1)}, bf16[80,512]{1,0:T(8,128)(2,1)S(1)}, u32[]{:S(2)}, u32[]{:S(2)}) %collective-permute-start.4) | collective-permute-done | bytes 81952 | tf_op jit(solution)/shard_map/ppermute | solution.py:296
  116.5 0.7 shard_map.100
  117.2 8.4 %all-to-all-done.4 = bf16[8,320,512]{2,1,0:T(8,128)(2,1)} async-done(((bf16[8,320,512]{2,1,0:T(8,128)(2,1)}), bf16[8,320,512]{2,1,0:T(8,128)(2,1)}, u32[]{:S(2)}, u32[]{:S(2)}) %all-to-all-start.4) | async-done | bytes 2621472 | tf_op jit(solution)/shard_map/all_to_all | solution.py:399
  125.6 3.3 %all-to-all-start.3 = ((bf16[4,16,640]{2,1,0:T(8,128)(2,1)}), bf16[4,16,640]{2,1,0:T(8,128)(2,1)S(1)}, u32[]{:S(2)}, u32[]{:S(2)}) async-start(bf16[4,16,640]{2,1,0:T(8,128)(2,1)} %shard_map.100), calls=%async_computation.4 | async-start | bytes 163840 | tf_op jit(solution)/shard_map/all_to_all | solution.py:413
  128.9 3.6 %copy.11 = bf16[1,8,40,8,512]{4,3,1,2,0:T(8,128)(2,1)} copy(bf16[1,8,40,8,512]{4,3,2,1,0:T(8,128)(2,1)} %bitcast.11) | data formatting | bytes 5242880 | tf_op jit(solution)/shard_map/all_to_all | solution.py:399
  132.5 8.8 %all-to-all-done.3.refs_0_ = bf16[4,16,640]{2,1,0:T(8,128)(2,1)S(1)} async-done(((bf16[4,16,640]{2,1,0:T(8,128)(2,1)}), bf16[4,16,640]{2,1,0:T(8,128)(2,1)S(1)}, u32[]{:S(2)}, u32[]{:S(2)}) %all-to-all-start.3) | async-done | bytes 81952 | tf_op jit(solution)/shard_map/all_to_all | solution.py:413
  (27 shorter events, 2.4 us)
Async XLA Ops:
  7.2 50.4 %all-gather.3.cloned.1.call-start = ((), (), s32[]{:S(2)}) async-start(), calls=%async_computation.7 | async-start | bytes 2654208 | tf_op jit(solution)/shard_map/all_gather | solution.py:317
  9.6 92.7 %reduce-scatter.2.cloned.1.call-start = ((), (), s32[]{:S(2)}) async-start(), calls=%async_computation.6 | async-start | bytes 2621440 | tf_op jit(solution)/shard_map/reduce_scatter | solution.py:344
  46.9 10.6 %collective-permute-start = (bf16[4,4,16,512]{3,2,1,0:T(8,128)(2,1)S(1)}, bf16[4,4,16,512]{3,2,1,0:T(8,128)(2,1)S(1)}, u32[]{:S(2)}, u32[]{:S(2)}) collective-permute-start(bf16[4,4,16,512]{3,2,1,0:T(8,128)(2,1)S(1)} %all_to_all.39.refs_0_), channel_id=1, source_target_pairs={{0,8},{8,16},{16,24},{24,0},{1,9},{9,17},{17,25},{25,1},{2,10},{10... | collective-permute-start | bytes 786440 | tf_op jit(solution)/shard_map/ppermute | solution.py:296
  50.1 13.0 %collective-permute-start.1 = (bf16[4,4,16,512]{3,2,1,0:T(8,128)(2,1)S(1)}, bf16[4,4,16,512]{3,2,1,0:T(8,128)(2,1)S(1)}, u32[]{:S(2)}, u32[]{:S(2)}) collective-permute-start(bf16[4,4,16,512]{3,2,1,0:T(8,128)(2,1)S(1)} %all_to_all.39.refs_0_), channel_id=1, source_target_pairs={{0,16},{8,24},{16,0},{24,8},{1,17},{9,25},{17,1},{25,9},{2,18},{10... | collective-permute-start | bytes 786440 | tf_op jit(solution)/shard_map/ppermute | solution.py:296
  54.4 9.7 %collective-permute-start.2 = (bf16[4,4,16,512]{3,2,1,0:T(8,128)(2,1)S(1)}, bf16[4,4,16,512]{3,2,1,0:T(8,128)(2,1)S(1)}, u32[]{:S(2)}, u32[]{:S(2)}) collective-permute-start(bf16[4,4,16,512]{3,2,1,0:T(8,128)(2,1)S(1)} %all_to_all.39.refs_0_), channel_id=1, source_target_pairs={{0,24},{8,0},{16,8},{24,16},{1,25},{9,1},{17,9},{25,17},{2,26},{10... | collective-permute-start | bytes 786440 | tf_op jit(solution)/shard_map/ppermute | solution.py:296
  57.5 6.5 %copy-start.4 = (f32[512]{0:T(512)S(1)}, f32[512]{0:T(512)}, u32[]{:S(2)}) copy-start(f32[512]{0:T(512)} %param.10) | copy-start | bytes 6148
  64.1 0.7 copy-start.5
  64.8 13.4 %copy-start.2 = (s32[1024,2]{0,1:T(2,128)S(1)}, s32[1024,2]{0,1:T(2,128)}, u32[]{:S(2)}) copy-start(s32[1024,2]{0,1:T(2,128)} %param.13) | copy-start | bytes 24580
  64.8 13.4 %copy-start.3 = (f32[1024,2]{0,1:T(2,128)S(1)}, f32[1024,2]{0,1:T(2,128)}, u32[]{:S(2)}) copy-start(f32[1024,2]{0,1:T(2,128)} %param.12) | copy-start | bytes 24580
  64.8 18.2 %copy-start = (bf16[1024,512]{1,0:T(8,128)(2,1)S(1)}, bf16[1024,512]{1,0:T(8,128)(2,1)}, u32[]{:S(2)}) copy-start(bf16[1024,512]{1,0:T(8,128)(2,1)} %refs_5_.1) | copy-start | bytes 3145732
  64.8 18.2 %copy-start.6 = (f32[8,128]{1,0:T(8,128)S(1)}, f32[8,128]{1,0:T(8,128)}, u32[]{:S(2)}) copy-start(f32[8,128]{1,0:T(8,128)} %get-tuple-element.26.given_ref.refs_0_) | copy-start | bytes 12292
  69.9 13.0 %all-to-all-start.2 = ((f32[8,8,128]{2,1,0:T(8,128)}), f32[8,8,128]{2,1,0:T(8,128)S(1)}, u32[]{:S(2)}, u32[]{:S(2)}) async-start(f32[8,8,128]{2,1,0:T(8,128)} %get-tuple-element.28), calls=%async_computation.3 | async-start | bytes 65536 | tf_op jit(solution)/shard_map/all_to_all | solution.py:373
  88.5 37.1 %all-to-all-start.4 = ((bf16[8,320,512]{2,1,0:T(8,128)(2,1)}), bf16[8,320,512]{2,1,0:T(8,128)(2,1)}, u32[]{:S(2)}, u32[]{:S(2)}) async-start(bf16[8,320,512]{2,1,0:T(8,128)(2,1)} %shard_map.98), calls=%async_computation.5 | async-start | bytes 5242880 | tf_op jit(solution)/shard_map/all_to_all | solution.py:399
  102.3 1.0 copy-start.1
  103.5 9.0 %collective-permute-start.3 = (bf16[80,512]{1,0:T(8,128)(2,1)S(1)}, bf16[80,512]{1,0:T(8,128)(2,1)S(1)}, u32[]{:S(2)}, u32[]{:S(2)}) collective-permute-start(bf16[80,512]{1,0:T(8,128)(2,1)S(1)} %get-tuple-element.35), channel_id=1, source_target_pairs={{0,32},{32,64},{64,96},{96,0},{1,33},{33,65},{65,97},{97,1},{2,34}... | collective-permute-start | bytes 245768 | tf_op jit(solution)/shard_map/ppermute | solution.py:296
  106.3 9.6 %collective-permute-start.4 = (bf16[80,512]{1,0:T(8,128)(2,1)S(1)}, bf16[80,512]{1,0:T(8,128)(2,1)S(1)}, u32[]{:S(2)}, u32[]{:S(2)}) collective-permute-start(bf16[80,512]{1,0:T(8,128)(2,1)S(1)} %get-tuple-element.36), channel_id=1, source_target_pairs={{0,64},{32,96},{64,0},{96,32},{1,65},{33,97},{65,1},{97,33},{2,66}... | collective-permute-start | bytes 245768 | tf_op jit(solution)/shard_map/ppermute | solution.py:296
  109.5 7.0 %collective-permute-start.5 = (bf16[80,512]{1,0:T(8,128)(2,1)S(1)}, bf16[80,512]{1,0:T(8,128)(2,1)S(1)}, u32[]{:S(2)}, u32[]{:S(2)}) collective-permute-start(bf16[80,512]{1,0:T(8,128)(2,1)S(1)} %get-tuple-element.37), channel_id=1, source_target_pairs={{0,96},{32,0},{64,32},{96,64},{1,97},{33,1},{65,33},{97,65},{2,98}... | collective-permute-start | bytes 245768 | tf_op jit(solution)/shard_map/ppermute | solution.py:296
  125.6 15.7 %all-to-all-start.3 = ((bf16[4,16,640]{2,1,0:T(8,128)(2,1)}), bf16[4,16,640]{2,1,0:T(8,128)(2,1)S(1)}, u32[]{:S(2)}, u32[]{:S(2)}) async-start(bf16[4,16,640]{2,1,0:T(8,128)(2,1)} %shard_map.100), calls=%async_computation.4 | async-start | bytes 163840 | tf_op jit(solution)/shard_map/all_to_all | solution.py:413
Sparse Core Ops, SparseCore 0:
  10.7 39.0 all-gather.2
  63.2 32.3 reduce-scatter.1

commit v9 on v8

--- a/solution.py
+++ b/solution.py
@@ -151,17 +151,14 @@
 
     @pl.when(step == 0)
     def _():
-        xs, zl = len(parts), parts[0].shape[0]
+        xs = len(parts)
         gets = [pltpu.make_async_copy(given_ref, inverse_ref, sem)]
         gets[0].start()
         for x_step, part in enumerate(parts):
             x = lax.rem(me_ref[0] + (xs - x_step), xs)
-            for low in range(zl):
-                get = pltpu.make_async_copy(
-                    part.at[low], weight_ref.at[:, low, x], sems.at[x_step, low]
-                )
-                get.start()
-                gets.append(get)
+            get = pltpu.make_async_copy(part, weight_ref.at[:, :, x], sems.at[x_step])
+            get.start()
+            gets.append(get)
         d_gain_ref[...] = jnp.zeros(d_gain_ref.shape, jnp.float32)
         for get in gets:
             get.wait()
@@ -312,11 +309,12 @@
 
     packed, copies = call(
         pack_kernel, value_grad, attn_input, value_weight,
-        out=[((own_rows + PAD, features), bf16), ((zh, rows, columns), bf16)],
+        out=[((own_rows + PAD, features), bf16), ((zh * zl, rows, columns), bf16)],
     )
     gathered = lax.all_gather(packed, EXPERT, axis=0)
 
-    weight = to_all(lax.all_to_all(copies, "zh", 0, 0, tiled=True), "zl")
+    weight = lax.all_to_all(copies, ("zh", "zl"), 0, 0, tiled=True)
+    weight = weight.reshape(zh, zl, rows, columns)
     weights = [weight] + [further(weight, "x", step) for step in range(1, xs)]
     gathered, weights[1] = lax.optimization_barrier((gathered, weights[1]))
 
@@ -363,7 +361,7 @@
         scratch=[
             pltpu.VMEM((8, group // 8), f32),
             pltpu.VMEM((zh, zl, xs, rows, columns), bf16),
-            pltpu.SemaphoreType.DMA((xs, zl)),
+            pltpu.SemaphoreType.DMA((xs,)),
             pltpu.SemaphoreType.DMA(()),
         ],
         grid=2,

time: 150 us -> 149 us (level)
  starting transfers between devices: 36.2 us -> 45.3 us
  blocking collectives: 46.1 us -> 37.3 us
  waiting for transfers between devices: 26.6 us -> 24.7 us
    all_to_all x2 -> x1, blocking collectives: 37.3 us -> 28.9 us  [on_device(): weight = lax.all_to_all(copies, ('zh', 'zl'), 0, 0, tiled=True)]
    all_to_all x1, starting transfers between devices: 3.29 us -> 7.6 us  [on_device(): parts = lax.all_to_all(parts, 'zh', 0, 0, tiled=True)]
    all_to_all x1, starting transfers between devices: 8.25 us -> 10.9 us  [on_device(): inner = lax.all_to_all(inner, EXPERT, 0, 0, tiled=True)]
    ppermute x6, starting transfers between devices: 19.5 us -> 21.7 us  [further(): lax.ppermute(part, axis, [(i, (i + step) % size) for i in range(size)])]
    all_to_all x1, waiting for transfers between devices: 8.36 us -> 6.77 us  [on_device(): lax.all_to_all(sent, EXPERT, split_axis=0, concat_axis=2, tiled=True)]
  transfers between devices with their start and end apart: 11 -> 11, of which waited for: 6 -> 6; matrix products, arithmetic and copies ran while one was open for 2% -> 2% of each run, Pallas kernels for 12% -> 11%
where the time goes in v9:
time: 149 us; the launch traced here: 147 us
  starting transfers between devices  45.3 us (30%)
  blocking collectives  37.3 us (25%)
  waiting for transfers between devices  24.7 us (17%)
  Pallas kernels  19.9 us (13%)
  between operations  14.2 us (10%)
  local copies, waits for them, and re-layouts  5.33 us (4%)
    all_to_all x1, blocking collectives, on_device(): weight = lax.all_to_all(copies, ('zh', 'zl'), 0, 0, tiled=True)  28.9 us
    ppermute x6, starting transfers between devices, further(): lax.ppermute(part, axis, [(i, (i + step) % size) for i in range(size)])  21.7 us
    pallas_call x8, Pallas kernels, call(): pl.pallas_call(kernel, grid=(grid,), in_specs=in_specs or [SMEM if o.shap...  19.9 us
    all_to_all x1, starting transfers between devices, on_device(): inner = lax.all_to_all(inner, EXPERT, 0, 0, tiled=True)  10.9 us
    all_to_all x1, waiting for transfers between devices, on_device(): parts = lax.all_to_all(parts, 'zh', 0, 0, tiled=True)  8.96 us
    psum x1, blocking collectives, on_device(): d_gain = lax.psum(own_gain, 'x')  8.43 us
    all_to_all x1, starting transfers between devices, on_device(): parts = lax.all_to_all(parts, 'zh', 0, 0, tiled=True)  7.6 us
    all_to_all x1, waiting for transfers between devices, on_device(): lax.all_to_all(sent, EXPERT, split_axis=0, concat_axis=2, tiled=True)  6.77 us
  transfers between devices with their start and end apart: 11, of which 6 were waited for; matrix products, arithmetic and copies ran while one was open for 2% of the time, Pallas kernels for 11%

profile of v9, /device:TPU:1, one launch (start us, length us, event | category | flops | bytes accessed | tf_op | source)
XLA Modules:
  0.0 146.7 jit_solution(11216438091973802630)
XLA Ops:
  7.2 2.4 %shard_map.94 = (bf16[144,1024]{1,0:T(8,128)(2,1)}, bf16[16,16,512]{2,1,0:T(8,128)(2,1)}) custom-call(bf16[128,1024]{1,0:T(8,128)(2,1)} %value_ref.1, bf16[1024,512]{1,0:T(8,128)(2,1)} %refs_5_.1, bf16[16,512]{1,0:T(8,128)(2,1)} %weight_ref.1), custom_call_target="tpu_custom_call" | custom-call | tf_op jit(solution)/shard_map/pallas_call | solution.py:33
  9.7 28.9 %all_to_all.33 = bf16[16,16,512]{2,1,0:T(8,128)(2,1)S(1)} all-to-all(bf16[16,16,512]{2,1,0:T(8,128)(2,1)} %get-tuple-element.23), channel_id=1, replica_groups=mesh['zh'=4,'zl'=4,'x'=4,'y'=4,'core'=2] {'zh','zl'}, dimensions={0} | all-to-all | bytes 524288 | tf_op jit(solution)/shard_map/all_to_all | solution.py:316
  38.6 3.1 %collective-permute-start = (bf16[4,4,16,512]{3,2,1,0:T(8,128)(2,1)S(1)}, bf16[4,4,16,512]{3,2,1,0:T(8,128)(2,1)S(1)}, u32[]{:S(2)}, u32[]{:S(2)}) collective-permute-start(bf16[4,4,16,512]{3,2,1,0:T(8,128)(2,1)S(1)} %bitcast.14), channel_id=1, source_target_pairs={{0,8},{8,16},{16,24},{24,0},{1,9},{9,17},{17,25},{25,1},{2,10},{10... | collective-permute-start | bytes 786440 | tf_op jit(solution)/shard_map/ppermute | solution.py:293
  41.7 4.4 %collective-permute-start.1 = (bf16[4,4,16,512]{3,2,1,0:T(8,128)(2,1)S(1)}, bf16[4,4,16,512]{3,2,1,0:T(8,128)(2,1)S(1)}, u32[]{:S(2)}, u32[]{:S(2)}) collective-permute-start(bf16[4,4,16,512]{3,2,1,0:T(8,128)(2,1)S(1)} %bitcast.15), channel_id=1, source_target_pairs={{0,16},{8,24},{16,0},{24,8},{1,17},{9,25},{17,1},{25,9},{2,18},{10... | collective-permute-start | bytes 786440 | tf_op jit(solution)/shard_map/ppermute | solution.py:293
  46.1 3.1 %collective-permute-start.2 = (bf16[4,4,16,512]{3,2,1,0:T(8,128)(2,1)S(1)}, bf16[4,4,16,512]{3,2,1,0:T(8,128)(2,1)S(1)}, u32[]{:S(2)}, u32[]{:S(2)}) collective-permute-start(bf16[4,4,16,512]{3,2,1,0:T(8,128)(2,1)S(1)} %bitcast.16), channel_id=1, source_target_pairs={{0,24},{8,0},{16,8},{24,16},{1,25},{9,1},{17,9},{25,17},{2,26},{10... | collective-permute-start | bytes 786440 | tf_op jit(solution)/shard_map/ppermute | solution.py:293
  49.8 5.5 %shard_map.95 = (f32[4,4,4,16,512]{4,3,2,1,0:T(8,128)}, f32[8,128]{1,0:T(8,128)}) custom-call(bf16[8,144,1024]{2,1,0:T(8,128)(2,1)} %bitcast.23, bf16[1024,512]{1,0:T(8,128)(2,1)} %refs_5_.1, f32[1,512]{1,0:T(1,128)} %bitcast.20), custom_call_target="tpu_custom_call" | custom-call | tf_op jit(solution)/shard_map/pallas_call | solution.py:33
  55.3 0.7 copy-done.5
  56.0 4.7 %shard_map.96 = (f32[1024,512]{1,0:T(8,128)}, f32[8,8,128]{2,1,0:T(8,128)}, f32[1,512]{1,0:T(1,128)S(1)}) custom-call(s32[1]{0:T(128)} %bitcast.5.me_ref, bf16[8,144,1024]{2,1,0:T(8,128)(2,1)} %bitcast.24, bf16[1024,512]{1,0:T(8,128)(2,1)} %refs_5_.1, bf16[1024,512]{1,0:T(8,128)(2,1)} %grad_ref.1, f32[1,512]{1,0:T(1,128)S(1)} %bitcast.21, ...), custom_call_target="tpu_custom_call" | custom-call | flops 4000000000 | bytes 10000000 | tf_op jit(solution)/shard_map/pallas_call | solution.py:33
  60.8 10.9 %all-to-all-start.1 = ((f32[8,8,128]{2,1,0:T(8,128)}), f32[8,8,128]{2,1,0:T(8,128)S(1)}, u32[]{:S(2)}, u32[]{:S(2)}) async-start(f32[8,8,128]{2,1,0:T(8,128)} %get-tuple-element.28), calls=%async_computation.2 | async-start | bytes 65536 | tf_op jit(solution)/shard_map/all_to_all | solution.py:371
  72.0 4.4 %all-to-all-done.1.refs_1_ = f32[8,8,128]{2,1,0:T(8,128)S(1)} async-done(((f32[8,8,128]{2,1,0:T(8,128)}), f32[8,8,128]{2,1,0:T(8,128)S(1)}, u32[]{:S(2)}, u32[]{:S(2)}) %all-to-all-start.1) | async-done | bytes 32800 | tf_op jit(solution)/shard_map/all_to_all | solution.py:371
  76.5 5.5 %shard_map.98 = bf16[8,320,512]{2,1,0:T(8,128)(2,1)} custom-call(f32[8,128]{1,0:T(8,128)S(1)} %copy-done.6, f32[8,8,128]{2,1,0:T(8,128)S(1)} %all-to-all-done.1.refs_1_, s32[8,1024]{1,0:T(8,128)S(1)} %get-tuple-element.29.refs_2_, f32[8,1024]{1,0:T(8,128)S(1)} %get-tuple-element.30.refs_3_, f32[1024,512]{1,0:T(8,128)} %get-tuple-element.31.refs_4_, ...), custom_call_target="tpu_custom_call" | custom-call | flops 20000000000 | bytes 10000000 | tf_op jit(solution)/shard_map/pallas_call | solution.py:33
  82.0 5.0 %all-to-all-start.3 = ((bf16[8,320,512]{2,1,0:T(8,128)(2,1)}), bf16[8,320,512]{2,1,0:T(8,128)(2,1)}, u32[]{:S(2)}, u32[]{:S(2)}) async-start(bf16[8,320,512]{2,1,0:T(8,128)(2,1)} %shard_map.98), calls=%async_computation.4 | async-start | bytes 5242880 | tf_op jit(solution)/shard_map/all_to_all | solution.py:397
  87.0 8.4 %psum.7.d_gain_ref = f32[1,512]{1,0:T(1,128)S(1)} all-reduce(f32[1,512]{1,0:T(1,128)S(1)} %get-tuple-element.33), channel_id=1, replica_groups=mesh['zh'=4,'zl'=4,'x'=4,'y'=4,'core'=2] {'x'}, use_global_device_ids=true, to_apply=%region_1.0 | all-reduce | flops 512 | bytes 4096 | tf_op jit(solution)/shard_map/psum | solution.py:399
  95.4 1.0 copy-done.1
  96.6 5.2 %collective-permute-start.3 = (bf16[80,512]{1,0:T(8,128)(2,1)S(1)}, bf16[80,512]{1,0:T(8,128)(2,1)S(1)}, u32[]{:S(2)}, u32[]{:S(2)}) collective-permute-start(bf16[80,512]{1,0:T(8,128)(2,1)S(1)} %get-tuple-element.35), channel_id=1, source_target_pairs={{0,32},{32,64},{64,96},{96,0},{1,33},{33,65},{65,97},{97,1},{2,34}... | collective-permute-start | bytes 245768 | tf_op jit(solution)/shard_map/ppermute | solution.py:293
  101.8 3.6 %collective-permute-start.4 = (bf16[80,512]{1,0:T(8,128)(2,1)S(1)}, bf16[80,512]{1,0:T(8,128)(2,1)S(1)}, u32[]{:S(2)}, u32[]{:S(2)}) collective-permute-start(bf16[80,512]{1,0:T(8,128)(2,1)S(1)} %get-tuple-element.36), channel_id=1, source_target_pairs={{0,64},{32,96},{64,0},{96,32},{1,65},{33,97},{65,1},{97,33},{2,66}... | collective-permute-start | bytes 245768 | tf_op jit(solution)/shard_map/ppermute | solution.py:293
  105.4 2.3 %collective-permute-start.5 = (bf16[80,512]{1,0:T(8,128)(2,1)S(1)}, bf16[80,512]{1,0:T(8,128)(2,1)S(1)}, u32[]{:S(2)}, u32[]{:S(2)}) collective-permute-start(bf16[80,512]{1,0:T(8,128)(2,1)S(1)} %get-tuple-element.37), channel_id=1, source_target_pairs={{0,96},{32,0},{64,32},{96,64},{1,97},{33,1},{65,33},{97,65},{2,98}... | collective-permute-start | bytes 245768 | tf_op jit(solution)/shard_map/ppermute | solution.py:293
  107.7 1.2 collective-permute-done.4.c_ref
  108.9 2.7 %collective-permute-done.5.d_ref = bf16[80,512]{1,0:T(8,128)(2,1)S(1)} collective-permute-done((bf16[80,512]{1,0:T(8,128)(2,1)S(1)}, bf16[80,512]{1,0:T(8,128)(2,1)S(1)}, u32[]{:S(2)}, u32[]{:S(2)}) %collective-permute-start.5) | collective-permute-done | bytes 81952 | tf_op jit(solution)/shard_map/ppermute | solution.py:293
  111.6 0.7 shard_map.100
  112.3 6.8 %all-to-all-done.3 = bf16[8,320,512]{2,1,0:T(8,128)(2,1)} async-done(((bf16[8,320,512]{2,1,0:T(8,128)(2,1)}), bf16[8,320,512]{2,1,0:T(8,128)(2,1)}, u32[]{:S(2)}, u32[]{:S(2)}) %all-to-all-start.3) | async-done | bytes 2621472 | tf_op jit(solution)/shard_map/all_to_all | solution.py:397
  119.1 7.6 %all-to-all-start.2 = ((bf16[4,16,640]{2,1,0:T(8,128)(2,1)}), bf16[4,16,640]{2,1,0:T(8,128)(2,1)S(1)}, u32[]{:S(2)}, u32[]{:S(2)}) async-start(bf16[4,16,640]{2,1,0:T(8,128)(2,1)} %shard_map.100), calls=%async_computation.3 | async-start | bytes 163840 | tf_op jit(solution)/shard_map/all_to_all | solution.py:411
  126.7 3.6 %copy.11 = bf16[1,8,40,8,512]{4,3,1,2,0:T(8,128)(2,1)} copy(bf16[1,8,40,8,512]{4,3,2,1,0:T(8,128)(2,1)} %bitcast.12) | data formatting | bytes 5242880 | tf_op jit(solution)/shard_map/all_to_all | solution.py:397
  130.3 9.0 %all-to-all-done.2.refs_0_ = bf16[4,16,640]{2,1,0:T(8,128)(2,1)S(1)} async-done(((bf16[4,16,640]{2,1,0:T(8,128)(2,1)}), bf16[4,16,640]{2,1,0:T(8,128)(2,1)S(1)}, u32[]{:S(2)}, u32[]{:S(2)}) %all-to-all-start.2) | async-done | bytes 81952 | tf_op jit(solution)/shard_map/all_to_all | solution.py:411
  (25 shorter events, 1.8 us)
Async XLA Ops:
  7.2 42.6 %all-gather.3.cloned.1.call-start = ((), (), s32[]{:S(2)}) async-start(), calls=%async_computation.6 | async-start | bytes 2654208 | tf_op jit(solution)/shard_map/all_gather | solution.py:314
  9.6 85.8 %reduce-scatter.2.cloned.1.call-start = ((), (), s32[]{:S(2)}) async-start(), calls=%async_computation.5 | async-start | bytes 2621440 | tf_op jit(solution)/shard_map/reduce_scatter | solution.py:342
  38.6 10.6 %collective-permute-start = (bf16[4,4,16,512]{3,2,1,0:T(8,128)(2,1)S(1)}, bf16[4,4,16,512]{3,2,1,0:T(8,128)(2,1)S(1)}, u32[]{:S(2)}, u32[]{:S(2)}) collective-permute-start(bf16[4,4,16,512]{3,2,1,0:T(8,128)(2,1)S(1)} %bitcast.14), channel_id=1, source_target_pairs={{0,8},{8,16},{16,24},{24,0},{1,9},{9,17},{17,25},{25,1},{2,10},{10... | collective-permute-start | bytes 786440 | tf_op jit(solution)/shard_map/ppermute | solution.py:293
  41.7 13.6 %collective-permute-start.1 = (bf16[4,4,16,512]{3,2,1,0:T(8,128)(2,1)S(1)}, bf16[4,4,16,512]{3,2,1,0:T(8,128)(2,1)S(1)}, u32[]{:S(2)}, u32[]{:S(2)}) collective-permute-start(bf16[4,4,16,512]{3,2,1,0:T(8,128)(2,1)S(1)} %bitcast.15), channel_id=1, source_target_pairs={{0,16},{8,24},{16,0},{24,8},{1,17},{9,25},{17,1},{25,9},{2,18},{10... | collective-permute-start | bytes 786440 | tf_op jit(solution)/shard_map/ppermute | solution.py:293
  46.1 9.2 %collective-permute-start.2 = (bf16[4,4,16,512]{3,2,1,0:T(8,128)(2,1)S(1)}, bf16[4,4,16,512]{3,2,1,0:T(8,128)(2,1)S(1)}, u32[]{:S(2)}, u32[]{:S(2)}) collective-permute-start(bf16[4,4,16,512]{3,2,1,0:T(8,128)(2,1)S(1)} %bitcast.16), channel_id=1, source_target_pairs={{0,24},{8,0},{16,8},{24,16},{1,25},{9,1},{17,9},{25,17},{2,26},{10... | collective-permute-start | bytes 786440 | tf_op jit(solution)/shard_map/ppermute | solution.py:293
  49.8 5.6 %copy-start.4 = (f32[512]{0:T(512)S(1)}, f32[512]{0:T(512)}, u32[]{:S(2)}) copy-start(f32[512]{0:T(512)} %param.10) | copy-start | bytes 6148
  55.3 0.7 copy-start.5
  56.0 15.7 %copy-start.2 = (s32[1024,2]{0,1:T(2,128)S(1)}, s32[1024,2]{0,1:T(2,128)}, u32[]{:S(2)}) copy-start(s32[1024,2]{0,1:T(2,128)} %param.13) | copy-start | bytes 24580
  56.0 15.7 %copy-start.3 = (f32[1024,2]{0,1:T(2,128)S(1)}, f32[1024,2]{0,1:T(2,128)}, u32[]{:S(2)}) copy-start(f32[1024,2]{0,1:T(2,128)} %param.12) | copy-start | bytes 24580
  56.0 20.4 %copy-start = (bf16[1024,512]{1,0:T(8,128)(2,1)S(1)}, bf16[1024,512]{1,0:T(8,128)(2,1)}, u32[]{:S(2)}) copy-start(bf16[1024,512]{1,0:T(8,128)(2,1)} %refs_5_.1) | copy-start | bytes 3145732
  56.0 20.4 %copy-start.6 = (f32[8,128]{1,0:T(8,128)S(1)}, f32[8,128]{1,0:T(8,128)}, u32[]{:S(2)}) copy-start(f32[8,128]{1,0:T(8,128)} %get-tuple-element.26.given_ref.refs_0_) | copy-start | bytes 12292
  60.8 15.7 %all-to-all-start.1 = ((f32[8,8,128]{2,1,0:T(8,128)}), f32[8,8,128]{2,1,0:T(8,128)S(1)}, u32[]{:S(2)}, u32[]{:S(2)}) async-start(f32[8,8,128]{2,1,0:T(8,128)} %get-tuple-element.28), calls=%async_computation.2 | async-start | bytes 65536 | tf_op jit(solution)/shard_map/all_to_all | solution.py:371
  82.0 37.1 %all-to-all-start.3 = ((bf16[8,320,512]{2,1,0:T(8,128)(2,1)}), bf16[8,320,512]{2,1,0:T(8,128)(2,1)}, u32[]{:S(2)}, u32[]{:S(2)}) async-start(bf16[8,320,512]{2,1,0:T(8,128)(2,1)} %shard_map.98), calls=%async_computation.4 | async-start | bytes 5242880 | tf_op jit(solution)/shard_map/all_to_all | solution.py:397
  95.4 1.0 copy-start.1
  96.6 11.2 %collective-permute-start.3 = (bf16[80,512]{1,0:T(8,128)(2,1)S(1)}, bf16[80,512]{1,0:T(8,128)(2,1)S(1)}, u32[]{:S(2)}, u32[]{:S(2)}) collective-permute-start(bf16[80,512]{1,0:T(8,128)(2,1)S(1)} %get-tuple-element.35), channel_id=1, source_target_pairs={{0,32},{32,64},{64,96},{96,0},{1,33},{33,65},{65,97},{97,1},{2,34}... | collective-permute-start | bytes 245768 | tf_op jit(solution)/shard_map/ppermute | solution.py:293
  101.8 7.1 %collective-permute-start.4 = (bf16[80,512]{1,0:T(8,128)(2,1)S(1)}, bf16[80,512]{1,0:T(8,128)(2,1)S(1)}, u32[]{:S(2)}, u32[]{:S(2)}) collective-permute-start(bf16[80,512]{1,0:T(8,128)(2,1)S(1)} %get-tuple-element.36), channel_id=1, source_target_pairs={{0,64},{32,96},{64,0},{96,32},{1,65},{33,97},{65,1},{97,33},{2,66}... | collective-permute-start | bytes 245768 | tf_op jit(solution)/shard_map/ppermute | solution.py:293
  105.4 6.2 %collective-permute-start.5 = (bf16[80,512]{1,0:T(8,128)(2,1)S(1)}, bf16[80,512]{1,0:T(8,128)(2,1)S(1)}, u32[]{:S(2)}, u32[]{:S(2)}) collective-permute-start(bf16[80,512]{1,0:T(8,128)(2,1)S(1)} %get-tuple-element.37), channel_id=1, source_target_pairs={{0,96},{32,0},{64,32},{96,64},{1,97},{33,1},{65,33},{97,65},{2,98}... | collective-permute-start | bytes 245768 | tf_op jit(solution)/shard_map/ppermute | solution.py:293
  119.1 20.2 %all-to-all-start.2 = ((bf16[4,16,640]{2,1,0:T(8,128)(2,1)}), bf16[4,16,640]{2,1,0:T(8,128)(2,1)S(1)}, u32[]{:S(2)}, u32[]{:S(2)}) async-start(bf16[4,16,640]{2,1,0:T(8,128)(2,1)} %shard_map.100), calls=%async_computation.3 | async-start | bytes 163840 | tf_op jit(solution)/shard_map/all_to_all | solution.py:411
Sparse Core Ops, SparseCore 0:
  10.7 39.0 all-gather.2
  55.4 37.8 reduce-scatter.1

commit v10 on v9

--- a/solution.py
+++ b/solution.py
@@ -57,15 +57,23 @@
     return rows.astype(jnp.bfloat16)
 
 
-def pack_kernel(value_ref, input_ref, weight_ref, packed_ref, copies_ref):
-    rows = value_ref.shape[0]
-    inputs = input_ref[...].astype(jnp.float32)
-    squares = jnp.sum(inputs * inputs, axis=1, keepdims=True)
-    row = jnp.transpose(jnp.broadcast_to(squares, (squares.shape[0], 8)))[0:1, :]
-    packed_ref[0:rows, :] = value_ref[...]
-    packed_ref[rows:, :] = pieces(row)
-    for peer in range(copies_ref.shape[0]):
-        copies_ref[peer] = weight_ref[...]
+def squares_kernel(input_ref, squares_ref):
+    tile = squares_ref.shape[1]
+    for at in range(squares_ref.shape[0]):
+        inputs = input_ref[at * tile : (at + 1) * tile, :].astype(jnp.float32)
+        squares = jnp.sum(inputs * inputs, axis=1, keepdims=True)
+        squares_ref[at : at + 1, :] = jnp.transpose(jnp.broadcast_to(squares, (tile, 8)))[0:1, :]
+
+
+def norm_kernel(width, squares_ref, input_ref, gain_ref, normed_ref, inverse_ref):
+    inverse = 1.0 / jnp.sqrt(squares_ref[...] / width + epsilon)
+    inverse_ref[...] = inverse
+    factor = jnp.transpose(inverse)
+    tile = inverse.shape[1]
+    for at in range(inverse.shape[0]):
+        tokens = slice(at * tile, (at + 1) * tile)
+        scaled = input_ref[tokens, :].astype(jnp.float32) * factor[:, at : at + 1]
+        normed_ref[tokens, :] = (scaled * gain_ref[...]).astype(jnp.bfloat16)
 
 
 def route_kernel(routes_ref, logits_ref, slot_ref, gate_ref):
@@ -89,38 +97,13 @@
     gate_ref[...] = jnp.where(first, gate_first, jnp.where(second, gate_second, 0.0))
 
 
-def value_kernel(
-    width, gathered_ref, whole_input_ref, gain_ref, d_value_ref, inverse_ref,
-    squares_ref, input_ref, value_ref, normed_ref, partial_ref, sems,
-):
-    devices, rows, features = value_ref.shape
-    group = input_ref.shape[0]
-    get_squares = pltpu.make_async_copy(
-        gathered_ref.at[:, pl.ds(rows, PAD), :], squares_ref, sems.at[0]
-    )
-    get_value = pltpu.make_async_copy(
-        gathered_ref.at[:, pl.ds(0, rows), :], value_ref, sems.at[1]
-    )
-    get_input = pltpu.make_async_copy(whole_input_ref, input_ref, sems.at[2])
-    get_squares.start()
-    get_input.start()
-    get_value.start()
-    get_squares.wait()
-    squares = jnp.zeros((1, group), jnp.float32)
-    for device in range(devices):
-        part = squares_ref[device].astype(jnp.float32)
-        squares += jnp.sum(part, axis=0, keepdims=True)
-    inverse = 1.0 / jnp.sqrt(squares / width + epsilon)
-    tile = group // 8
-    for at in range(8):
-        inverse_ref[at : at + 1, :] = inverse[:, at * tile : (at + 1) * tile]
-    get_input.wait()
-    scaled = input_ref[...].astype(jnp.float32) * column(inverse)
-    normed_ref[...] = (scaled * gain_ref[...]).astype(jnp.bfloat16)
-
+def value_kernel(given_ref, normed_ref, d_value_ref, value_ref, partial_ref, get_sem, sems):
+    get = pltpu.make_async_copy(given_ref, value_ref, get_sem)
+    get.start()
     zh, xs, zl, own, _ = partial_ref.shape
-    block = features // zh
-    get_value.wait()
+    group = normed_ref.shape[0]
+    block = value_ref.shape[2] // zh
+    get.wait()
     puts = []
     for high in range(zh):
         partial = lax.dot_general(
@@ -134,7 +117,7 @@
                 start = (low * xs + x) * own
                 partial_ref[high, x, low] = partial[start : start + own, :]
         put = pltpu.make_async_copy(
-            partial_ref.at[high], d_value_ref.at[:, :, high], sems.at[3 + high]
+            partial_ref.at[high], d_value_ref.at[:, :, high], sems.at[high]
         )
         put.start()
         puts.append(put)
@@ -307,14 +290,19 @@
     f32, bf16 = jnp.float32, jnp.bfloat16
     gain_row = norm_gain[None]
 
-    packed, copies = call(
-        pack_kernel, value_grad, attn_input, value_weight,
-        out=[((own_rows + PAD, features), bf16), ((zh * zl, rows, columns), bf16)],
-    )
-    gathered = lax.all_gather(packed, EXPERT, axis=0)
-
-    weight = lax.all_to_all(copies, ("zh", "zl"), 0, 0, tiled=True)
+    gathered = lax.all_gather(value_grad, EXPERT, axis=0)
+
+    weight = jnp.broadcast_to(value_weight[None], (zh * zl, rows, columns))
+    weight = lax.all_to_all(weight, ("zh", "zl"), 0, 0, tiled=True)
     weight = weight.reshape(zh, zl, rows, columns)
+    (squares,) = call(squares_kernel, attn_input, out=[((8, group // 8), f32)], limit=24)
+    squares = lax.psum(squares, EXPERT)
+    normed, inverse = call(
+        lambda *refs: norm_kernel(width, *refs), squares, attn_input, gain_row,
+        out=[((group, columns), bf16), ((8, group // 8), f32)],
+        limit=24,
+    )
+    weight, normed = lax.optimization_barrier((weight, normed))
     weights = [weight] + [further(weight, "x", step) for step in range(1, xs)]
     gathered, weights[1] = lax.optimization_barrier((gathered, weights[1]))
 
@@ -324,18 +312,16 @@
         limit=24,
     )
 
-    d_value, inverse = call(
-        lambda *refs: value_kernel(width, *refs), gathered, attn_input, gain_row,
-        out=[((xs, zl, zh, rows, columns), f32), ((8, group // 8), f32)],
-        in_specs=[ANY, ANY, whole((1, columns))],
-        out_specs=[ANY, whole((8, group // 8))],
+    (d_value,) = call(
+        value_kernel, gathered, normed,
+        out=[((xs, zl, zh, rows, columns), f32)],
+        in_specs=[ANY, whole((group, columns))],
+        out_specs=[ANY],
         scratch=[
-            pltpu.VMEM((experts, PAD, features), bf16),
-            pltpu.VMEM((group, columns), bf16),
             pltpu.VMEM((experts, own_rows, features), bf16),
-            pltpu.VMEM((group, columns), bf16),
             pltpu.VMEM((zh, xs, zl, rows, columns), f32),
-            pltpu.SemaphoreType.DMA((3 + zh,)),
+            pltpu.SemaphoreType.DMA(()),
+            pltpu.SemaphoreType.DMA((zh,)),
         ],
         limit=VALUE_LIMIT,
     )

time: 149 us -> 151 us (1.013)
  blocking collectives: 37.3 us -> 22.4 us
  starting transfers between devices: 45.3 us -> 59.1 us
  local copies, waits for them, and re-layouts: 5.33 us -> 8.96 us
  Pallas kernels: 19.9 us -> 17.7 us
    all_to_all x1 -> x0, blocking collectives: 28.9 us -> none  [on_device(): weight = lax.all_to_all(copies, ('zh', 'zl'), 0, 0, tiled=True)]
    all_to_all x0 -> x1, starting transfers between devices: none -> 15.7 us  [on_device(): weight = lax.all_to_all(weight, ('zh', 'zl'), 0, 0, tiled=True)]
    psum x0 -> x1, blocking collectives: none -> 13.2 us  [on_device(): squares = lax.psum(squares, EXPERT)]
    all_to_all x1, starting transfers between devices: 10.9 us -> 6.69 us  [on_device(): inner = lax.all_to_all(inner, EXPERT, 0, 0, tiled=True)]
    all_to_all x1, starting transfers between devices: 7.6 us -> 10.6 us  [on_device(): parts = lax.all_to_all(parts, 'zh', 0, 0, tiled=True)]
    unnamed x14 -> x18, local copies, waits for them, and re-layouts: 1.74 us -> 3.93 us
    pallas_call x8 -> x9, Pallas kernels: 19.9 us -> 17.7 us  [call(): pl.pallas_call(kernel, grid=(grid,), in_specs=in_specs or [SMEM if o.shap...]
  transfers between devices with their start and end apart: 11 -> 12, of which waited for: 6 -> 7; matrix products, arithmetic and copies ran while one was open for 2% -> 3% of each run, Pallas kernels for 11% -> 11%
where the time goes in v10:
time: 151 us; the launch traced here: 149 us
  starting transfers between devices  59.1 us (39%)
  waiting for transfers between devices  26.2 us (17%)
  blocking collectives  22.4 us (15%)
  Pallas kernels  17.7 us (12%)
  between operations  14.2 us (9%)
  local copies, waits for them, and re-layouts  8.96 us (6%)
    ppermute x6, starting transfers between devices, further(): lax.ppermute(part, axis, [(i, (i + step) % size) for i in range(size)])  20.9 us
    pallas_call x9, Pallas kernels, call(): pl.pallas_call(kernel, grid=(grid,), in_specs=in_specs or [SMEM if o.shap...  17.7 us
    all_to_all x1, starting transfers between devices, on_device(): weight = lax.all_to_all(weight, ('zh', 'zl'), 0, 0, tiled=True)  15.7 us
    psum x1, blocking collectives, on_device(): squares = lax.psum(squares, EXPERT)  13.2 us
    all_to_all x1, starting transfers between devices, on_device(): parts = lax.all_to_all(parts, 'zh', 0, 0, tiled=True)  10.6 us
    psum x1, blocking collectives, on_device(): d_gain = lax.psum(own_gain, 'x')  9.11 us
    all_to_all x1, waiting for transfers between devices, on_device(): parts = lax.all_to_all(parts, 'zh', 0, 0, tiled=True)  8.22 us
    all_to_all x1, waiting for transfers between devices, on_device(): lax.all_to_all(sent, EXPERT, split_axis=0, concat_axis=2, tiled=True)  7.86 us
  transfers between devices with their start and end apart: 12, of which 7 were waited for; matrix products, arithmetic and copies ran while one was open for 3% of the time, Pallas kernels for 11%

profile of v10, /device:TPU:1, one launch (start us, length us, event | category | flops | bytes accessed | tf_op | source)
XLA Modules:
  0.0 148.6 jit_solution(6271953220138923768)
XLA Ops:
  7.9 1.4 broadcast_in_dim.4
  9.4 15.7 %all-to-all-start = ((bf16[16,16,512]{2,1,0:T(8,128)(2,1)}), bf16[16,16,512]{2,1,0:T(8,128)(2,1)S(1)}, u32[]{:S(2)}, u32[]{:S(2)}) async-start(bf16[16,16,512]{2,1,0:T(8,128)(2,1)} %broadcast_in_dim.4), calls=%async_computation | async-start | bytes 524288 | tf_op jit(solution)/shard_map/all_to_all | solution.py:296
  25.2 1.2 copy-done
  26.8 13.2 %psum.14.refs_0_ = f32[8,128]{1,0:T(8,128)S(1)} all-reduce(f32[8,128]{1,0:T(8,128)S(1)} %shard_map.94), channel_id=1, replica_groups=mesh['zh'=4,'zl'=4,'x'=4,'y'=4,'core'=2] {'y','core'}, use_global_device_ids=true, to_apply=%region_0.0 | all-reduce | flops 1024 | bytes 8192 | tf_op jit(solution)/shard_map/psum | solution.py:299
  42.1 3.1 %collective-permute-start = (bf16[4,4,16,512]{3,2,1,0:T(8,128)(2,1)S(1)}, bf16[4,4,16,512]{3,2,1,0:T(8,128)(2,1)S(1)}, u32[]{:S(2)}, u32[]{:S(2)}) collective-permute-start(bf16[4,4,16,512]{3,2,1,0:T(8,128)(2,1)S(1)} %bitcast.14), channel_id=1, source_target_pairs={{0,8},{8,16},{16,24},{24,0},{1,9},{9,17},{17,25},{25,1},{2,10},{10... | collective-permute-start | bytes 786440 | tf_op jit(solution)/shard_map/ppermute | solution.py:276
  45.2 4.4 %collective-permute-start.1 = (bf16[4,4,16,512]{3,2,1,0:T(8,128)(2,1)S(1)}, bf16[4,4,16,512]{3,2,1,0:T(8,128)(2,1)S(1)}, u32[]{:S(2)}, u32[]{:S(2)}) collective-permute-start(bf16[4,4,16,512]{3,2,1,0:T(8,128)(2,1)S(1)} %bitcast.15), channel_id=1, source_target_pairs={{0,16},{8,24},{16,0},{24,8},{1,17},{9,25},{17,1},{25,9},{2,18},{10... | collective-permute-start | bytes 786440 | tf_op jit(solution)/shard_map/ppermute | solution.py:276
  49.6 3.0 %collective-permute-start.2 = (bf16[4,4,16,512]{3,2,1,0:T(8,128)(2,1)S(1)}, bf16[4,4,16,512]{3,2,1,0:T(8,128)(2,1)S(1)}, u32[]{:S(2)}, u32[]{:S(2)}) collective-permute-start(bf16[4,4,16,512]{3,2,1,0:T(8,128)(2,1)S(1)} %bitcast.16), channel_id=1, source_target_pairs={{0,24},{8,0},{16,8},{24,16},{1,25},{9,1},{17,9},{25,17},{2,26},{10... | collective-permute-start | bytes 786440 | tf_op jit(solution)/shard_map/ppermute | solution.py:276
  52.7 5.0 %shard_map.96 = f32[4,4,4,16,512]{4,3,2,1,0:T(8,128)} custom-call(bf16[8,128,1024]{2,1,0:T(8,128)(2,1)} %bitcast.24, bf16[1024,512]{1,0:T(8,128)(2,1)} %copy-done.3), custom_call_target="tpu_custom_call" | custom-call | tf_op jit(solution)/shard_map/pallas_call | solution.py:33
  57.7 2.1 %collective-permute-done.2.refs_3_ = bf16[4,4,16,512]{3,2,1,0:T(8,128)(2,1)S(1)} collective-permute-done((bf16[4,4,16,512]{3,2,1,0:T(8,128)(2,1)S(1)}, bf16[4,4,16,512]{3,2,1,0:T(8,128)(2,1)S(1)}, u32[]{:S(2)}, u32[]{:S(2)}) %collective-permute-start.2) | collective-permute-done | bytes 262176 | tf_op jit(solution)/shard_map/ppermute | solution.py:276
  59.8 4.7 %shard_map.97 = (f32[1024,512]{1,0:T(8,128)}, f32[8,8,128]{2,1,0:T(8,128)}, f32[1,512]{1,0:T(1,128)S(1)}) custom-call(s32[1]{0:T(128)} %bitcast.5.me_ref, bf16[8,128,1024]{2,1,0:T(8,128)(2,1)} %bitcast.25, bf16[1024,512]{1,0:T(8,128)(2,1)} %refs_5_.1, bf16[1024,512]{1,0:T(8,128)(2,1)} %grad_ref.1, f32[1,512]{1,0:T(1,128)S(1)} %bitcast.21, ...), custom_call_target="tpu_custom_call" | custom-call | flops 4000000000 | bytes 10000000 | tf_op jit(solution)/shard_map/pallas_call | solution.py:33
  64.6 6.7 %all-to-all-start.1 = ((f32[8,8,128]{2,1,0:T(8,128)}), f32[8,8,128]{2,1,0:T(8,128)S(1)}, u32[]{:S(2)}, u32[]{:S(2)}) async-start(f32[8,8,128]{2,1,0:T(8,128)} %get-tuple-element.28), calls=%async_computation.2 | async-start | bytes 65536 | tf_op jit(solution)/shard_map/all_to_all | solution.py:357
  71.6 4.4 %all-to-all-done.1.refs_1_ = f32[8,8,128]{2,1,0:T(8,128)S(1)} async-done(((f32[8,8,128]{2,1,0:T(8,128)}), f32[8,8,128]{2,1,0:T(8,128)S(1)}, u32[]{:S(2)}, u32[]{:S(2)}) %all-to-all-start.1) | async-done | bytes 32800 | tf_op jit(solution)/shard_map/all_to_all | solution.py:357
  76.0 5.5 %shard_map.99 = bf16[8,320,512]{2,1,0:T(8,128)(2,1)} custom-call(f32[8,128]{1,0:T(8,128)S(1)} %get-tuple-element.26.given_ref.refs_0_, f32[8,8,128]{2,1,0:T(8,128)S(1)} %all-to-all-done.1.refs_1_, s32[8,1024]{1,0:T(8,128)S(1)} %get-tuple-element.29.refs_2_, f32[8,1024]{1,0:T(8,128)S(1)} %get-tuple-element.30.refs_3_, f32[1024,512]{1,0:T(8,128)} %get-tuple-element.31.refs_4_, ...), custom_call_target="tpu_custom_call" | custom-call | flops 20000000000 | bytes 10000000 | tf_op jit(solution)/shard_map/pallas_call | solution.py:33
  81.5 5.1 %all-to-all-start.3 = ((bf16[8,320,512]{2,1,0:T(8,128)(2,1)}), bf16[8,320,512]{2,1,0:T(8,128)(2,1)}, u32[]{:S(2)}, u32[]{:S(2)}) async-start(bf16[8,320,512]{2,1,0:T(8,128)(2,1)} %shard_map.99), calls=%async_computation.4 | async-start | bytes 5242880 | tf_op jit(solution)/shard_map/all_to_all | solution.py:383
  86.6 9.1 %psum.15.d_gain_ref = f32[1,512]{1,0:T(1,128)S(1)} all-reduce(f32[1,512]{1,0:T(1,128)S(1)} %get-tuple-element.33), channel_id=1, replica_groups=mesh['zh'=4,'zl'=4,'x'=4,'y'=4,'core'=2] {'x'}, use_global_device_ids=true, to_apply=%region_2.0 | all-reduce | flops 512 | bytes 4096 | tf_op jit(solution)/shard_map/psum | solution.py:385
  95.8 1.0 copy-done.4
  96.9 3.8 %collective-permute-start.3 = (bf16[80,512]{1,0:T(8,128)(2,1)S(1)}, bf16[80,512]{1,0:T(8,128)(2,1)S(1)}, u32[]{:S(2)}, u32[]{:S(2)}) collective-permute-start(bf16[80,512]{1,0:T(8,128)(2,1)S(1)} %get-tuple-element.35), channel_id=1, source_target_pairs={{0,32},{32,64},{64,96},{96,0},{1,33},{33,65},{65,97},{97,1},{2,34}... | collective-permute-start | bytes 245768 | tf_op jit(solution)/shard_map/ppermute | solution.py:276
  100.7 3.6 %collective-permute-start.4 = (bf16[80,512]{1,0:T(8,128)(2,1)S(1)}, bf16[80,512]{1,0:T(8,128)(2,1)S(1)}, u32[]{:S(2)}, u32[]{:S(2)}) collective-permute-start(bf16[80,512]{1,0:T(8,128)(2,1)S(1)} %get-tuple-element.36), channel_id=1, source_target_pairs={{0,64},{32,96},{64,0},{96,32},{1,65},{33,97},{65,1},{97,33},{2,66}... | collective-permute-start | bytes 245768 | tf_op jit(solution)/shard_map/ppermute | solution.py:276
  104.4 3.0 %collective-permute-start.5 = (bf16[80,512]{1,0:T(8,128)(2,1)S(1)}, bf16[80,512]{1,0:T(8,128)(2,1)S(1)}, u32[]{:S(2)}, u32[]{:S(2)}) collective-permute-start(bf16[80,512]{1,0:T(8,128)(2,1)S(1)} %get-tuple-element.37), channel_id=1, source_target_pairs={{0,96},{32,0},{64,32},{96,64},{1,97},{33,1},{65,33},{97,65},{2,98}... | collective-permute-start | bytes 245768 | tf_op jit(solution)/shard_map/ppermute | solution.py:276
  108.1 2.0 %collective-permute-done.5.d_ref = bf16[80,512]{1,0:T(8,128)(2,1)S(1)} collective-permute-done((bf16[80,512]{1,0:T(8,128)(2,1)S(1)}, bf16[80,512]{1,0:T(8,128)(2,1)S(1)}, u32[]{:S(2)}, u32[]{:S(2)}) %collective-permute-start.5) | collective-permute-done | bytes 81952 | tf_op jit(solution)/shard_map/ppermute | solution.py:276
  110.8 7.9 %all-to-all-done.3 = bf16[8,320,512]{2,1,0:T(8,128)(2,1)} async-done(((bf16[8,320,512]{2,1,0:T(8,128)(2,1)}), bf16[8,320,512]{2,1,0:T(8,128)(2,1)}, u32[]{:S(2)}, u32[]{:S(2)}) %all-to-all-start.3) | async-done | bytes 2621472 | tf_op jit(solution)/shard_map/all_to_all | solution.py:383
  118.6 10.6 %all-to-all-start.2 = ((bf16[4,16,640]{2,1,0:T(8,128)(2,1)}), bf16[4,16,640]{2,1,0:T(8,128)(2,1)S(1)}, u32[]{:S(2)}, u32[]{:S(2)}) async-start(bf16[4,16,640]{2,1,0:T(8,128)(2,1)} %shard_map.101), calls=%async_computation.3 | async-start | bytes 163840 | tf_op jit(solution)/shard_map/all_to_all | solution.py:397
  129.3 3.6 %copy.11 = bf16[1,8,40,8,512]{4,3,1,2,0:T(8,128)(2,1)} copy(bf16[1,8,40,8,512]{4,3,2,1,0:T(8,128)(2,1)} %bitcast.12) | data formatting | bytes 5242880 | tf_op jit(solution)/shard_map/all_to_all | solution.py:383
  132.9 8.2 %all-to-all-done.2.refs_0_ = bf16[4,16,640]{2,1,0:T(8,128)(2,1)S(1)} async-done(((bf16[4,16,640]{2,1,0:T(8,128)(2,1)}), bf16[4,16,640]{2,1,0:T(8,128)(2,1)S(1)}, u32[]{:S(2)}, u32[]{:S(2)}) %all-to-all-start.2) | async-done | bytes 81952 | tf_op jit(solution)/shard_map/all_to_all | solution.py:397
  (33 shorter events, 5.8 us)
Async XLA Ops:
  7.2 32.8 %copy-start.1 = (bf16[1024,512]{1,0:T(8,128)(2,1)S(1)}, bf16[1024,512]{1,0:T(8,128)(2,1)}, u32[]{:S(2)}) copy-start(bf16[1024,512]{1,0:T(8,128)(2,1)} %refs_5_.1) | copy-start | bytes 3145732
  7.2 45.5 %all-gather.3.cloned.1.call-start = ((), (), s32[]{:S(2)}) async-start(), calls=%async_computation.6 | async-start | bytes 2359296 | tf_op jit(solution)/shard_map/all_gather | solution.py:293
  9.4 32.7 %all-to-all-start = ((bf16[16,16,512]{2,1,0:T(8,128)(2,1)}), bf16[16,16,512]{2,1,0:T(8,128)(2,1)S(1)}, u32[]{:S(2)}, u32[]{:S(2)}) async-start(bf16[16,16,512]{2,1,0:T(8,128)(2,1)} %broadcast_in_dim.4), calls=%async_computation | async-start | bytes 524288 | tf_op jit(solution)/shard_map/all_to_all | solution.py:296
  25.1 70.7 %reduce-scatter.2.cloned.1.call-start = ((), (), s32[]{:S(2)}) async-start(), calls=%async_computation.5 | async-start | bytes 2621440 | tf_op jit(solution)/shard_map/reduce_scatter | solution.py:328
  25.2 1.2 copy-start
  40.0 0.7 copy-start.7
  41.1 1.0 copy-start.3
  42.1 10.6 %collective-permute-start = (bf16[4,4,16,512]{3,2,1,0:T(8,128)(2,1)S(1)}, bf16[4,4,16,512]{3,2,1,0:T(8,128)(2,1)S(1)}, u32[]{:S(2)}, u32[]{:S(2)}) collective-permute-start(bf16[4,4,16,512]{3,2,1,0:T(8,128)(2,1)S(1)} %bitcast.14), channel_id=1, source_target_pairs={{0,8},{8,16},{16,24},{24,0},{1,9},{9,17},{17,25},{25,1},{2,10},{10... | collective-permute-start | bytes 786440 | tf_op jit(solution)/shard_map/ppermute | solution.py:276
  45.2 12.5 %collective-permute-start.1 = (bf16[4,4,16,512]{3,2,1,0:T(8,128)(2,1)S(1)}, bf16[4,4,16,512]{3,2,1,0:T(8,128)(2,1)S(1)}, u32[]{:S(2)}, u32[]{:S(2)}) collective-permute-start(bf16[4,4,16,512]{3,2,1,0:T(8,128)(2,1)S(1)} %bitcast.15), channel_id=1, source_target_pairs={{0,16},{8,24},{16,0},{24,8},{1,17},{9,25},{17,1},{25,9},{2,18},{10... | collective-permute-start | bytes 786440 | tf_op jit(solution)/shard_map/ppermute | solution.py:276
  49.6 10.2 %collective-permute-start.2 = (bf16[4,4,16,512]{3,2,1,0:T(8,128)(2,1)S(1)}, bf16[4,4,16,512]{3,2,1,0:T(8,128)(2,1)S(1)}, u32[]{:S(2)}, u32[]{:S(2)}) collective-permute-start(bf16[4,4,16,512]{3,2,1,0:T(8,128)(2,1)S(1)} %bitcast.16), channel_id=1, source_target_pairs={{0,24},{8,0},{16,8},{24,16},{1,25},{9,1},{17,9},{25,17},{2,26},{10... | collective-permute-start | bytes 786440 | tf_op jit(solution)/shard_map/ppermute | solution.py:276
  52.7 7.2 %copy-start.8 = (f32[512]{0:T(512)S(1)}, f32[512]{0:T(512)}, u32[]{:S(2)}) copy-start(f32[512]{0:T(512)} %param.10) | copy-start | bytes 6148
  59.8 11.5 %copy-start.5 = (s32[1024,2]{0,1:T(2,128)S(1)}, s32[1024,2]{0,1:T(2,128)}, u32[]{:S(2)}) copy-start(s32[1024,2]{0,1:T(2,128)} %param.13) | copy-start | bytes 24580
  59.8 11.5 %copy-start.6 = (f32[1024,2]{0,1:T(2,128)S(1)}, f32[1024,2]{0,1:T(2,128)}, u32[]{:S(2)}) copy-start(f32[1024,2]{0,1:T(2,128)} %param.12) | copy-start | bytes 24580
  59.8 16.2 %copy-start.2 = (bf16[1024,512]{1,0:T(8,128)(2,1)S(1)}, bf16[1024,512]{1,0:T(8,128)(2,1)}, u32[]{:S(2)}) copy-start(bf16[1024,512]{1,0:T(8,128)(2,1)} %refs_5_.1) | copy-start | bytes 3145732
  64.6 11.4 %all-to-all-start.1 = ((f32[8,8,128]{2,1,0:T(8,128)}), f32[8,8,128]{2,1,0:T(8,128)S(1)}, u32[]{:S(2)}, u32[]{:S(2)}) async-start(f32[8,8,128]{2,1,0:T(8,128)} %get-tuple-element.28), calls=%async_computation.2 | async-start | bytes 65536 | tf_op jit(solution)/shard_map/all_to_all | solution.py:357
  81.5 37.1 %all-to-all-start.3 = ((bf16[8,320,512]{2,1,0:T(8,128)(2,1)}), bf16[8,320,512]{2,1,0:T(8,128)(2,1)}, u32[]{:S(2)}, u32[]{:S(2)}) async-start(bf16[8,320,512]{2,1,0:T(8,128)(2,1)} %shard_map.99), calls=%async_computation.4 | async-start | bytes 5242880 | tf_op jit(solution)/shard_map/all_to_all | solution.py:383
  95.8 1.0 copy-start.4
  96.9 10.4 %collective-permute-start.3 = (bf16[80,512]{1,0:T(8,128)(2,1)S(1)}, bf16[80,512]{1,0:T(8,128)(2,1)S(1)}, u32[]{:S(2)}, u32[]{:S(2)}) collective-permute-start(bf16[80,512]{1,0:T(8,128)(2,1)S(1)} %get-tuple-element.35), channel_id=1, source_target_pairs={{0,32},{32,64},{64,96},{96,0},{1,33},{33,65},{65,97},{97,1},{2,34}... | collective-permute-start | bytes 245768 | tf_op jit(solution)/shard_map/ppermute | solution.py:276
  100.7 7.4 %collective-permute-start.4 = (bf16[80,512]{1,0:T(8,128)(2,1)S(1)}, bf16[80,512]{1,0:T(8,128)(2,1)S(1)}, u32[]{:S(2)}, u32[]{:S(2)}) collective-permute-start(bf16[80,512]{1,0:T(8,128)(2,1)S(1)} %get-tuple-element.36), channel_id=1, source_target_pairs={{0,64},{32,96},{64,0},{96,32},{1,65},{33,97},{65,1},{97,33},{2,66}... | collective-permute-start | bytes 245768 | tf_op jit(solution)/shard_map/ppermute | solution.py:276
  104.4 5.7 %collective-permute-start.5 = (bf16[80,512]{1,0:T(8,128)(2,1)S(1)}, bf16[80,512]{1,0:T(8,128)(2,1)S(1)}, u32[]{:S(2)}, u32[]{:S(2)}) collective-permute-start(bf16[80,512]{1,0:T(8,128)(2,1)S(1)} %get-tuple-element.37), channel_id=1, source_target_pairs={{0,96},{32,0},{64,32},{96,64},{1,97},{33,1},{65,33},{97,65},{2,98}... | collective-permute-start | bytes 245768 | tf_op jit(solution)/shard_map/ppermute | solution.py:276
  118.6 22.4 %all-to-all-start.2 = ((bf16[4,16,640]{2,1,0:T(8,128)(2,1)}), bf16[4,16,640]{2,1,0:T(8,128)(2,1)S(1)}, u32[]{:S(2)}, u32[]{:S(2)}) async-start(bf16[4,16,640]{2,1,0:T(8,128)(2,1)} %shard_map.101), calls=%async_computation.3 | async-start | bytes 163840 | tf_op jit(solution)/shard_map/all_to_all | solution.py:397
Sparse Core Ops, SparseCore 0:
  10.2 38.6 all-gather.2
  57.8 37.9 reduce-scatter.1

commit v11 on v9

--- a/solution.py
+++ b/solution.py
@@ -245,13 +245,15 @@
         out[rows:, :] = behind
 
 
-def high_split_kernel(a_ref, b_ref, c_ref, d_ref, out_ref):
+def high_split_kernel(me_ref, a_ref, b_ref, c_ref, d_ref, *refs):
+    outs, total_ref = refs[:-1], refs[-1]
     total = a_ref[...].astype(jnp.float32)
     for ref in (b_ref, c_ref, d_ref):
         total += ref[...].astype(jnp.float32)
-    count, own, _ = out_ref.shape
+    count, own = len(outs), outs[0].shape[0]
     columns = total.shape[1]
     rows = total.shape[0] - PAD
+    total_ref[...] = total
     gain = jnp.sum(total[rows:, :], axis=0, keepdims=True)
     parts = pieces(gain).astype(jnp.float32)
     blocks = columns // 128
@@ -261,15 +263,16 @@
         for block in range(blocks):
             row = parts[part : part + 1, block * 128 : (block + 1) * 128]
             behind = jnp.where(at == part * blocks + block, row, behind)
-    for to in range(count):
-        out_ref[to, :, 0:columns] = total[to * own : (to + 1) * own, :].astype(jnp.bfloat16)
-        out_ref[to, :, columns:] = behind.astype(jnp.bfloat16)
-
-
-def finish_kernel(rescale, parts_ref, d_value_ref, d_gain_ref):
-    total = parts_ref[0].astype(jnp.float32)
-    for at in range(1, parts_ref.shape[0]):
-        total += parts_ref[at].astype(jnp.float32)
+    for k, out in enumerate(outs):
+        start = pl.multiple_of(lax.rem(me_ref[0] + k, count) * own, own)
+        out[:, 0:columns] = total_ref[pl.ds(start, own), :].astype(jnp.bfloat16)
+        out[:, columns:] = behind.astype(jnp.bfloat16)
+
+
+def finish_kernel(rescale, a_ref, b_ref, c_ref, d_ref, d_value_ref, d_gain_ref):
+    total = a_ref[...].astype(jnp.float32)
+    for ref in (b_ref, c_ref, d_ref):
+        total += ref[...].astype(jnp.float32)
     columns = d_value_ref.shape[1]
     d_value_ref[...] = (total[:, 0:columns] * rescale).astype(jnp.bfloat16)
     blocks = columns // 128
@@ -405,12 +408,14 @@
         scratch=[pltpu.VMEM((features // xs, columns), f32), pltpu.SemaphoreType.DMA(())],
     )
     parts = [parts[0]] + [further(parts[k], "zl", k) for k in range(1, zl)]
-    (parts,) = call(
-        high_split_kernel, *parts, out=[((zh, rows, columns + 128), bf16)], limit=8,
-    )
-    parts = lax.all_to_all(parts, "zh", 0, 0, tiled=True)
+    parts = call(
+        high_split_kernel, lax.axis_index("zh").reshape(1), *parts,
+        out=[((rows, columns + 128), bf16)] * zh, limit=8,
+        scratch=[pltpu.VMEM(parts[0].shape, f32)],
+    )
+    parts = [parts[0]] + [further(parts[k], "zh", k) for k in range(1, zh)]
     d_value, d_gain = call(
-        lambda *refs: finish_kernel(rescale, *refs), parts,
+        lambda *refs: finish_kernel(rescale, *refs), *parts,
         out=[((rows, columns), bf16), ((1, columns), f32)], limit=8,
     )
     return (d_value, d_gain.reshape(columns), arrived)

time: 149 us -> 143 us (0.960)
  waiting for transfers between devices: 24.7 us -> 8.95 us
  starting transfers between devices: 45.3 us -> 56 us
    ppermute x6 -> x9, starting transfers between devices: 21.7 us -> 39.9 us  [further(): lax.ppermute(part, axis, [(i, (i + step) % size) for i in range(size)])]
    all_to_all x1 -> x0, waiting for transfers between devices: 8.96 us -> none  [on_device(): parts = lax.all_to_all(parts, 'zh', 0, 0, tiled=True)]
    all_to_all x1 -> x0, starting transfers between devices: 7.6 us -> none  [on_device(): parts = lax.all_to_all(parts, 'zh', 0, 0, tiled=True)]
    all_to_all x1, waiting for transfers between devices: 6.77 us -> 0.01 us  [on_device(): lax.all_to_all(sent, EXPERT, split_axis=0, concat_axis=2, tiled=True)]
    ppermute x6 -> x9, waiting for transfers between devices: 3.87 us -> 3.88 us  [further(): lax.ppermute(part, axis, [(i, (i + step) % size) for i in range(size)])]
  transfers between devices with their start and end apart: 11 -> 13, of which waited for: 6 -> 4; matrix products, arithmetic and copies ran while one was open for 2% -> 3% of each run, Pallas kernels for 11% -> 12%
where the time goes in v11:
time: 143 us; the launch traced here: 141 us
  starting transfers between devices  56 us (39%)
  blocking collectives  37.3 us (26%)
  Pallas kernels  19.3 us (13%)
  between operations  14.2 us (10%)
  waiting for transfers between devices  8.95 us (6%)
  local copies, waits for them, and re-layouts  5.33 us (4%)
    ppermute x9, starting transfers between devices, further(): lax.ppermute(part, axis, [(i, (i + step) % size) for i in range(size)])  39.9 us
    all_to_all x1, blocking collectives, on_device(): weight = lax.all_to_all(copies, ('zh', 'zl'), 0, 0, tiled=True)  28.9 us
    pallas_call x8, Pallas kernels, call(): pl.pallas_call(kernel, grid=(grid,), in_specs=in_specs or [SMEM if o.shap...  19.3 us
    all_to_all x1, starting transfers between devices, on_device(): inner = lax.all_to_all(inner, EXPERT, 0, 0, tiled=True)  10.9 us
    psum x1, blocking collectives, on_device(): d_gain = lax.psum(own_gain, 'x')  8.42 us
    all_to_all x1, starting transfers between devices, on_device(): lax.all_to_all(sent, EXPERT, split_axis=0, concat_axis=2, tiled=True)  5.03 us
    all_to_all x1, waiting for transfers between devices, on_device(): inner = lax.all_to_all(inner, EXPERT, 0, 0, tiled=True)  4.42 us
    ppermute x9, waiting for transfers between devices, further(): lax.ppermute(part, axis, [(i, (i + step) % size) for i in range(size)])  3.88 us
  transfers between devices with their start and end apart: 13, of which 4 were waited for; matrix products, arithmetic and copies ran while one was open for 3% of the time, Pallas kernels for 12%

profile of v11, /device:TPU:1, one launch (start us, length us, event | category | flops | bytes accessed | tf_op | source)
XLA Modules:
  0.0 141.1 jit_solution(259526243920364038)
XLA Ops:
  7.2 2.4 %shard_map.94 = (bf16[144,1024]{1,0:T(8,128)(2,1)}, bf16[16,16,512]{2,1,0:T(8,128)(2,1)}) custom-call(bf16[128,1024]{1,0:T(8,128)(2,1)} %value_ref.1, bf16[1024,512]{1,0:T(8,128)(2,1)} %refs_5_.1, bf16[16,512]{1,0:T(8,128)(2,1)} %weight_ref.1), custom_call_target="tpu_custom_call" | custom-call | tf_op jit(solution)/shard_map/pallas_call | solution.py:33
  9.7 28.9 %all_to_all.28 = bf16[16,16,512]{2,1,0:T(8,128)(2,1)S(1)} all-to-all(bf16[16,16,512]{2,1,0:T(8,128)(2,1)} %get-tuple-element.27), channel_id=1, replica_groups=mesh['zh'=4,'zl'=4,'x'=4,'y'=4,'core'=2] {'zh','zl'}, dimensions={0} | all-to-all | bytes 524288 | tf_op jit(solution)/shard_map/all_to_all | solution.py:319
  38.6 3.1 %collective-permute-start = (bf16[4,4,16,512]{3,2,1,0:T(8,128)(2,1)S(1)}, bf16[4,4,16,512]{3,2,1,0:T(8,128)(2,1)S(1)}, u32[]{:S(2)}, u32[]{:S(2)}) collective-permute-start(bf16[4,4,16,512]{3,2,1,0:T(8,128)(2,1)S(1)} %bitcast.15), channel_id=1, source_target_pairs={{0,8},{8,16},{16,24},{24,0},{1,9},{9,17},{17,25},{25,1},{2,10},{10... | collective-permute-start | bytes 786440 | tf_op jit(solution)/shard_map/ppermute | solution.py:296
  41.7 4.4 %collective-permute-start.1 = (bf16[4,4,16,512]{3,2,1,0:T(8,128)(2,1)S(1)}, bf16[4,4,16,512]{3,2,1,0:T(8,128)(2,1)S(1)}, u32[]{:S(2)}, u32[]{:S(2)}) collective-permute-start(bf16[4,4,16,512]{3,2,1,0:T(8,128)(2,1)S(1)} %bitcast.16), channel_id=1, source_target_pairs={{0,16},{8,24},{16,0},{24,8},{1,17},{9,25},{17,1},{25,9},{2,18},{10... | collective-permute-start | bytes 786440 | tf_op jit(solution)/shard_map/ppermute | solution.py:296
  46.1 3.1 %collective-permute-start.2 = (bf16[4,4,16,512]{3,2,1,0:T(8,128)(2,1)S(1)}, bf16[4,4,16,512]{3,2,1,0:T(8,128)(2,1)S(1)}, u32[]{:S(2)}, u32[]{:S(2)}) collective-permute-start(bf16[4,4,16,512]{3,2,1,0:T(8,128)(2,1)S(1)} %bitcast.17), channel_id=1, source_target_pairs={{0,24},{8,0},{16,8},{24,16},{1,25},{9,1},{17,9},{25,17},{2,26},{10... | collective-permute-start | bytes 786440 | tf_op jit(solution)/shard_map/ppermute | solution.py:296
  49.8 5.5 %shard_map.95 = (f32[4,4,4,16,512]{4,3,2,1,0:T(8,128)}, f32[8,128]{1,0:T(8,128)}) custom-call(bf16[8,144,1024]{2,1,0:T(8,128)(2,1)} %bitcast.24, bf16[1024,512]{1,0:T(8,128)(2,1)} %refs_5_.1, f32[1,512]{1,0:T(1,128)} %bitcast.21), custom_call_target="tpu_custom_call" | custom-call | tf_op jit(solution)/shard_map/pallas_call | solution.py:33
  55.4 0.7 copy-done.5
  56.0 4.8 %shard_map.96 = (f32[1024,512]{1,0:T(8,128)}, f32[8,8,128]{2,1,0:T(8,128)}, f32[1,512]{1,0:T(1,128)S(1)}) custom-call(s32[1]{0:T(128)} %bitcast.6.me_ref, bf16[8,144,1024]{2,1,0:T(8,128)(2,1)} %bitcast.25, bf16[1024,512]{1,0:T(8,128)(2,1)} %refs_5_.1, bf16[1024,512]{1,0:T(8,128)(2,1)} %grad_ref.1, f32[1,512]{1,0:T(1,128)S(1)} %bitcast.22, ...), custom_call_target="tpu_custom_call" | custom-call | flops 4000000000 | bytes 10000000 | tf_op jit(solution)/shard_map/pallas_call | solution.py:33
  60.8 10.9 %all-to-all-start.1 = ((f32[8,8,128]{2,1,0:T(8,128)}), f32[8,8,128]{2,1,0:T(8,128)S(1)}, u32[]{:S(2)}, u32[]{:S(2)}) async-start(f32[8,8,128]{2,1,0:T(8,128)} %get-tuple-element.32), calls=%async_computation.2 | async-start | bytes 65536 | tf_op jit(solution)/shard_map/all_to_all | solution.py:374
  72.1 4.4 %all-to-all-done.1.refs_1_ = f32[8,8,128]{2,1,0:T(8,128)S(1)} async-done(((f32[8,8,128]{2,1,0:T(8,128)}), f32[8,8,128]{2,1,0:T(8,128)S(1)}, u32[]{:S(2)}, u32[]{:S(2)}) %all-to-all-start.1) | async-done | bytes 32800 | tf_op jit(solution)/shard_map/all_to_all | solution.py:374
  76.5 5.5 %shard_map.98 = bf16[8,320,512]{2,1,0:T(8,128)(2,1)} custom-call(f32[8,128]{1,0:T(8,128)S(1)} %copy-done.6, f32[8,8,128]{2,1,0:T(8,128)S(1)} %all-to-all-done.1.refs_1_, s32[8,1024]{1,0:T(8,128)S(1)} %get-tuple-element.33.refs_2_, f32[8,1024]{1,0:T(8,128)S(1)} %get-tuple-element.34.refs_3_, f32[1024,512]{1,0:T(8,128)} %get-tuple-element.35.refs_4_, ...), custom_call_target="tpu_custom_call" | custom-call | flops 20000000000 | bytes 10000000 | tf_op jit(solution)/shard_map/pallas_call | solution.py:33
  82.0 5.0 %all-to-all-start.2 = ((bf16[8,320,512]{2,1,0:T(8,128)(2,1)}), bf16[8,320,512]{2,1,0:T(8,128)(2,1)}, u32[]{:S(2)}, u32[]{:S(2)}) async-start(bf16[8,320,512]{2,1,0:T(8,128)(2,1)} %shard_map.98), calls=%async_computation.3 | async-start | bytes 5242880 | tf_op jit(solution)/shard_map/all_to_all | solution.py:400
  87.0 8.4 %psum.7.d_gain_ref = f32[1,512]{1,0:T(1,128)S(1)} all-reduce(f32[1,512]{1,0:T(1,128)S(1)} %get-tuple-element.37), channel_id=1, replica_groups=mesh['zh'=4,'zl'=4,'x'=4,'y'=4,'core'=2] {'x'}, use_global_device_ids=true, to_apply=%region_1.0 | all-reduce | flops 512 | bytes 4096 | tf_op jit(solution)/shard_map/psum | solution.py:402
  95.5 1.0 copy-done.1
  96.6 5.2 %collective-permute-start.3 = (bf16[80,512]{1,0:T(8,128)(2,1)S(1)}, bf16[80,512]{1,0:T(8,128)(2,1)S(1)}, u32[]{:S(2)}, u32[]{:S(2)}) collective-permute-start(bf16[80,512]{1,0:T(8,128)(2,1)S(1)} %get-tuple-element.39), channel_id=1, source_target_pairs={{0,32},{32,64},{64,96},{96,0},{1,33},{33,65},{65,97},{97,1},{2,34}... | collective-permute-start | bytes 245768 | tf_op jit(solution)/shard_map/ppermute | solution.py:296
  101.8 3.6 %collective-permute-start.4 = (bf16[80,512]{1,0:T(8,128)(2,1)S(1)}, bf16[80,512]{1,0:T(8,128)(2,1)S(1)}, u32[]{:S(2)}, u32[]{:S(2)}) collective-permute-start(bf16[80,512]{1,0:T(8,128)(2,1)S(1)} %get-tuple-element.40), channel_id=1, source_target_pairs={{0,64},{32,96},{64,0},{96,32},{1,65},{33,97},{65,1},{97,33},{2,66}... | collective-permute-start | bytes 245768 | tf_op jit(solution)/shard_map/ppermute | solution.py:296
  105.4 2.3 %collective-permute-start.5 = (bf16[80,512]{1,0:T(8,128)(2,1)S(1)}, bf16[80,512]{1,0:T(8,128)(2,1)S(1)}, u32[]{:S(2)}, u32[]{:S(2)}) collective-permute-start(bf16[80,512]{1,0:T(8,128)(2,1)S(1)} %get-tuple-element.41), channel_id=1, source_target_pairs={{0,96},{32,0},{64,32},{96,64},{1,97},{33,1},{65,33},{97,65},{2,98}... | collective-permute-start | bytes 245768 | tf_op jit(solution)/shard_map/ppermute | solution.py:296
  107.8 1.1 collective-permute-done.4.c_ref
  108.9 2.7 %collective-permute-done.5.d_ref = bf16[80,512]{1,0:T(8,128)(2,1)S(1)} collective-permute-done((bf16[80,512]{1,0:T(8,128)(2,1)S(1)}, bf16[80,512]{1,0:T(8,128)(2,1)S(1)}, u32[]{:S(2)}, u32[]{:S(2)}) %collective-permute-start.5) | collective-permute-done | bytes 81952 | tf_op jit(solution)/shard_map/ppermute | solution.py:296
  111.7 4.7 %collective-permute-start.6 = (bf16[16,640]{1,0:T(8,128)(2,1)S(1)}, bf16[16,640]{1,0:T(8,128)(2,1)S(1)}, u32[]{:S(2)}, u32[]{:S(2)}) collective-permute-start(bf16[16,640]{1,0:T(8,128)(2,1)S(1)} %get-tuple-element.43), channel_id=1, source_target_pairs={{0,128},{128,256},{256,384},{384,0},{1,129},{129,257},{257,385},{3... | collective-permute-start | bytes 61448 | tf_op jit(solution)/shard_map/ppermute | solution.py:296
  116.4 6.8 %collective-permute-start.7 = (bf16[16,640]{1,0:T(8,128)(2,1)S(1)}, bf16[16,640]{1,0:T(8,128)(2,1)S(1)}, u32[]{:S(2)}, u32[]{:S(2)}) collective-permute-start(bf16[16,640]{1,0:T(8,128)(2,1)S(1)} %get-tuple-element.44), channel_id=1, source_target_pairs={{0,256},{128,384},{256,0},{384,128},{1,257},{129,385},{257,1},{385... | collective-permute-start | bytes 61448 | tf_op jit(solution)/shard_map/ppermute | solution.py:296
  123.3 6.7 %collective-permute-start.8 = (bf16[16,640]{1,0:T(8,128)(2,1)S(1)}, bf16[16,640]{1,0:T(8,128)(2,1)S(1)}, u32[]{:S(2)}, u32[]{:S(2)}) collective-permute-start(bf16[16,640]{1,0:T(8,128)(2,1)S(1)} %get-tuple-element.45), channel_id=1, source_target_pairs={{0,384},{128,0},{256,128},{384,256},{1,385},{129,1},{257,129},{385... | collective-permute-start | bytes 61448 | tf_op jit(solution)/shard_map/ppermute | solution.py:296
  130.0 3.6 %copy.11 = bf16[1,8,40,8,512]{4,3,1,2,0:T(8,128)(2,1)} copy(bf16[1,8,40,8,512]{4,3,2,1,0:T(8,128)(2,1)} %bitcast.13) | data formatting | bytes 5242880 | tf_op jit(solution)/shard_map/all_to_all | solution.py:400
  133.6 0.6 shard_map.101
  (29 shorter events, 1.2 us)
Async XLA Ops:
  7.2 42.6 %all-gather.3.cloned.1.call-start = ((), (), s32[]{:S(2)}) async-start(), calls=%async_computation.5 | async-start | bytes 2654208 | tf_op jit(solution)/shard_map/all_gather | solution.py:317
  9.6 85.8 %reduce-scatter.2.cloned.1.call-start = ((), (), s32[]{:S(2)}) async-start(), calls=%async_computation.4 | async-start | bytes 2621440 | tf_op jit(solution)/shard_map/reduce_scatter | solution.py:345
  38.6 10.6 %collective-permute-start = (bf16[4,4,16,512]{3,2,1,0:T(8,128)(2,1)S(1)}, bf16[4,4,16,512]{3,2,1,0:T(8,128)(2,1)S(1)}, u32[]{:S(2)}, u32[]{:S(2)}) collective-permute-start(bf16[4,4,16,512]{3,2,1,0:T(8,128)(2,1)S(1)} %bitcast.15), channel_id=1, source_target_pairs={{0,8},{8,16},{16,24},{24,0},{1,9},{9,17},{17,25},{25,1},{2,10},{10... | collective-permute-start | bytes 786440 | tf_op jit(solution)/shard_map/ppermute | solution.py:296
  41.7 13.6 %collective-permute-start.1 = (bf16[4,4,16,512]{3,2,1,0:T(8,128)(2,1)S(1)}, bf16[4,4,16,512]{3,2,1,0:T(8,128)(2,1)S(1)}, u32[]{:S(2)}, u32[]{:S(2)}) collective-permute-start(bf16[4,4,16,512]{3,2,1,0:T(8,128)(2,1)S(1)} %bitcast.16), channel_id=1, source_target_pairs={{0,16},{8,24},{16,0},{24,8},{1,17},{9,25},{17,1},{25,9},{2,18},{10... | collective-permute-start | bytes 786440 | tf_op jit(solution)/shard_map/ppermute | solution.py:296
  46.1 9.3 %collective-permute-start.2 = (bf16[4,4,16,512]{3,2,1,0:T(8,128)(2,1)S(1)}, bf16[4,4,16,512]{3,2,1,0:T(8,128)(2,1)S(1)}, u32[]{:S(2)}, u32[]{:S(2)}) collective-permute-start(bf16[4,4,16,512]{3,2,1,0:T(8,128)(2,1)S(1)} %bitcast.17), channel_id=1, source_target_pairs={{0,24},{8,0},{16,8},{24,16},{1,25},{9,1},{17,9},{25,17},{2,26},{10... | collective-permute-start | bytes 786440 | tf_op jit(solution)/shard_map/ppermute | solution.py:296
  49.8 5.6 %copy-start.4 = (f32[512]{0:T(512)S(1)}, f32[512]{0:T(512)}, u32[]{:S(2)}) copy-start(f32[512]{0:T(512)} %param.10) | copy-start | bytes 6148
  55.3 0.7 copy-start.5
  56.0 15.7 %copy-start.2 = (s32[1024,2]{0,1:T(2,128)S(1)}, s32[1024,2]{0,1:T(2,128)}, u32[]{:S(2)}) copy-start(s32[1024,2]{0,1:T(2,128)} %param.13) | copy-start | bytes 24580
  56.0 15.7 %copy-start.3 = (f32[1024,2]{0,1:T(2,128)S(1)}, f32[1024,2]{0,1:T(2,128)}, u32[]{:S(2)}) copy-start(f32[1024,2]{0,1:T(2,128)} %param.12) | copy-start | bytes 24580
  56.0 20.4 %copy-start = (bf16[1024,512]{1,0:T(8,128)(2,1)S(1)}, bf16[1024,512]{1,0:T(8,128)(2,1)}, u32[]{:S(2)}) copy-start(bf16[1024,512]{1,0:T(8,128)(2,1)} %refs_5_.1) | copy-start | bytes 3145732
  56.0 20.4 %copy-start.6 = (f32[8,128]{1,0:T(8,128)S(1)}, f32[8,128]{1,0:T(8,128)}, u32[]{:S(2)}) copy-start(f32[8,128]{1,0:T(8,128)} %get-tuple-element.30.given_ref.refs_0_) | copy-start | bytes 12292
  60.8 15.7 %all-to-all-start.1 = ((f32[8,8,128]{2,1,0:T(8,128)}), f32[8,8,128]{2,1,0:T(8,128)S(1)}, u32[]{:S(2)}, u32[]{:S(2)}) async-start(f32[8,8,128]{2,1,0:T(8,128)} %get-tuple-element.32), calls=%async_computation.2 | async-start | bytes 65536 | tf_op jit(solution)/shard_map/all_to_all | solution.py:374
  82.0 48.0 %all-to-all-start.2 = ((bf16[8,320,512]{2,1,0:T(8,128)(2,1)}), bf16[8,320,512]{2,1,0:T(8,128)(2,1)}, u32[]{:S(2)}, u32[]{:S(2)}) async-start(bf16[8,320,512]{2,1,0:T(8,128)(2,1)} %shard_map.98), calls=%async_computation.3 | async-start | bytes 5242880 | tf_op jit(solution)/shard_map/all_to_all | solution.py:400
  95.4 1.0 copy-start.1
  96.6 11.2 %collective-permute-start.3 = (bf16[80,512]{1,0:T(8,128)(2,1)S(1)}, bf16[80,512]{1,0:T(8,128)(2,1)S(1)}, u32[]{:S(2)}, u32[]{:S(2)}) collective-permute-start(bf16[80,512]{1,0:T(8,128)(2,1)S(1)} %get-tuple-element.39), channel_id=1, source_target_pairs={{0,32},{32,64},{64,96},{96,0},{1,33},{33,65},{65,97},{97,1},{2,34}... | collective-permute-start | bytes 245768 | tf_op jit(solution)/shard_map/ppermute | solution.py:296
  101.8 7.1 %collective-permute-start.4 = (bf16[80,512]{1,0:T(8,128)(2,1)S(1)}, bf16[80,512]{1,0:T(8,128)(2,1)S(1)}, u32[]{:S(2)}, u32[]{:S(2)}) collective-permute-start(bf16[80,512]{1,0:T(8,128)(2,1)S(1)} %get-tuple-element.40), channel_id=1, source_target_pairs={{0,64},{32,96},{64,0},{96,32},{1,65},{33,97},{65,1},{97,33},{2,66}... | collective-permute-start | bytes 245768 | tf_op jit(solution)/shard_map/ppermute | solution.py:296
  105.4 6.2 %collective-permute-start.5 = (bf16[80,512]{1,0:T(8,128)(2,1)S(1)}, bf16[80,512]{1,0:T(8,128)(2,1)S(1)}, u32[]{:S(2)}, u32[]{:S(2)}) collective-permute-start(bf16[80,512]{1,0:T(8,128)(2,1)S(1)} %get-tuple-element.41), channel_id=1, source_target_pairs={{0,96},{32,0},{64,32},{96,64},{1,97},{33,1},{65,33},{97,65},{2,98}... | collective-permute-start | bytes 245768 | tf_op jit(solution)/shard_map/ppermute | solution.py:296
  111.7 21.9 %collective-permute-start.6 = (bf16[16,640]{1,0:T(8,128)(2,1)S(1)}, bf16[16,640]{1,0:T(8,128)(2,1)S(1)}, u32[]{:S(2)}, u32[]{:S(2)}) collective-permute-start(bf16[16,640]{1,0:T(8,128)(2,1)S(1)} %get-tuple-element.43), channel_id=1, source_target_pairs={{0,128},{128,256},{256,384},{384,0},{1,129},{129,257},{257,385},{3... | collective-permute-start | bytes 61448 | tf_op jit(solution)/shard_map/ppermute | solution.py:296
  116.4 17.2 %collective-permute-start.7 = (bf16[16,640]{1,0:T(8,128)(2,1)S(1)}, bf16[16,640]{1,0:T(8,128)(2,1)S(1)}, u32[]{:S(2)}, u32[]{:S(2)}) collective-permute-start(bf16[16,640]{1,0:T(8,128)(2,1)S(1)} %get-tuple-element.44), channel_id=1, source_target_pairs={{0,256},{128,384},{256,0},{384,128},{1,257},{129,385},{257,1},{385... | collective-permute-start | bytes 61448 | tf_op jit(solution)/shard_map/ppermute | solution.py:296
  123.3 10.3 %collective-permute-start.8 = (bf16[16,640]{1,0:T(8,128)(2,1)S(1)}, bf16[16,640]{1,0:T(8,128)(2,1)S(1)}, u32[]{:S(2)}, u32[]{:S(2)}) collective-permute-start(bf16[16,640]{1,0:T(8,128)(2,1)S(1)} %get-tuple-element.45), channel_id=1, source_target_pairs={{0,384},{128,0},{256,128},{384,256},{1,385},{129,1},{257,129},{385... | collective-permute-start | bytes 61448 | tf_op jit(solution)/shard_map/ppermute | solution.py:296
Sparse Core Ops, SparseCore 0:
  10.7 39.0 all-gather.2
  55.4 37.8 reduce-scatter.1

commit v12 on v11

--- a/solution.py
+++ b/solution.py
@@ -13,7 +13,7 @@
 PAD = 16
 VALUE_LIMIT = 62
 NORMED_LIMIT = 52
-DISPATCH_LIMIT = 52
+DISPATCH_LIMIT = 57
 NORMED_FLOPS = 4 * 10**9
 DISPATCH_FLOPS = 20 * 10**9
 

time: 143 us -> 144 us (level)
  the two profiles are of different devices: /device:TPU:1 before, /device:TPU:8 now
where the time goes in v12:
time: 144 us; the launch traced here: 143 us
  starting transfers between devices  49.2 us (34%)
  blocking collectives  43.2 us (30%)
  Pallas kernels  20.5 us (14%)
  between operations  14.3 us (10%)
  waiting for transfers between devices  10.3 us (7%)
  local copies, waits for them, and re-layouts  5.41 us (4%)
    ppermute x9, starting transfers between devices, further(): lax.ppermute(part, axis, [(i, (i + step) % size) for i in range(size)])  39.2 us
    all_to_all x1, blocking collectives, on_device(): weight = lax.all_to_all(copies, ('zh', 'zl'), 0, 0, tiled=True)  33.6 us
    pallas_call x8, Pallas kernels, call(): pl.pallas_call(kernel, grid=(grid,), in_specs=in_specs or [SMEM if o.shap...  20.5 us
    psum x1, blocking collectives, on_device(): d_gain = lax.psum(own_gain, 'x')  9.66 us
    ppermute x9, waiting for transfers between devices, further(): lax.ppermute(part, axis, [(i, (i + step) % size) for i in range(size)])  7.78 us
    all_to_all x1, starting transfers between devices, on_device(): lax.all_to_all(sent, EXPERT, split_axis=0, concat_axis=2, tiled=True)  4.98 us
    all_to_all x1, starting transfers between devices, on_device(): inner = lax.all_to_all(inner, EXPERT, 0, 0, tiled=True)  4.92 us
    unnamed x16, local copies, waits for them, and re-layouts  3.56 us
  transfers between devices with their start and end apart: 13, of which 5 were waited for; matrix products, arithmetic and copies ran while one was open for 1% of the time, Pallas kernels for 12%

profile of v12, /device:TPU:8, one launch (start us, length us, event | category | flops | bytes accessed | tf_op | source)
XLA Modules:
  0.0 142.9 jit_solution(3782100044761794595)
XLA Ops:
  7.2 2.4 %shard_map.94 = (bf16[144,1024]{1,0:T(8,128)(2,1)}, bf16[16,16,512]{2,1,0:T(8,128)(2,1)}) custom-call(bf16[128,1024]{1,0:T(8,128)(2,1)} %value_ref.1, bf16[1024,512]{1,0:T(8,128)(2,1)} %refs_5_.1, bf16[16,512]{1,0:T(8,128)(2,1)} %weight_ref.1), custom_call_target="tpu_custom_call" | custom-call | tf_op jit(solution)/shard_map/pallas_call | solution.py:33
  9.7 33.6 %all_to_all.28 = bf16[16,16,512]{2,1,0:T(8,128)(2,1)S(1)} all-to-all(bf16[16,16,512]{2,1,0:T(8,128)(2,1)} %get-tuple-element.27), channel_id=1, replica_groups=mesh['zh'=4,'zl'=4,'x'=4,'y'=4,'core'=2] {'zh','zl'}, dimensions={0} | all-to-all | bytes 524288 | tf_op jit(solution)/shard_map/all_to_all | solution.py:319
  43.3 3.4 %collective-permute-start = (bf16[4,4,16,512]{3,2,1,0:T(8,128)(2,1)S(1)}, bf16[4,4,16,512]{3,2,1,0:T(8,128)(2,1)S(1)}, u32[]{:S(2)}, u32[]{:S(2)}) collective-permute-start(bf16[4,4,16,512]{3,2,1,0:T(8,128)(2,1)S(1)} %bitcast.15), channel_id=1, source_target_pairs={{0,8},{8,16},{16,24},{24,0},{1,9},{9,17},{17,25},{25,1},{2,10},{10... | collective-permute-start | bytes 786440 | tf_op jit(solution)/shard_map/ppermute | solution.py:296
  46.7 4.6 %collective-permute-start.1 = (bf16[4,4,16,512]{3,2,1,0:T(8,128)(2,1)S(1)}, bf16[4,4,16,512]{3,2,1,0:T(8,128)(2,1)S(1)}, u32[]{:S(2)}, u32[]{:S(2)}) collective-permute-start(bf16[4,4,16,512]{3,2,1,0:T(8,128)(2,1)S(1)} %bitcast.16), channel_id=1, source_target_pairs={{0,16},{8,24},{16,0},{24,8},{1,17},{9,25},{17,1},{25,9},{2,18},{10... | collective-permute-start | bytes 786440 | tf_op jit(solution)/shard_map/ppermute | solution.py:296
  51.3 3.3 %collective-permute-start.2 = (bf16[4,4,16,512]{3,2,1,0:T(8,128)(2,1)S(1)}, bf16[4,4,16,512]{3,2,1,0:T(8,128)(2,1)S(1)}, u32[]{:S(2)}, u32[]{:S(2)}) collective-permute-start(bf16[4,4,16,512]{3,2,1,0:T(8,128)(2,1)S(1)} %bitcast.17), channel_id=1, source_target_pairs={{0,24},{8,0},{16,8},{24,16},{1,25},{9,1},{17,9},{25,17},{2,26},{10... | collective-permute-start | bytes 786440 | tf_op jit(solution)/shard_map/ppermute | solution.py:296
  54.7 5.5 %shard_map.95 = (f32[4,4,4,16,512]{4,3,2,1,0:T(8,128)}, f32[8,128]{1,0:T(8,128)}) custom-call(bf16[8,144,1024]{2,1,0:T(8,128)(2,1)} %bitcast.25, bf16[1024,512]{1,0:T(8,128)(2,1)} %refs_5_.1, f32[1,512]{1,0:T(1,128)} %bitcast.21), custom_call_target="tpu_custom_call" | custom-call | tf_op jit(solution)/shard_map/pallas_call | solution.py:33
  61.0 4.7 %shard_map.96 = (f32[1024,512]{1,0:T(8,128)}, f32[8,8,128]{2,1,0:T(8,128)}, f32[1,512]{1,0:T(1,128)S(1)}) custom-call(s32[1]{0:T(128)} %bitcast.6.me_ref, bf16[8,144,1024]{2,1,0:T(8,128)(2,1)} %bitcast.26, bf16[1024,512]{1,0:T(8,128)(2,1)} %refs_5_.1, bf16[1024,512]{1,0:T(8,128)(2,1)} %grad_ref.1, f32[1,512]{1,0:T(1,128)S(1)} %bitcast.22, ...), custom_call_target="tpu_custom_call" | custom-call | flops 4000000000 | bytes 10000000 | tf_op jit(solution)/shard_map/pallas_call | solution.py:33
  65.7 4.9 %all-to-all-start.1 = ((f32[8,8,128]{2,1,0:T(8,128)}), f32[8,8,128]{2,1,0:T(8,128)S(1)}, u32[]{:S(2)}, u32[]{:S(2)}) async-start(f32[8,8,128]{2,1,0:T(8,128)} %get-tuple-element.32), calls=%async_computation.2 | async-start | bytes 65536 | tf_op jit(solution)/shard_map/all_to_all | solution.py:374
  72.1 2.5 %all-to-all-done.1.refs_1_ = f32[8,8,128]{2,1,0:T(8,128)S(1)} async-done(((f32[8,8,128]{2,1,0:T(8,128)}), f32[8,8,128]{2,1,0:T(8,128)S(1)}, u32[]{:S(2)}, u32[]{:S(2)}) %all-to-all-start.1) | async-done | bytes 32800 | tf_op jit(solution)/shard_map/all_to_all | solution.py:374
  75.2 6.8 %shard_map.98 = bf16[8,320,512]{2,1,0:T(8,128)(2,1)} custom-call(f32[8,128]{1,0:T(8,128)} %get-tuple-element.30.given_ref.refs_0_, f32[8,8,128]{2,1,0:T(8,128)} %copy-done.7, s32[8,1024]{1,0:T(8,128)} %copy-done.4, f32[8,1024]{1,0:T(8,128)} %copy-done.5, f32[1024,512]{1,0:T(8,128)} %get-tuple-element.35.refs_4_, bf16[1024,512]{1,0:T(8,128)(2,1)} %refs_5_.1), custom_call_target="tpu_custom_call" | custom-call | flops 20000000000 | bytes 10000000 | tf_op jit(solution)/shard_map/pallas_call | solution.py:33
  82.0 5.0 %all-to-all-start.2 = ((bf16[8,320,512]{2,1,0:T(8,128)(2,1)}), bf16[8,320,512]{2,1,0:T(8,128)(2,1)S(1)}, u32[]{:S(2)}, u32[]{:S(2)}) async-start(bf16[8,320,512]{2,1,0:T(8,128)(2,1)} %shard_map.98), calls=%async_computation.3 | async-start | bytes 5242880 | tf_op jit(solution)/shard_map/all_to_all | solution.py:400
  87.0 9.7 %psum.7.d_gain_ref = f32[1,512]{1,0:T(1,128)S(1)} all-reduce(f32[1,512]{1,0:T(1,128)S(1)} %get-tuple-element.37), channel_id=1, replica_groups=mesh['zh'=4,'zl'=4,'x'=4,'y'=4,'core'=2] {'x'}, use_global_device_ids=true, to_apply=%region_1.0 | all-reduce | flops 512 | bytes 4096 | tf_op jit(solution)/shard_map/psum | solution.py:402
  96.7 1.0 copy-done
  97.8 5.5 %collective-permute-start.3 = (bf16[80,512]{1,0:T(8,128)(2,1)S(1)}, bf16[80,512]{1,0:T(8,128)(2,1)S(1)}, u32[]{:S(2)}, u32[]{:S(2)}) collective-permute-start(bf16[80,512]{1,0:T(8,128)(2,1)S(1)} %get-tuple-element.39), channel_id=1, source_target_pairs={{0,32},{32,64},{64,96},{96,0},{1,33},{33,65},{65,97},{97,1},{2,34}... | collective-permute-start | bytes 245768 | tf_op jit(solution)/shard_map/ppermute | solution.py:296
  103.3 3.8 %collective-permute-start.4 = (bf16[80,512]{1,0:T(8,128)(2,1)S(1)}, bf16[80,512]{1,0:T(8,128)(2,1)S(1)}, u32[]{:S(2)}, u32[]{:S(2)}) collective-permute-start(bf16[80,512]{1,0:T(8,128)(2,1)S(1)} %get-tuple-element.40), channel_id=1, source_target_pairs={{0,64},{32,96},{64,0},{96,32},{1,65},{33,97},{65,1},{97,33},{2,66}... | collective-permute-start | bytes 245768 | tf_op jit(solution)/shard_map/ppermute | solution.py:296
  107.2 2.5 %collective-permute-start.5 = (bf16[80,512]{1,0:T(8,128)(2,1)S(1)}, bf16[80,512]{1,0:T(8,128)(2,1)S(1)}, u32[]{:S(2)}, u32[]{:S(2)}) collective-permute-start(bf16[80,512]{1,0:T(8,128)(2,1)S(1)} %get-tuple-element.41), channel_id=1, source_target_pairs={{0,96},{32,0},{64,32},{96,64},{1,97},{33,1},{65,33},{97,65},{2,98}... | collective-permute-start | bytes 245768 | tf_op jit(solution)/shard_map/ppermute | solution.py:296
  109.7 2.2 %collective-permute-done.4.c_ref = bf16[80,512]{1,0:T(8,128)(2,1)S(1)} collective-permute-done((bf16[80,512]{1,0:T(8,128)(2,1)S(1)}, bf16[80,512]{1,0:T(8,128)(2,1)S(1)}, u32[]{:S(2)}, u32[]{:S(2)}) %collective-permute-start.4) | collective-permute-done | bytes 81952 | tf_op jit(solution)/shard_map/ppermute | solution.py:296
  111.9 1.6 %collective-permute-done.5.d_ref = bf16[80,512]{1,0:T(8,128)(2,1)S(1)} collective-permute-done((bf16[80,512]{1,0:T(8,128)(2,1)S(1)}, bf16[80,512]{1,0:T(8,128)(2,1)S(1)}, u32[]{:S(2)}, u32[]{:S(2)}) %collective-permute-start.5) | collective-permute-done | bytes 81952 | tf_op jit(solution)/shard_map/ppermute | solution.py:296
  113.6 4.8 %collective-permute-start.6 = (bf16[16,640]{1,0:T(8,128)(2,1)S(1)}, bf16[16,640]{1,0:T(8,128)(2,1)S(1)}, u32[]{:S(2)}, u32[]{:S(2)}) collective-permute-start(bf16[16,640]{1,0:T(8,128)(2,1)S(1)} %get-tuple-element.43), channel_id=1, source_target_pairs={{0,128},{128,256},{256,384},{384,0},{1,129},{129,257},{257,385},{3... | collective-permute-start | bytes 61448 | tf_op jit(solution)/shard_map/ppermute | solution.py:296
  118.4 7.4 %collective-permute-start.7 = (bf16[16,640]{1,0:T(8,128)(2,1)S(1)}, bf16[16,640]{1,0:T(8,128)(2,1)S(1)}, u32[]{:S(2)}, u32[]{:S(2)}) collective-permute-start(bf16[16,640]{1,0:T(8,128)(2,1)S(1)} %get-tuple-element.44), channel_id=1, source_target_pairs={{0,256},{128,384},{256,0},{384,128},{1,257},{129,385},{257,1},{385... | collective-permute-start | bytes 61448 | tf_op jit(solution)/shard_map/ppermute | solution.py:296
  125.8 3.8 %collective-permute-start.8 = (bf16[16,640]{1,0:T(8,128)(2,1)S(1)}, bf16[16,640]{1,0:T(8,128)(2,1)S(1)}, u32[]{:S(2)}, u32[]{:S(2)}) collective-permute-start(bf16[16,640]{1,0:T(8,128)(2,1)S(1)} %get-tuple-element.45), channel_id=1, source_target_pairs={{0,384},{128,0},{256,128},{384,256},{1,385},{129,1},{257,129},{385... | collective-permute-start | bytes 61448 | tf_op jit(solution)/shard_map/ppermute | solution.py:296
  129.6 1.9 %copy.11 = bf16[1,8,40,8,512]{4,3,1,2,0:T(8,128)(2,1)} copy(bf16[1,8,40,8,512]{4,3,2,1,0:T(8,128)(2,1)S(1)} %bitcast.23) | data formatting | bytes 5242880 | tf_op jit(solution)/shard_map/all_to_all | solution.py:400
  131.5 1.3 collective-permute-done.7.refs_2_
  132.8 2.6 %collective-permute-done.8.refs_3_ = bf16[16,640]{1,0:T(8,128)(2,1)S(1)} collective-permute-done((bf16[16,640]{1,0:T(8,128)(2,1)S(1)}, bf16[16,640]{1,0:T(8,128)(2,1)S(1)}, u32[]{:S(2)}, u32[]{:S(2)}) %collective-permute-start.8) | collective-permute-done | bytes 20512 | tf_op jit(solution)/shard_map/ppermute | solution.py:296
  (31 shorter events, 3.8 us)
Async XLA Ops:
  7.2 47.5 %all-gather.3.cloned.1.call-start = ((), (), s32[]{:S(2)}) async-start(), calls=%async_computation.5 | async-start | bytes 2654208 | tf_op jit(solution)/shard_map/all_gather | solution.py:317
  9.6 87.0 %reduce-scatter.2.cloned.1.call-start = ((), (), s32[]{:S(2)}) async-start(), calls=%async_computation.4 | async-start | bytes 2621440 | tf_op jit(solution)/shard_map/reduce_scatter | solution.py:345
  43.3 11.4 %collective-permute-start = (bf16[4,4,16,512]{3,2,1,0:T(8,128)(2,1)S(1)}, bf16[4,4,16,512]{3,2,1,0:T(8,128)(2,1)S(1)}, u32[]{:S(2)}, u32[]{:S(2)}) collective-permute-start(bf16[4,4,16,512]{3,2,1,0:T(8,128)(2,1)S(1)} %bitcast.15), channel_id=1, source_target_pairs={{0,8},{8,16},{16,24},{24,0},{1,9},{9,17},{17,25},{25,1},{2,10},{10... | collective-permute-start | bytes 786440 | tf_op jit(solution)/shard_map/ppermute | solution.py:296
  46.7 13.6 %collective-permute-start.1 = (bf16[4,4,16,512]{3,2,1,0:T(8,128)(2,1)S(1)}, bf16[4,4,16,512]{3,2,1,0:T(8,128)(2,1)S(1)}, u32[]{:S(2)}, u32[]{:S(2)}) collective-permute-start(bf16[4,4,16,512]{3,2,1,0:T(8,128)(2,1)S(1)} %bitcast.16), channel_id=1, source_target_pairs={{0,16},{8,24},{16,0},{24,8},{1,17},{9,25},{17,1},{25,9},{2,18},{10... | collective-permute-start | bytes 786440 | tf_op jit(solution)/shard_map/ppermute | solution.py:296
  51.3 9.0 %collective-permute-start.2 = (bf16[4,4,16,512]{3,2,1,0:T(8,128)(2,1)S(1)}, bf16[4,4,16,512]{3,2,1,0:T(8,128)(2,1)S(1)}, u32[]{:S(2)}, u32[]{:S(2)}) collective-permute-start(bf16[4,4,16,512]{3,2,1,0:T(8,128)(2,1)S(1)} %bitcast.17), channel_id=1, source_target_pairs={{0,24},{8,0},{16,8},{24,16},{1,25},{9,1},{17,9},{25,17},{2,26},{10... | collective-permute-start | bytes 786440 | tf_op jit(solution)/shard_map/ppermute | solution.py:296
  54.7 5.6 %copy-start.3 = (f32[512]{0:T(512)S(1)}, f32[512]{0:T(512)}, u32[]{:S(2)}) copy-start(f32[512]{0:T(512)} %param.10) | copy-start | bytes 6148
  60.3 0.7 copy-start.6
  61.0 9.6 %copy-start.1 = (s32[1024,2]{0,1:T(2,128)S(1)}, s32[1024,2]{0,1:T(2,128)}, u32[]{:S(2)}) copy-start(s32[1024,2]{0,1:T(2,128)} %param.13) | copy-start | bytes 24580
  61.0 9.6 %copy-start.2 = (f32[1024,2]{0,1:T(2,128)S(1)}, f32[1024,2]{0,1:T(2,128)}, u32[]{:S(2)}) copy-start(f32[1024,2]{0,1:T(2,128)} %param.12) | copy-start | bytes 24580
  65.7 8.9 %all-to-all-start.1 = ((f32[8,8,128]{2,1,0:T(8,128)}), f32[8,8,128]{2,1,0:T(8,128)S(1)}, u32[]{:S(2)}, u32[]{:S(2)}) async-start(f32[8,8,128]{2,1,0:T(8,128)} %get-tuple-element.32), calls=%async_computation.2 | async-start | bytes 65536 | tf_op jit(solution)/shard_map/all_to_all | solution.py:374
  70.9 0.6 copy-start.4
  71.5 0.6 copy-start.5
  74.6 0.6 copy-start.7
  82.0 47.6 %all-to-all-start.2 = ((bf16[8,320,512]{2,1,0:T(8,128)(2,1)}), bf16[8,320,512]{2,1,0:T(8,128)(2,1)S(1)}, u32[]{:S(2)}, u32[]{:S(2)}) async-start(bf16[8,320,512]{2,1,0:T(8,128)(2,1)} %shard_map.98), calls=%async_computation.3 | async-start | bytes 5242880 | tf_op jit(solution)/shard_map/all_to_all | solution.py:400
  96.7 1.0 copy-start
  97.8 11.8 %collective-permute-start.3 = (bf16[80,512]{1,0:T(8,128)(2,1)S(1)}, bf16[80,512]{1,0:T(8,128)(2,1)S(1)}, u32[]{:S(2)}, u32[]{:S(2)}) collective-permute-start(bf16[80,512]{1,0:T(8,128)(2,1)S(1)} %get-tuple-element.39), channel_id=1, source_target_pairs={{0,32},{32,64},{64,96},{96,0},{1,33},{33,65},{65,97},{97,1},{2,34}... | collective-permute-start | bytes 245768 | tf_op jit(solution)/shard_map/ppermute | solution.py:296
  103.3 8.5 %collective-permute-start.4 = (bf16[80,512]{1,0:T(8,128)(2,1)S(1)}, bf16[80,512]{1,0:T(8,128)(2,1)S(1)}, u32[]{:S(2)}, u32[]{:S(2)}) collective-permute-start(bf16[80,512]{1,0:T(8,128)(2,1)S(1)} %get-tuple-element.40), channel_id=1, source_target_pairs={{0,64},{32,96},{64,0},{96,32},{1,65},{33,97},{65,1},{97,33},{2,66}... | collective-permute-start | bytes 245768 | tf_op jit(solution)/shard_map/ppermute | solution.py:296
  107.2 6.3 %collective-permute-start.5 = (bf16[80,512]{1,0:T(8,128)(2,1)S(1)}, bf16[80,512]{1,0:T(8,128)(2,1)S(1)}, u32[]{:S(2)}, u32[]{:S(2)}) collective-permute-start(bf16[80,512]{1,0:T(8,128)(2,1)S(1)} %get-tuple-element.41), channel_id=1, source_target_pairs={{0,96},{32,0},{64,32},{96,64},{1,97},{33,1},{65,33},{97,65},{2,98}... | collective-permute-start | bytes 245768 | tf_op jit(solution)/shard_map/ppermute | solution.py:296
  113.6 17.9 %collective-permute-start.6 = (bf16[16,640]{1,0:T(8,128)(2,1)S(1)}, bf16[16,640]{1,0:T(8,128)(2,1)S(1)}, u32[]{:S(2)}, u32[]{:S(2)}) collective-permute-start(bf16[16,640]{1,0:T(8,128)(2,1)S(1)} %get-tuple-element.43), channel_id=1, source_target_pairs={{0,128},{128,256},{256,384},{384,0},{1,129},{129,257},{257,385},{3... | collective-permute-start | bytes 61448 | tf_op jit(solution)/shard_map/ppermute | solution.py:296
  118.4 14.5 %collective-permute-start.7 = (bf16[16,640]{1,0:T(8,128)(2,1)S(1)}, bf16[16,640]{1,0:T(8,128)(2,1)S(1)}, u32[]{:S(2)}, u32[]{:S(2)}) collective-permute-start(bf16[16,640]{1,0:T(8,128)(2,1)S(1)} %get-tuple-element.44), channel_id=1, source_target_pairs={{0,256},{128,384},{256,0},{384,128},{1,257},{129,385},{257,1},{385... | collective-permute-start | bytes 61448 | tf_op jit(solution)/shard_map/ppermute | solution.py:296
  125.8 9.6 %collective-permute-start.8 = (bf16[16,640]{1,0:T(8,128)(2,1)S(1)}, bf16[16,640]{1,0:T(8,128)(2,1)S(1)}, u32[]{:S(2)}, u32[]{:S(2)}) collective-permute-start(bf16[16,640]{1,0:T(8,128)(2,1)S(1)} %get-tuple-element.45), channel_id=1, source_target_pairs={{0,384},{128,0},{256,128},{384,256},{1,385},{129,1},{257,129},{385... | collective-permute-start | bytes 61448 | tf_op jit(solution)/shard_map/ppermute | solution.py:296
Sparse Core Ops, SparseCore 0:
  10.7 36.6 all-gather.2
  60.4 31.9 reduce-scatter.1
